TPU v7x, 32 devices: a whole 2x2x4 slice. The times are simulated.
32 devices in a mesh: rows: 4 (over y, core), chan: 8 (over z, x).
Axes of the slice: x: 2, y: 2, z: 4, core: 2. Of those that a mesh axis runs over, the one named last changes fastest.
Arguments:
- tokens: float32 [16384, 1024], P(('rows', 'chan')), may hold values from -6 to 6
- segments: int32 [16384], P('rows'), may hold values from 0 to 32, as said below
- gelu_weight: bfloat16 [1024, 1536], P(None, 'chan'), may hold values from -0.1875 to 0.1875
- gelu_bias: bfloat16 [1536], P('chan'), may hold values from -3 to 3
- input_weight: bfloat16 [1024, 1536], P(None, 'chan'), may hold values from -0.1875 to 0.1875
- input_bias: bfloat16 [1536], P('chan'), may hold values from -3 to 3
- conv_taps: bfloat16 [4, 1536], P(None, 'chan'), may hold values from -3 to 3
- conv_bias: bfloat16 [1536], P('chan'), may hold values from -2 to 2
- decay_gate: bfloat16 [1536, 192], P('chan'), may hold values from -0.4375 to 0.4375
- decay_bias: bfloat16 [1536], P('chan'), may hold values from -3 to 3
- input_gate: bfloat16 [1536, 192], P('chan'), may hold values from -0.4375 to 0.4375
- ingate_bias: bfloat16 [1536], P('chan'), may hold values from -3 to 3
- decay_param: bfloat16 [1536], P('chan'), may hold values from -8 to -1
- out_weight: bfloat16 [1536, 1024], P('chan'), may hold values from -0.3125 to 0.3125
- mixer_gain: float32 [1024], replicated, may hold values from 0.5 to 1.5
- gate_weight: bfloat16 [1024, 3072], P(None, 'chan'), may hold values from -0.1875 to 0.1875
- up_weight: bfloat16 [1024, 3072], P(None, 'chan'), may hold values from -0.1875 to 0.1875
- down_weight: bfloat16 [3072, 1024], P('chan'), may hold values from -0.21875 to 0.21875
- feed_gain: float32 [1024], replicated, may hold values from 0.5 to 1.5
- cotangent: float32 [16384, 1024], P(('rows', 'chan'))
Outputs:
- block_output: float32 [16384, 1024], P(('rows', 'chan'))
- tokens_grad: float32 [16384, 1024], P(('rows', 'chan'))
- gelu_weight_grad: float32 [1024, 1536], P(None, 'chan')
- gelu_bias_grad: float32 [1536], P('chan')
- input_weight_grad: float32 [1024, 1536], P(None, 'chan')
- input_bias_grad: float32 [1536], P('chan')
- conv_taps_grad: float32 [4, 1536], P(None, 'chan')
- conv_bias_grad: float32 [1536], P('chan')
- decay_gate_grad: float32 [1536, 192], P('chan')
- decay_bias_grad: float32 [1536], P('chan')
- input_gate_grad: float32 [1536, 192], P('chan')
- ingate_bias_grad: float32 [1536], P('chan')
- decay_param_grad: float32 [1536], P('chan')
- out_weight_grad: float32 [1536, 1024], P('chan')
- mixer_gain_grad: float32 [1024], replicated
- gate_weight_grad: float32 [1024, 3072], P(None, 'chan')
- up_weight_grad: float32 [1024, 3072], P(None, 'chan')
- down_weight_grad: float32 [3072, 1024], P('chan')
- feed_gain_grad: float32 [1024], replicated
- mean_decay: float32 [1536], P('chan')
Inputs may be any that keep to these rules, and one draw needn't show every extreme that they name: Each packed row of 4096 tokens holds 8 segments, the first beginning at the row's first token; numbers rise by one at each new segment, across rows too, and are 0 on a run of padding of at most 128 tokens at the row's end, which every row but the last has. The first 6 segments end within the row's first 512 tokens and the last one begins within its last 512 tokens.
All inputs are finite; a program needn't handle non-finite values.
Results may differ from a plain program's by a relative error of at most 0.0085.
Values may be sent and summed in bfloat16 or wider, within the bound.
No kernel may reach another device: no remote copies, remote signals or barrier semaphores. Data moves between devices by JAX's collectives and lax.ppermute only.
A program may use at most 448 MiB of HBM per device.

v0:
```python
import functools

import jax
import jax.numpy as jnp
from jax import lax
from jax.experimental import pallas as pl
from jax.experimental.pallas import tpu as pltpu
from jax.sharding import PartitionSpec as P

LOW = jnp.bfloat16
WIDE = jnp.float32
RIM = 16
STEP = 16
VMEM_BYTES = 56 * 1024 * 1024
GELU_SLOPE = 0.7978845608028654
GELU_CUBE = 0.044715


def params(**more):
    return pltpu.CompilerParams(vmem_limit_bytes=VMEM_BYTES, **more)


def moved_by(value, axis, steps):
    count = lax.axis_size(axis)
    leading, last = (max(0, -steps), min(count, count - steps))
    return lax.ppermute(value, axis, [(source, source + steps) for source in range(leading, last)])


def swapped(value, axis, bits):
    count = lax.axis_size(axis)
    return lax.ppermute(value, axis, [(source, source ^ bits) for source in range(count)])


def join(earlier, later):
    return jnp.concatenate(
        [earlier[0:1] * later[0:1], later[0:1] * earlier[1:2] + later[1:2]], 0
    )


def entering(value, axis, sign):
    count = lax.axis_size(axis)
    if count in (4, 8):
        (partner,) = yield [(value, axis, 1, swapped)]
        later = (lax.axis_index(axis) & 1) == (1 if sign > 0 else 0)
        both = join(jnp.where(later, partner, value), jnp.where(later, value, partner))
        came = yield [(both, axis, 2 * sign * reach) for reach in range(1, count // 2)]
        total = came[-1]
        for one in came[-2::-1]:
            total = join(total, one)
        return jnp.where(later, join(total, partner)[1:2], total[1:2])
    total = value
    came = yield [(value, axis, sign * reach) for reach in (1, 2, 3) if reach < count]
    for one in came:
        total = join(one, total)
    reach = 4
    while 2 * reach < count:
        (one,) = yield [(total, axis, sign * reach)]
        total = join(one, total)
        reach *= 2
    came = yield [(total, axis, sign * far) for far in (1, reach + 1) if far < count]
    last = came[0]
    for one in came[1:]:
        last = join(one, last)
    return last[1:2]


def rms_norm(values, gain):
    return values * lax.rsqrt(jnp.mean(values * values, axis=-1, keepdims=True) + 1e-06) * gain


def nt(left, right):
    return lax.dot_general(left, right, (((1,), (1,)), ((), ())), preferred_element_type=WIDE)


def tn(left, right):
    return lax.dot_general(left, right, (((0,), (0,)), ((), ())), preferred_element_type=WIDE)


def nn(left, right):
    return lax.dot_general(left, right, (((1,), (0,)), ((), ())), preferred_element_type=WIDE)


def sigmoid(value):
    return 0.5 * jnp.tanh(0.5 * value) + 0.5


def gelu_parts(value):
    square = value * value
    bend = jnp.tanh(GELU_SLOPE * value * (1.0 + GELU_CUBE * square))
    half = 0.5 + 0.5 * bend
    slope = half + 0.5 * GELU_SLOPE * value * (1.0 - bend * bend) * (1.0 + 3.0 * GELU_CUBE * square)
    return value * half, slope


def loop(count, unroll, body, init):
    while count % unroll:
        unroll -= 1

    def several(index, carry):
        for turn in range(unroll):
            carry = body(index * unroll + turn, carry)
        return carry

    return lax.fori_loop(0, count // unroll, several, init)


def cost(microseconds):
    return pl.CostEstimate(
        flops=int(microseconds * 1.1e7), bytes_accessed=int(microseconds * 3.5e4), transcendentals=0
    )


def fold(value):
    total = value[0:8]
    for group in range(1, value.shape[0] // 8):
        total = total + value[8 * group : 8 * group + 8]
    return total


def fill_gates(packed, gates, block):
    width = 2 * block
    lines = packed.shape[1] * 3 // 4

    @pl.when(pl.program_id(0) == 0)
    def _():
        gates[...] = jnp.zeros_like(gates)

    parts = []
    for unit in range(packed.shape[0]):
        value = packed[unit].astype(WIDE)[:lines]
        parts += [value[:, 0:width], value[:, 512 : 512 + width]]
    parts = jnp.concatenate(parts, 0).astype(LOW)
    for half in (0, block):
        gates[half : half + block, half : half + block] = parts[half : half + block, 0:block]
        gates[half : half + block, width + half : width + half + block] = parts[
            half : half + block, block:
        ]


def mixer_forward_kernel(
    normed, u_weight, packed, vec, mask, u_out, conv_out, r_out, i_out, h_out, f_out, sum_out,
    low, zed, gates,
):
    ext = normed.shape[0]
    width = u_out.shape[1]
    fill_gates(packed, gates, width // 2)
    count = (ext - RIM) // STEP
    u_out[...] = nt(normed[...], u_weight[...]) + vec[1:2, :]

    def convolve(index, _):
        base = pl.multiple_of(index * STEP, STEP)
        own = pl.ds(base, STEP)
        window = u_out[pl.ds(base + 8, STEP + 8), :]
        flags = mask[pl.ds(base + RIM, STEP), :]
        conv = vec[2:3, :] + vec[6:7, :] * window[8:]
        for shift in (1, 2, 3):
            conv = conv + flags[:, shift : shift + 1] * (
                vec[6 + shift : 7 + shift, :] * window[8 - shift : 8 - shift + STEP]
            )
        conv = conv * flags[:, 4:5]
        conv_out[own, :] = conv
        low[own, :] = conv.astype(LOW)
        return 0

    loop(count, 4, convolve, 0)
    zed[...] = nn(low[...], gates[...])
    line = lax.broadcasted_iota(jnp.int32, (8, width), 0)

    def advance(index, carry):
        state, factor, total = carry
        own = pl.ds(pl.multiple_of(index * STEP, STEP), STEP)
        going = mask[pl.ds(pl.multiple_of(index * STEP + RIM, STEP), STEP), :][:, 0:1]
        rate = sigmoid(zed[own, 0:width] + vec[3:4, :])
        into = sigmoid(zed[own, width:] + vec[4:5, :])
        decay = jnp.exp(vec[5:6, :] * rate)
        r_out[own, :] = rate
        i_out[own, :] = into
        scale = jnp.where(going == 0.0, 1.0, jnp.sqrt(1.01 - decay * decay))
        inject = conv_out[own, :] * into * scale
        carried = decay * going
        total = total + fold(decay)
        for group in range(STEP // 8):
            part = slice(8 * group, 8 * group + 8)
            mul, add = carried[part], inject[part]
            for reach in (1, 2, 4):
                inside = line >= reach
                add = add + mul * jnp.where(inside, pltpu.roll(add, reach, 0), 0.0)
                mul = mul * jnp.where(inside, pltpu.roll(mul, reach, 0), 1.0)
            here = add + mul * state
            gone = mul * factor
            rows = pl.ds(pl.multiple_of(index * STEP + 8 * group, 8), 8)
            h_out[rows, :] = here
            f_out[rows, :] = gone
            state, factor = here[7:8], gone[7:8]
        return state, factor, total

    zero = jnp.zeros((1, width), WIDE)
    _, _, total = loop(
        count, 4, advance, (zero, zero + 1.0, jnp.zeros((8, width), WIDE))
    )
    sum_out[...] = total


def mixer_forward(normed, u_weight, packed, vec, mask, width):
    ext, model = normed.shape
    tokens = ext - RIM
    total = u_weight.shape[0]
    pairs = total // width
    units = packed.shape[0] // pairs
    by_lane = lambda length: pl.BlockSpec((length, width), lambda step: (0, step))
    whole = lambda array: pl.BlockSpec(array.shape, lambda step: (0,) * array.ndim)
    flat = jax.ShapeDtypeStruct((tokens, total), WIDE)
    return pl.pallas_call(
        mixer_forward_kernel,
        grid=(pairs,),
        in_specs=[
            whole(normed),
            pl.BlockSpec((width, model), lambda step: (step, 0)),
            pl.BlockSpec((units, *packed.shape[1:]), lambda step: (step, 0, 0)),
            by_lane(vec.shape[0]),
            whole(mask),
        ],
        out_specs=[by_lane(ext)] + [by_lane(tokens)] * 5 + [by_lane(8)],
        out_shape=[jax.ShapeDtypeStruct((ext, total), WIDE)] + [flat] * 5
        + [jax.ShapeDtypeStruct((8, total), WIDE)],
        scratch_shapes=[
            pltpu.VMEM((tokens, width), LOW),
            pltpu.VMEM((tokens, 2 * width), WIDE),
            pltpu.VMEM((width, 2 * width), LOW),
        ],
        compiler_params=params(),
        cost_estimate=cost(26),
        name="mixer_forward",
    )(normed, u_weight, packed, vec, mask)


def gelu_branch_kernel(normed, weight, vec, active_out, slope_out, held):
    held[...] = nt(normed[RIM:, :], weight[...]) + vec[0:1, :]

    def act(index, _):
        own = pl.ds(pl.multiple_of(index * STEP, STEP), STEP)
        active_out[own, :], slope_out[own, :] = gelu_parts(held[own, :])
        return 0

    loop(held.shape[0] // STEP, 4, act, 0)


def gelu_branch(normed, weight, vec, width):
    length, total = normed.shape[0] - RIM, weight.shape[0]
    model = normed.shape[1]
    lane = lambda lines: pl.BlockSpec((lines, width), lambda step: (0, step))
    return pl.pallas_call(
        gelu_branch_kernel,
        grid=(total // width,),
        in_specs=[
            pl.BlockSpec(normed.shape, lambda step: (0, 0)),
            pl.BlockSpec((width, model), lambda step: (step, 0)),
            lane(vec.shape[0]),
        ],
        out_specs=[lane(length), lane(length)],
        out_shape=[jax.ShapeDtypeStruct((length, total), WIDE)] * 2,
        scratch_shapes=[pltpu.VMEM((length, width), WIDE)],
        compiler_params=params(),
        cost_estimate=cost(8),
        name="gelu_branch",
    )(normed, weight, vec)


def mixer_out_kernel(active, h, f, state, weight, tokens, gain, mixed, middle, normed):
    def gate(index, _):
        own = pl.ds(pl.multiple_of(index * STEP, STEP), STEP)
        mixed[own, :] = ((h[own, :] + f[own, :] * state[...]) * active[own, :]).astype(LOW)
        return 0

    loop(active.shape[0] // STEP, 4, gate, 0)
    total = tokens[...] + nn(mixed[...], weight[...])
    middle[...] = total
    scale = lax.rsqrt(jnp.mean(total * total, axis=-1, keepdims=True) + 1e-06)
    normed[...] = (total * scale * gain[...]).astype(LOW)


def mixer_out(active, h, f, state, weight, tokens, gain):
    length, model = tokens.shape
    total = active.shape[1]
    tile = 256 if length % 256 == 0 else length
    row = lambda lanes: pl.BlockSpec((tile, lanes), lambda step: (step, 0))
    one = lambda array: pl.BlockSpec(array.shape, lambda step: (0, 0))
    return pl.pallas_call(
        mixer_out_kernel,
        grid=(length // tile,),
        in_specs=[
            row(total), row(total), row(total), one(state), one(weight), row(model), one(gain),
        ],
        out_specs=[row(total), row(model), row(model)],
        out_shape=[
            jax.ShapeDtypeStruct((length, total), LOW),
            jax.ShapeDtypeStruct((length, model), WIDE),
            jax.ShapeDtypeStruct((length, model), LOW),
        ],
        compiler_params=params(),
        cost_estimate=cost(9),
        name="mixer_out",
    )(active, h, f, state, weight, tokens, gain)


def spread(place, wide, keep, send, matrix, group, rows, lanes=slice(None), count=None):
    part = rows // 4
    if part % 8:
        value = wide[:, 0:count]
        pieces = [value[begin : begin + part] for begin in range(0, group * rows, part)]
        mine = place[1] * 4 + place[2]
        bit = 1
        while bit < len(pieces):
            turned = (mine & bit) != 0
            pieces = [
                jnp.where(turned, pieces[index ^ bit], pieces[index])
                for index in range(len(pieces))
            ]
            bit *= 2
    for slot in range(group):
        shard = slot ^ place[1]
        for turn in range(4):
            if part % 8:
                value = pieces[4 * slot + turn]
            else:
                begin = pl.multiple_of(shard * rows + (turn ^ place[2]) * part, 8)
                value = wide[pl.ds(begin, part), 0:count]
            (keep, send)[turn & 1][slot, matrix, turn >> 1, :, lanes] = value.astype(LOW)


def feed_kernel(
    group, place, normed, cot, out_in, units, out, grad, keep, send, gate_s, up_s, back_s, hidden_l,
    both_l, held, sems, turned, cot_turned,
):
    model = normed.shape[1]
    width = gate_s.shape[0]
    rows = width // group
    part, half = rows // 4, rows // 2
    step = pl.program_id(0)

    def copies(index):
        for member in range(group):
            for turn in range(4):
                unit = (place[0] ^ (group * index + member)) * 4 + (place[1] ^ turn)
                order = 4 * member + (turn % 2) * 2 + turn // 2
                slot = index % 2
                yield pltpu.make_async_copy(
                    units.at[unit], held.at[slot, :, order], sems.at[slot, 4 * member + turn]
                )

    @pl.when(step == 0)
    def _():
        for copy in copies(0):
            copy.start()
        out[...] = out_in[...]
        grad[...] = jnp.zeros_like(grad)
        turned[...] = jnp.transpose(normed[...])
        cot_turned[...] = jnp.transpose(cot[...])

    @pl.when(step + 1 < pl.num_programs(0))
    def _():
        for copy in copies(step + 1):
            copy.start()

    for copy in copies(step):
        copy.wait()

    def weight(begin, end):
        if part % 16 == 0:
            return held[step % 2, begin:end].reshape((end - begin) * width, model)
        pieces = [
            held[step % 2, matrix, order].astype(WIDE)
            for matrix in range(begin, end)
            for order in range(4 * group)
        ]
        return jnp.concatenate(pieces, 0).astype(LOW)

    first, third = weight(0, 2), weight(2, 3)
    gate_s[...] = nn(first[:width], turned[...])
    up_s[...] = nn(first[width:], turned[...])
    back_s[...] = nn(third, cot_turned[...])

    def act(index, _):
        base = pl.multiple_of(index * STEP, STEP)
        own = pl.ds(base, STEP)
        up, back = up_s[own, :], back_s[own, :]
        value, slope = gelu_parts(gate_s[own, :])
        hidden_l[own, :] = (value * up).astype(LOW)
        both_l[own, :] = (back * up * slope).astype(LOW)
        both_l[pl.ds(base + width, STEP), :] = (back * value).astype(LOW)
        return 0

    loop(width // STEP, 4, act, 0)
    out[...] += tn(hidden_l[...], third)
    grad[...] += tn(both_l[...], first)
    for member in range(group):
        for matrix, (value, offset) in enumerate(((both_l, 0), (both_l, width), (hidden_l, 0))):
            begin = offset + member * rows
            keep[member, matrix] = value[begin : begin + half, :]
            send[member, matrix] = value[begin + half : begin + rows, :]


def feed(place, normed, cot, out_in, units):
    length, model = normed.shape
    part = units.shape[2]
    slots = units.shape[0] // 4
    group = 2
    width = 4 * part * group
    whole = lambda array: pl.BlockSpec(array.shape, lambda step, place: (0,) * array.ndim)
    piece = pl.BlockSpec((group, 3, 2 * part, length), lambda step, place: (step, 0, 0, 0))
    wide = jax.ShapeDtypeStruct((length, model), WIDE)
    grads = jax.ShapeDtypeStruct((slots, 3, 2 * part, length), LOW)
    return pl.pallas_call(
        functools.partial(feed_kernel, group),
        grid_spec=pltpu.PrefetchScalarGridSpec(
            num_scalar_prefetch=1,
            grid=(slots // group,),
            in_specs=[
                whole(normed), whole(cot), whole(out_in), pl.BlockSpec(memory_space=pl.ANY),
            ],
            out_specs=[whole(out_in), whole(out_in), piece, piece],
            scratch_shapes=[pltpu.VMEM((width, length), WIDE)] * 3
            + [pltpu.VMEM((width, length), LOW), pltpu.VMEM((2 * width, length), LOW)]
            + [pltpu.VMEM((2, 3, 4 * group, part, model), LOW)]
            + [pltpu.SemaphoreType.DMA((2, 4 * group))]
            + [pltpu.VMEM((model, length), LOW)] * 2,
        ),
        out_shape=[wide, wide, grads, grads],
        compiler_params=params(),
        cost_estimate=cost(34),
        name="feed",
    )(place, normed, cot, out_in, units)


def feed_grads_kernel(parity, count, mine, theirs, normed, cot, normed_too, cot_too, near, far):
    part = mine.shape[2] // 2
    step = pl.program_id(0)
    for matrix in range(3):
        right, right_too = (cot, cot_too) if matrix == 2 else (normed, normed_too)
        value = nn(mine[0, matrix], right[...]) + nn(theirs[0, matrix], right_too[...])
        value = value.astype(LOW)
        if parity == 0:
            near[0, matrix] = value[:part]
            far[0, matrix] = value[part:]
            continue
        for place, out in ((0, near), (count // 2, far)):

            @pl.when((step >= place) & (step < place + count // 2))
            def _():
                out[0, matrix, 0] = value[:part]
                out[0, matrix, 1] = value[part:]


def feed_grads(parity, mine, theirs, normed, cot, normed_too, cot_too):
    slots, _, rows, length = mine.shape
    model = normed.shape[1]
    count, part = slots // 2, rows // 2
    whole = lambda array: pl.BlockSpec(array.shape, lambda step: (0,) * array.ndim)

    def source(step):
        if parity == 0:
            return 4 * (step // 2) + step % 2, 0, 0, 0
        last = (step >= count // 2).astype(jnp.int32)
        return 4 * (step - last * (count // 2)) + 2 + last, 0, 0, 0

    if parity == 0:
        specs = [pl.BlockSpec((1, 3, part, model), lambda step: (step, 0, 0, 0))] * 2
        shape = jax.ShapeDtypeStruct((count, 3, part, model), LOW)
    else:
        clipped = lambda first: lambda step: (jnp.clip(step - first, 0, count // 2 - 1), 0, 0, 0, 0)
        specs = [
            pl.BlockSpec((1, 3, 2, part, model), clipped(first)) for first in (0, count // 2)
        ]
        shape = jax.ShapeDtypeStruct((count // 2, 3, 2, part, model), LOW)
    return pl.pallas_call(
        functools.partial(feed_grads_kernel, parity, count),
        grid=(count,),
        in_specs=[pl.BlockSpec((1, 3, rows, length), source)] * 2 + [whole(normed)] * 4,
        out_specs=specs,
        out_shape=[shape, shape],
        compiler_params=params(),
        cost_estimate=cost(2000),
        name="feed_grads",
    )(mine, theirs, normed, cot, normed_too, cot_too)


def middle_back_kernel(
    middle, grad, cot, gain, weight, active_in, slope_in, h, f, state, mid_grad, mid_low, state_grad, y_grad,
    gain_sum, back_sum, bias_sum, mixed_s,
):
    @pl.when(pl.program_id(0) == 0)
    def _():
        gain_sum[...] = jnp.zeros_like(gain_sum)
        back_sum[...] = jnp.zeros_like(back_sum)
        bias_sum[...] = jnp.zeros_like(bias_sum)

    value, error = middle[...], grad[...]
    scale = lax.rsqrt(jnp.mean(value * value, axis=-1, keepdims=True) + 1e-06)
    gained = gain[...] * error
    mean = jnp.mean(gained * value, axis=-1, keepdims=True)
    total = cot[...] + scale * gained - value * (scale * scale * scale * mean)
    gain_sum[...] += fold(error * value * scale)
    mid_grad[...] = total
    mid_low[...] = total.astype(LOW)
    mixed_s[...] = nt(mid_low[...], weight[...])

    def turn(index, carry):
        back, bias = carry
        own = pl.ds(pl.multiple_of(index * STEP, STEP), STEP)
        error = mixed_s[own, :]
        active, slope = active_in[own, :], slope_in[own, :]
        gone = f[own, :]
        full = h[own, :] + gone * state[...]
        here = error * active
        state_grad[own, :] = here
        low = (error * full * slope).astype(LOW)
        y_grad[own, :] = low
        return back + fold(here * gone), bias + fold(low.astype(WIDE))

    zero = jnp.zeros(back_sum.shape, WIDE)
    back, bias = loop(middle.shape[0] // STEP, 4, turn, (zero, zero))
    back_sum[...] += back
    bias_sum[...] += bias


def middle_back(middle, grad, cot, gain, weight, active, slope, h, f, state):
    length, model = middle.shape
    total = active.shape[1]
    tile = 256 if length % 256 == 0 else length
    row = lambda lanes: pl.BlockSpec((tile, lanes), lambda step: (step, 0))
    one = lambda lines, lanes: pl.BlockSpec((lines, lanes), lambda step: (0, 0))
    return pl.pallas_call(
        middle_back_kernel,
        grid=(length // tile,),
        in_specs=[
            row(model), row(model), row(model), one(1, model),
            one(total, model), row(total), row(total), row(total), row(total), one(1, total),
        ],
        out_specs=[
            row(model), row(model), row(total), row(total), one(8, model), one(8, total),
            one(8, total),
        ],
        out_shape=[
            jax.ShapeDtypeStruct((length, model), WIDE),
            jax.ShapeDtypeStruct((length, model), LOW),
            jax.ShapeDtypeStruct((length, total), WIDE),
            jax.ShapeDtypeStruct((length, total), LOW),
            jax.ShapeDtypeStruct((8, model), WIDE),
            jax.ShapeDtypeStruct((8, total), WIDE),
            jax.ShapeDtypeStruct((8, total), WIDE),
        ],
        scratch_shapes=[pltpu.VMEM((tile, total), WIDE)],
        compiler_params=params(),
        cost_estimate=cost(13),
        name="middle_back",
    )(middle, grad, cot, gain, weight, active, slope, h, f, state)


def mixer_back_kernel(
    rows, first, place, state_grad, r_in, i_in, conv_in, h, f, u, y_grad, mixed, y_weight, u_weight,
    packed, vec, mask, state, after, normed, mid_low, y_sum, decay_sum, *refs
):
    if not first:
        grad_in, refs = refs[2], refs[3:]
    (
        keep, send, normed_grad, conv_s, low, conv_l, grown, u_low, wide, gate_w, gates, sums,
    ) = refs
    length, width = state_grad.shape
    ext, model = normed.shape
    group = width // rows
    block = width // 2
    count = length // STEP
    line = lax.broadcasted_iota(jnp.int32, (8, width), 0)

    fill_gates(packed, gates, block)

    @pl.when(pl.program_id(0) == 0)
    def _():
        if first:
            normed_grad[...] = jnp.zeros_like(normed_grad)
        else:
            normed_grad[...] = grad_in[...]

    def retreat(index, carry):
        error, rate_sum, into_sum, slope_sum = carry
        base = pl.multiple_of((count - 1 - index) * STEP, STEP)
        own = pl.ds(base, STEP)
        going = mask[pl.ds(base + RIM, STEP), :][:, 0:1]
        rate, into, conv = r_in[own, :], i_in[own, :], conv_in[own, :]
        slope = vec[5:6, :]
        decay = jnp.exp(slope * rate)
        carried = decay * going
        given = state_grad[own, :]
        full = h[own, :] + f[own, :] * state[...]
        ahead = pl.ds(pl.multiple_of(jnp.maximum(base - 8, 0), 8), 8)
        edge = h[ahead, :][7:8] + f[ahead, :][7:8] * state[...]
        edge = jnp.where(base == 0, state[...], edge)
        parts = []
        for part in reversed(range(STEP // 8)):
            place_of = slice(8 * part, 8 * part + 8)
            mul = carried[place_of]
            add = mul * given[place_of]
            for reach in (1, 2, 4):
                inside = line < 8 - reach
                add = add + mul * jnp.where(inside, pltpu.roll(add, 8 - reach, 0), 0.0)
                mul = mul * jnp.where(inside, pltpu.roll(mul, 8 - reach, 0), 1.0)
            here = add + mul * error
            parts.append(given[place_of] + jnp.where(line < 7, pltpu.roll(here, 7, 0), error))
            error = here[0:1]
        grad = jnp.concatenate(parts[::-1], 0)
        befores = []
        for part in range(STEP // 8):
            last = edge if part == 0 else full[8 * part - 1 : 8 * part]
            befores.append(
                jnp.where(line > 0, pltpu.roll(full[8 * part : 8 * part + 8], 1, 0), last)
            )
        before = jnp.concatenate(befores, 0)
        root = lax.rsqrt(1.01 - decay * decay)
        scale = jnp.where(going == 0.0, 1.0, (1.01 - decay * decay) * root)
        through = grad * conv
        into_grad = through * scale
        conv_s[own, :] = grad * into * scale
        decay_grad = going * decay * (grad * before - through * into * decay * root)
        z_rate = decay_grad * slope * rate * (1.0 - rate)
        z_into = into_grad * into * (1.0 - into)
        low[own, 0:width] = z_rate.astype(LOW)
        low[own, width:] = z_into.astype(LOW)
        conv_l[own, :] = conv.astype(LOW)
        return (
            error,
            rate_sum + fold(z_rate),
            into_sum + fold(z_into),
            slope_sum + fold(decay_grad * rate),
        )

    zero = jnp.zeros((8, width), WIDE)
    _, rate_sum, into_sum, slope_sum = loop(
        count, 4, retreat, (after[...], zero, zero, zero)
    )
    conv_s[...] += nt(low[...], gates[...])
    gate_full = tn(conv_l[...], low[...])
    for half in (0, block):
        rows_of = slice(half, half + block)
        gate_w[rows_of, 0:block] = gate_full[rows_of, half : half + block]
        gate_w[rows_of, block:] = gate_full[rows_of, width + half : width + half + block]
    grown[0:RIM, :] = jnp.zeros((RIM, width), WIDE)
    grown[RIM + length :, :] = jnp.zeros((RIM, width), WIDE)

    def taps(index, carry):
        base = pl.multiple_of(index * STEP, STEP)
        window = u[pl.ds(base + 8, STEP + 8), :]
        flags = mask[pl.ds(base + RIM, STEP), :]
        error = conv_s[pl.ds(base, STEP), :] * flags[:, 4:5]
        grown[pl.ds(base + RIM, STEP), :] = error
        out = [carry[0] + fold(error), carry[1] + fold(error * window[8:])]
        for shift in (1, 2, 3):
            moved = window[8 - shift : 8 - shift + STEP]
            out.append(carry[1 + shift] + fold(flags[:, shift : shift + 1] * error * moved))
        return tuple(out)

    bias_sum, *tap_sums = loop(count, 4, taps, (zero,) * 5)

    def spread_back(index, total):
        base = pl.multiple_of(index * STEP, STEP)
        window = grown[pl.ds(base, STEP + 8), :]
        flags = mask[pl.ds(base, STEP + 8), :]
        value = vec[6:7, :] * window[0:STEP]
        for shift in (1, 2, 3):
            masked = flags[:, shift : shift + 1] * window
            value = value + vec[6 + shift : 7 + shift, :] * masked[shift : shift + STEP]
        rounded = value.astype(LOW)
        u_low[pl.ds(base, STEP), :] = rounded
        return total + fold(rounded.astype(WIDE))

    input_sum = loop(ext // STEP, 3, spread_back, zero)
    sums[...] = jnp.zeros_like(sums)
    slope_sum = slope_sum * vec[10:11, :]
    values = (y_sum[...], input_sum, *tap_sums, bias_sum, rate_sum, into_sum, slope_sum, decay_sum[...])
    for row, value in enumerate(values):
        sums[row : row + 1, :] = jnp.sum(value, axis=0, keepdims=True)
    wide[:, 0:128] = jnp.transpose(sums[...])
    spread(place, wide, keep, send, 0, group, rows, slice(3 * model + width, None), 128)
    wide[...] = tn(u_low[...], normed[...])
    spread(place, wide, keep, send, 0, group, rows, slice(0, model))
    spread(place, gate_w, keep, send, 0, group, rows, slice(3 * model, 3 * model + width))
    wide[...] = tn(y_grad[...], normed[RIM:, :])
    spread(place, wide, keep, send, 0, group, rows, slice(model, 2 * model))
    wide[...] = tn(mixed[...], mid_low[...])
    spread(place, wide, keep, send, 0, group, rows, slice(2 * model, 3 * model))
    normed_grad[...] += nn(u_low[...], u_weight[...])
    normed_grad[RIM:, :] += nn(y_grad[...], y_weight[...])


def mixer_back(
    place, state_grad, r, i, conv, h, f, u, y_grad, mixed, y_weight, u_weight, packed, vec, mask,
    state, after, normed, mid_low, y_sum, decay_sum, rows, width, begin, steps, so_far=(),
):
    length, total = state_grad.shape
    ext, model = normed.shape
    group, part = width // rows, rows // 4
    pair = lambda step, place: (step + begin) ^ place[0]
    whole = lambda array: pl.BlockSpec(array.shape, lambda step, place: (0,) * array.ndim)
    lane = lambda lines: pl.BlockSpec((lines, width), lambda step, place: (0, pair(step, place)))
    weight = pl.BlockSpec((width, model), lambda step, place: (pair(step, place), 0))
    units = packed.shape[0] * width // total
    lanes = 3 * model + width + 128
    piece = pl.BlockSpec((group, 1, 2, part, lanes), lambda step, place: (step + begin, 0, 0, 0, 0))
    shape = jax.ShapeDtypeStruct((total // rows, 1, 2, part, lanes), LOW)
    operands = [
        state_grad, r, i, conv, h, f, u, y_grad, mixed, y_weight, u_weight, packed, vec, mask,
        state, after, normed, mid_low, y_sum, decay_sum,
    ]
    kept = pl.BlockSpec(memory_space=pl.ANY)
    return pl.pallas_call(
        functools.partial(mixer_back_kernel, rows, not so_far),
        grid_spec=pltpu.PrefetchScalarGridSpec(
            num_scalar_prefetch=1,
            grid=(steps,),
            in_specs=[
                lane(length), lane(length), lane(length), lane(length), lane(length),
                lane(length), lane(ext), lane(length), lane(length), weight, weight,
                pl.BlockSpec(
                    (units, *packed.shape[1:]), lambda step, place: (pair(step, place), 0, 0)
                ),
                lane(vec.shape[0]), whole(mask), lane(1),
                lane(1), whole(normed), whole(mid_low), lane(8), lane(8),
            ]
            + ([kept, kept, whole(so_far[2])] if so_far else []),
            out_specs=[
                piece, piece, pl.BlockSpec((ext, model), lambda step, place: (0, 0)),
            ],
            scratch_shapes=[
                pltpu.VMEM((length, width), WIDE),
                pltpu.VMEM((length, 2 * width), LOW),
                pltpu.VMEM((length, width), LOW),
                pltpu.VMEM((ext + RIM, width), WIDE),
                pltpu.VMEM((ext, width), LOW),
                pltpu.VMEM((width, model), WIDE),
                pltpu.VMEM((width, width), WIDE),
                pltpu.VMEM((width, 2 * width), LOW),
                pltpu.VMEM((128, width), WIDE),
            ],
        ),
        out_shape=[shape, shape, jax.ShapeDtypeStruct((ext, model), WIDE)],
        input_output_aliases={len(operands) + 1 + k: k for k in range(2)} if so_far else {},
        compiler_params=params(),
        cost_estimate=cost(15 * steps),
        name="mixer_back",
    )(place, *operands, *so_far)


def wide_of(value):
    return value.astype(WIDE)


def pin_kernel(source, target):
    del source, target


class Clock:
    def __init__(self):
        self.time = jnp.zeros((8, 128), WIDE)

    def tick(self, values):
        values, self.time = lax.optimization_barrier((values, self.time))
        return values

    def pin(self):
        self.time = pl.pallas_call(
            pin_kernel,
            in_specs=[pl.BlockSpec(memory_space=pl.ANY)],
            out_specs=pl.BlockSpec(memory_space=pl.ANY),
            out_shape=jax.ShapeDtypeStruct(self.time.shape, WIDE),
            input_output_aliases={0: 0},
            cost_estimate=cost(5000),
            name="pin",
        )(self.time)


class Sums:
    def __init__(self, clock, stages, move=swapped, pin=False, start=True):
        self.clock = clock
        self.stages = stages
        self.move = move
        self.result = self.moving = None
        if start:
            self.begin(pin)

    def begin(self, pin=False):
        self.send(next(self.stages), pin)

    def send(self, transfers, pin):
        meanwhile = transfers.pop() if callable(transfers[-1]) else None
        values = self.clock.tick([transfer[0] for transfer in transfers])
        self.moving = [
            (transfer[3] if len(transfer) > 3 else self.move)(value, *transfer[1:3])
            for value, transfer in zip(values, transfers)
        ]
        if pin:
            self.clock.pin()
        if meanwhile:
            meanwhile()

    def step(self, pin=False):
        try:
            transfers = self.stages.send(self.clock.tick(self.moving))
        except StopIteration as end:
            self.result = end.value
        else:
            self.send(transfers, pin)

    def finish(self):
        while self.result is None:
            self.step()
        return self.result


def lockstep(clock, *groups):
    begun = [group for group in groups if group.moving is not None]
    arrived = clock.tick([group.moving for group in begun])
    transfers = []
    for group in groups:
        if group.moving is None:
            transfers.append(next(group.stages))
        else:
            transfers.append(group.stages.send(arrived[begun.index(group)]))
    values = clock.tick([[transfer[0] for transfer in one] for one in transfers])
    for group, one, own in zip(groups, transfers, values):
        group.moving = [group.move(value, *transfer[1:]) for value, transfer in zip(own, one)]


def halved(clock, keep, send):
    slots, matrices, _, part, lanes = keep.shape
    shape = (slots // 4, 2, 2, matrices, 2, part, lanes)
    keep = keep.reshape(shape)
    (came,) = yield [(send, "rows", 1)]
    came = came.reshape(shape)
    every = slice(None)
    near = {}

    def both(one, other, *where):
        return wide_of(one[where]) + wide_of(other[where])

    def meanwhile():
        one, other = clock.tick((keep, came))
        near["y"] = both(one, other, every, 0, every, every, 0)
        near["x"] = both(one, other, every, 1, 0)
        near.update(clock.tick(dict(near)))

    return (
        yield from owned(
            lambda place: near["y"][:, place],
            both(keep, came, every, 0, every, every, 1).astype(LOW),
            lambda place: near["x"][:, :, place],
            both(keep, came, every, 1, 1).astype(LOW),
            meanwhile,
        )
    )


def owned(near_y, far_y, near_x, far_x, meanwhile=None):
    from_y, from_x = yield [(far_y, "rows", 2), (far_x, "chan", 1)] + (
        [meanwhile] if meanwhile else []
    )
    rest = lambda place: wide_of(near_y(place)) + wide_of(from_y[:, place])
    also = lambda place: wide_of(near_x(place)) + wide_of(from_x[:, :, place])
    rest_came, also_came = yield [
        (rest(1).astype(LOW), "chan", 1),
        (also(1).astype(LOW), "rows", 2),
    ]
    rest, also = rest(0), also(0)
    parts = {}
    for index in range(rest.shape[0]):
        parts[2 * index] = rest[index] + wide_of(rest_came[index])
        parts[2 * index + 1] = also[index] + wide_of(also_came[index])
    came = yield [
        (value.astype(LOW), "chan", 2 * distance) for distance, value in parts.items() if distance
    ]
    total = parts[0]
    for value in came:
        total = total + wide_of(value)
    return total


def settled(total):
    total = total.astype(LOW)
    (came,) = yield [(total, "rows", 2)]
    pair = jnp.stack([total, came])
    (came,) = yield [(pair, "rows", 1)]
    return pair, came


def ordered(pair, came):
    four = jnp.stack([pair, came], 1)
    place = lax.axis_index("rows")
    four = jnp.where(place & 1, four[:, ::-1], four)
    four = jnp.where(place & 2, four[::-1], four)
    _, _, matrices, part, lanes = four.shape
    four = four.reshape(4, matrices, part, lanes).transpose(1, 0, 2, 3)
    return four.reshape(matrices, 4 * part, lanes).astype(WIDE)


def finish_rest_kernel(place, pair, came, into, gelu, out, gates, lines):
    part, model = pair.shape[2], into.shape[1]
    lanes = gates.shape[1]
    for quarter in range(4):
        turn = quarter ^ place[1]
        own, other = (ref[turn // 2, 0].astype(WIDE) for ref in (pair, came))
        value = jnp.where(turn % 2 == 0, own, other)
        rows = slice(quarter * part, quarter * part + part)
        into[rows, :] = value[:, 0:model]
        gelu[rows, :] = value[:, model : 2 * model]
        out[rows, :] = value[:, 2 * model : 3 * model]
        gates[rows, :] = value[:, 3 * model : 3 * model + lanes]
        lines[rows, :] = value[:, 3 * model + lanes :]


def finish_rest(place, pair, came, model, width):
    rows = 4 * pair.shape[2]
    vmem = pl.BlockSpec(memory_space=pltpu.VMEM)
    shape = lambda lanes: jax.ShapeDtypeStruct((rows, lanes), WIDE)
    return pl.pallas_call(
        finish_rest_kernel,
        grid_spec=pltpu.PrefetchScalarGridSpec(
            num_scalar_prefetch=1, grid=(1,), in_specs=[vmem] * 2, out_specs=[vmem] * 5
        ),
        out_shape=[shape(model)] * 3 + [shape(width), shape(128)],
        compiler_params=params(),
        cost_estimate=cost(3),
        name="finish_rest",
    )(place, pair, came)


def finish_kernel(place, pair, came, gate, up, down):
    def rows_of(matrix):
        parts = []
        for quarter in range(4):
            turn = quarter ^ place[1]
            own, other = (ref[turn // 2, matrix].astype(WIDE) for ref in (pair, came))
            parts.append(jnp.where(turn % 2 == 0, own, other))
        return jnp.concatenate(parts, 0)

    gate[...] = jnp.transpose(rows_of(0))
    up[...] = jnp.transpose(rows_of(1))
    down[...] = rows_of(2)


def finish(place, pair, came):
    _, _, part, model = pair.shape
    tall = jax.ShapeDtypeStruct((model, 4 * part), WIDE)
    vmem = pl.BlockSpec(memory_space=pltpu.VMEM)
    return pl.pallas_call(
        finish_kernel,
        grid_spec=pltpu.PrefetchScalarGridSpec(
            num_scalar_prefetch=1, grid=(1,), in_specs=[vmem] * 2, out_specs=[vmem] * 3
        ),
        out_shape=[tall, tall, jax.ShapeDtypeStruct((4 * part, model), WIDE)],
        compiler_params=params(),
        cost_estimate=cost(4),
        name="finish",
    )(place, pair, came)


def everywhere(value):
    for axis in ("rows", "chan"):
        bits = 1
        while bits < lax.axis_size(axis):
            (came,) = yield [(value, axis, bits)]
            value = value + came
            bits *= 2
    return value


def gathered(piece):
    parts = lax.axis_size("rows")
    share = piece.shape[0] // parts
    own = lax.dynamic_slice_in_dim(piece, lax.axis_index("rows") * share, share)
    full = lax.all_gather(own, ("chan", "rows"), axis=0, tiled=True)
    return full.reshape(lax.axis_size("chan"), piece.shape[0], piece.shape[1])


def pack_kernel(table, count, *refs):
    sources, outs, sems = refs[:count], refs[count:-1], refs[-1]
    copies = [
        pltpu.make_async_copy(
            sources[source].at[begin : begin + size],
            outs[out].at[at : at + size],
            sems.at[index],
        )
        for index, (out, at, source, begin, size) in enumerate(table)
    ]
    for copy in copies:
        copy.start()
    for copy in copies:
        copy.wait()


def pack(*lists):
    sources, table, shapes = [], [], []
    for out, pieces in enumerate(lists):
        at = 0
        for array, begin, size in pieces:
            known = [index for index, one in enumerate(sources) if one is array]
            if not known:
                known = [len(sources)]
                sources.append(array)
            table.append((out, at, known[0], begin, size))
            at += size
        shapes.append(jax.ShapeDtypeStruct((at, *pieces[0][0].shape[1:]), pieces[0][0].dtype))
    return pl.pallas_call(
        functools.partial(pack_kernel, table, len(sources)),
        in_specs=[pl.BlockSpec(memory_space=pl.ANY)] * len(sources),
        out_specs=[pl.BlockSpec(memory_space=pltpu.VMEM)] * len(shapes),
        scratch_shapes=[pltpu.SemaphoreType.DMA((len(table),))],
        out_shape=shapes,
        compiler_params=params(),
        cost_estimate=cost(0.01),
        name="pack",
    )(*sources)


def spread_units(units):
    pairs = range(2, lax.axis_size("chan") // 2)
    count = len(pairs)
    behind, *came = yield [(units[:2], "chan", 2)] + [
        (units[:1], "chan", 2 * pair) for pair in pairs
    ]
    singles = [(value, 0, 1) for value in came]
    (turned,) = pack([(units, 0, 1), (behind, 0, 2), *singles])
    (corners,) = yield [(turned, "chan", 1)]
    near, away = pack(
        [(behind, 0, 2), (corners, 1, 2)], [(corners, 0, 1), *singles, (corners, 3, count)]
    )
    over, near_too = yield [(away, "rows", 2), (near, "rows", 1)]
    size = 2 * count + 1
    (away,) = pack([(away, 0, size), (over, 0, size)])
    (away_too,) = yield [(away, "rows", 1)]
    return units, near, near_too, away, away_too


def unit_source(pair, side, turn, count):
    upper, other = turn // 2, turn % 2
    if pair == 0 and side == 0:
        return 0, 2 * other + upper
    if pair == 1:
        return 1 + other, 2 * side + upper
    if pair == 0:
        return 3 + other, upper * (2 * count + 1)
    return 3 + other, upper * (2 * count + 1) + 1 + side * count + pair - 2


def assemble_kernel(cuts, pairs, place, *refs):
    sources, outs, sems = refs[:5], refs[5:-1], refs[-1]
    copies = []
    for pair in range(pairs):
        for side in range(2):
            for turn in range(4):
                array, index = unit_source(pair, side, turn, pairs - 2)
                unit = ((2 * pair + side) ^ place[0]) * 4 + (turn ^ place[1])
                for (begin, end), out in zip(cuts, outs):
                    copies.append(
                        pltpu.make_async_copy(
                            sources[array].at[index, begin:end],
                            out.at[unit],
                            sems.at[len(copies)],
                        )
                    )
    for copy in copies:
        copy.start()
    for copy in copies:
        copy.wait()


def assembled(place, sources, cuts):
    pairs = lax.axis_size("chan") // 2
    model = sources[0].shape[2]
    anywhere = pl.BlockSpec(memory_space=pl.ANY)
    return pl.pallas_call(
        functools.partial(assemble_kernel, cuts, pairs),
        grid_spec=pltpu.PrefetchScalarGridSpec(
            num_scalar_prefetch=1,
            grid=(1,),
            in_specs=[anywhere] * 5,
            out_specs=[pl.BlockSpec(memory_space=pltpu.VMEM)] * len(cuts),
            scratch_shapes=[pltpu.SemaphoreType.DMA((8 * pairs * len(cuts),))],
        ),
        out_shape=[
            jax.ShapeDtypeStruct((8 * pairs, end - begin, model), LOW) for begin, end in cuts
        ],
        compiler_params=params(),
        cost_estimate=cost(5),
        name="assemble",
    )(place, *sources)


def local(
    tokens, segments, gelu_weight, gelu_bias, input_weight, input_bias, conv_taps, conv_bias,
    decay_gate, decay_bias, input_gate, ingate_bias, decay_param, out_weight, mixer_gain,
    gate_weight, up_weight, down_weight, feed_gain, cotangent,
):
    length, model = tokens.shape
    rim = conv_taps.shape[0] - 1
    chans = lax.axis_size("chan")
    me, row_place = lax.axis_index("chan"), lax.axis_index("rows")
    rows, block = decay_gate.shape
    total = rows * chans
    width = 2 * block
    group = width // rows

    padded = jnp.concatenate([jnp.full((rim,), -1, jnp.int32), segments])
    window = lax.dynamic_slice_in_dim(padded, me * length, length + rim)
    own = window[rim:]
    same = [own == window[rim - shift : rim - shift + length] for shift in range(1, rim + 1)]
    mask = jnp.stack([same[0], *same, own != 0] + [same[0]] * (7 - rim - 1), 1).astype(WIDE)
    mask = jnp.pad(mask, ((RIM, RIM), (0, 0)))

    small = jnp.concatenate(
        [
            jnp.stack([gelu_bias, input_bias, conv_bias, decay_bias, ingate_bias, decay_param]),
            conv_taps,
        ]
    )
    unit_rows = block // 4
    count = rows // unit_rows
    lines = unit_rows // 2
    place = jnp.stack([me, row_place]).astype(jnp.int32)
    clock = Clock()

    part = gate_weight.shape[1] // 4
    own_columns = lambda weight: lax.dynamic_slice_in_dim(weight, row_place * part, part, 1).T
    own_unit = jnp.stack(
        [
            own_columns(gate_weight),
            own_columns(up_weight),
            lax.dynamic_slice_in_dim(down_weight, row_place * part, part),
        ]
    )
    both = jnp.concatenate([decay_gate, input_gate], 1)
    both = jnp.pad(both, ((0, 0), (0, model // 2 - 2 * block)))
    both = both.reshape(count, 2, lines, model // 2).swapaxes(1, 2).reshape(count, lines, model)
    flat = small.reshape(small.shape[0], count, unit_rows).swapaxes(0, 1).reshape(count, 1, -1)
    flat = jnp.pad(flat, ((0, 0), (0, lines // 3 - 1), (0, model - flat.shape[2])))
    by_unit = lambda weight: weight.reshape(count, unit_rows, model)
    first = jnp.concatenate([by_unit(input_weight.T), both, flat], 1)
    second = jnp.concatenate([by_unit(gelu_weight.T), by_unit(out_weight)], 1)
    first_cuts = ((0, unit_rows), (unit_rows, first.shape[1]))
    second_cuts = ((0, unit_rows), (unit_rows, 2 * unit_rows))
    cot_low = cotangent.astype(LOW)
    rim_tokens = moved_by(tokens[length - rim :], "chan", 1)
    extended = jnp.concatenate([jnp.zeros((RIM - rim, model), WIDE), rim_tokens, tokens])
    if count == 4:
        quarters = lambda units: jnp.stack(
            [
                lax.dynamic_index_in_dim(units, row_place ^ bits, keepdims=False)
                for bits in (0, 2, 1, 3)
            ]
        )
        own_unit = clock.tick(own_unit)
        first = Sums(clock, spread_units(quarters(first)))
        second = Sums(clock, spread_units(quarters(second)), start=False)
        lockstep(clock, first, second)
        normed = clock.tick(rms_norm(clock.tick(extended), mixer_gain).astype(LOW))
        lockstep(clock, first, second)
        lockstep(clock, first, second)
        first.step()
        u_weight, packed = clock.tick(assembled(place, first.result, first_cuts))
    else:
        cut = lambda units, cuts: [
            gathered(units.reshape(-1, model))[:, begin:end] for begin, end in cuts
        ]
        normed = rms_norm(extended, mixer_gain).astype(LOW)
        u_weight, packed = cut(first, first_cuts)
        y_weight, o_weight = cut(second, second_cuts)
        y_weight, o_weight = (w.reshape(total, model) for w in (y_weight, o_weight))
    feed_units = lax.all_gather(own_unit[None], ("chan", "rows"), axis=0, tiled=True)
    u_weight = u_weight.reshape(total, model)
    small_full = packed[:, lines, : small.shape[0] * unit_rows]
    small_full = small_full.reshape(-1, small.shape[0], unit_rows).swapaxes(0, 1)
    small_full = small_full.reshape(small.shape[0], total).astype(WIDE)
    param = small_full[5:6]
    line = lax.broadcasted_iota(jnp.int32, (16, total), 0)
    vec = jnp.pad(small_full, ((0, 6), (0, 0)))
    vec = jnp.where(line == 5, -8.0 * jax.nn.softplus(param), vec)
    vec = jnp.where(line == 10, -8.0 * jax.nn.sigmoid(param), vec)

    u, conv, rate, into, state, factor, decay_sum = clock.tick(
        mixer_forward(normed, u_weight, packed, vec, mask, width)
    )
    carry = Sums(
        clock, entering(jnp.concatenate([factor[-1:], state[-1:]]), "chan", 1), moved_by
    )
    if count == 4:
        second.step()
        carry.step()
        second.step()
        y_weight, o_weight = clock.tick(assembled(place, second.result, second_cuts))
        y_weight, o_weight = (w.reshape(total, model) for w in (y_weight, o_weight))
    active, slope = clock.tick(gelu_branch(normed, y_weight, vec, width))
    carry = clock.tick(carry.finish())
    cot_too = swapped(cot_low, "rows", 1)
    mixed, middle, normed2 = clock.tick(
        mixer_out(active, state, factor, carry, o_weight, tokens, feed_gain[None])
    )
    cot_too = clock.tick(cot_too)
    normed2_too = swapped(normed2, "rows", 1)
    feed_units = clock.tick(feed_units)
    block_output, normed2_grad, mine, send = clock.tick(
        feed(place, normed2, cot_low, middle, feed_units)
    )
    theirs = swapped(send, "rows", 1)

    mid_grad, mid_low, state_grad, y_grad, feed_gain_sum, back_sum, y_sum = clock.tick(
        middle_back(
            middle, normed2_grad, cotangent, feed_gain[None], o_weight, active, slope, state,
            factor, carry,
        )
    )
    after = Sums(
        clock,
        entering(
            jnp.concatenate([factor[-1:], jnp.sum(back_sum, 0, keepdims=True)]), "chan", -1
        ),
        moved_by,
    )
    theirs, normed2_too = clock.tick((theirs, normed2_too))
    operands = (mine, theirs, normed2, cot_low, normed2_too, cot_too)
    near_y, far_y = clock.tick(feed_grads(0, *operands))
    split = lambda value: value.reshape(-1, 2, *value.shape[1:])
    moving = [swapped(split(far_y), "rows", 2)]
    after.step()
    near_x, far_x = clock.tick(feed_grads(1, *operands))
    moving.append(swapped(far_x, "chan", 1))
    stages = owned(
        lambda place: split(near_y)[:, place], far_y, lambda place: near_x[:, :, place], far_x
    )
    next(stages)
    fed = Sums(clock, stages, start=False)
    fed.moving = moving
    after = clock.tick(after.finish())
    place = jnp.stack([me // group, me % group, row_place]).astype(jnp.int32)
    pairs = total // width
    back = lambda after, begin, steps, so_far: clock.tick(
        mixer_back(
            place, state_grad, rate, into, conv, state, factor, u, y_grad, mixed, y_weight, u_weight,
            packed, vec, mask, carry, after, normed, mid_low, y_sum, decay_sum, rows, width, begin, steps, so_far,
        )
    )
    so_far = back(after, 1, pairs - 1, ())
    fed.step()
    so_far = clock.tick(so_far)
    keep, send, normed_grad = back(after, 0, 1, so_far)
    fed.moving = clock.tick(fed.moving)
    rest = Sums(clock, halved(clock, keep, send))
    rim_grad = moved_by(clock.tick(normed_grad[RIM - rim : RIM]), "chan", -1)
    rim_grad = clock.tick(rim_grad)
    error = normed_grad[RIM:] + jnp.concatenate([jnp.zeros((length - rim, model), WIDE), rim_grad])
    scale = lax.rsqrt(jnp.mean(tokens * tokens, axis=-1, keepdims=True) + 1e-06)
    gained = mixer_gain * error
    mean = jnp.mean(gained * tokens, axis=-1, keepdims=True)
    tokens_grad = clock.tick(mid_grad + scale * gained - tokens * (scale * scale * scale * mean))
    mixer_gain_sum = jnp.sum(error * tokens * scale, 0)

    gains = Sums(clock, everywhere(jnp.stack([mixer_gain_sum, jnp.sum(feed_gain_sum, 0)])))
    gains.step()
    rest.step(pin=True)
    fed.step()
    gains.moving = clock.tick(gains.moving)
    rest.step(pin=True)
    rest.step(pin=True)
    gains.step()
    gains.step()
    fed.step()
    fed = Sums(clock, settled(fed.result))
    gains.step()
    fed.step()
    gains = gains.finish()
    rest.step()
    rest = Sums(clock, settled(rest.result))
    fed.step()
    feed_sum = clock.tick(finish(jnp.stack([me, row_place]).astype(jnp.int32), *fed.result))
    pair, came = rest.finish()
    gains = gains + clock.time[:1, :1]
    if pair.shape[2] % 8:
        whole = ordered(pair, came)[0]
        input_sum, gelu_sum, out_sum = (whole[:, k * model : (k + 1) * model] for k in range(3))
        gates_sum, lines = whole[:, 3 * model : 3 * model + width], whole[:, 3 * model + width :]
    else:
        input_sum, gelu_sum, out_sum, gates_sum, lines = finish_rest(
            jnp.stack([me, row_place]).astype(jnp.int32), pair, came, model, width
        )
    lines = lines[:, :11].T
    mean_decay = lines[10] / (length * lax.axis_size("rows") * chans)
    return (
        block_output,
        tokens_grad,
        gelu_sum.T,
        lines[0],
        input_sum.T,
        lines[1],
        lines[2:6],
        lines[6],
        gates_sum[:, :block],
        lines[7],
        gates_sum[:, block:],
        lines[8],
        lines[9],
        out_sum,
        gains[0],
        feed_sum[0],
        feed_sum[1],
        feed_sum[2],
        gains[1],
        mean_decay,
    )


def solution(mesh):
    return jax.shard_map(
        local,
        mesh=mesh,
        in_specs=(
            P(("rows", "chan"), None),
            P("rows"),
            P(None, "chan"),
            P("chan"),
            P(None, "chan"),
            P("chan"),
            P(None, "chan"),
            P("chan"),
            P("chan", None),
            P("chan"),
            P("chan", None),
            P("chan"),
            P("chan"),
            P("chan", None),
            P(),
            P(None, "chan"),
            P(None, "chan"),
            P("chan", None),
            P(),
            P(("rows", "chan"), None),
        ),
        out_specs=(
            P(("rows", "chan"), None),
            P(("rows", "chan"), None),
            P(None, "chan"),
            P("chan"),
            P(None, "chan"),
            P("chan"),
            P(None, "chan"),
            P("chan"),
            P("chan", None),
            P("chan"),
            P("chan", None),
            P("chan"),
            P("chan"),
            P("chan", None),
            P(),
            P(None, "chan"),
            P(None, "chan"),
            P("chan", None),
            P(),
            P("chan"),
        ),
        check_vma=False,
    )
```

profile of v0, /device:TPU:0, one launch (start us, length us, event | category | flops | bytes accessed | tf_op | source)
XLA Modules:
  0.0 502.5 jit_solution(4314755056485357326)
XLA Ops:
  11.6 3.1 collective-permute-start.1
  14.7 2.6 collective-permute-start.2
  17.3 3.6 collective-permute-start
  24.3 5.1 %collective-permute-done.2.refs_2_ = bf16[1,80,1024]{2,1,0:T(8,128)(2,1)S(1)} collective-permute-done((bf16[1,80,1024]{2,1,0:T(8,128)(2,1)S(1)}, bf16[1,80,1024]{2,1,0:T(8,128)(2,1)S(1)}, u32[]{:S(2)}, u32[]{:S(2)}) %collective-permute-start.2) | collective-permute-done | bytes 163872 | tf_op jit(solution)/shard_map/ppermute | solution.py:31
  29.3 7.8 %collective-permute-done.3.refs_3_ = bf16[1,80,1024]{2,1,0:T(8,128)(2,1)S(1)} collective-permute-done((bf16[1,80,1024]{2,1,0:T(8,128)(2,1)S(1)}, bf16[1,80,1024]{2,1,0:T(8,128)(2,1)S(1)}, u32[]{:S(2)}, u32[]{:S(2)}) %collective-permute-start.3) | collective-permute-done | bytes 163872 | tf_op jit(solution)/shard_map/ppermute | solution.py:31
  38.5 2.1 pack.6
  42.9 2.8 collective-permute-start.6
  48.4 12.0 %collective-permute-done.6.refs_2_ = bf16[1,96,1024]{2,1,0:T(8,128)(2,1)S(1)} collective-permute-done((bf16[1,96,1024]{2,1,0:T(8,128)(2,1)S(1)}, bf16[1,96,1024]{2,1,0:T(8,128)(2,1)S(1)}, u32[]{:S(2)}, u32[]{:S(2)}) %collective-permute-start.6) | collective-permute-done | bytes 196640 | tf_op jit(solution)/shard_map/ppermute | solution.py:31
  60.4 11.1 %collective-permute-done.7.refs_3_ = bf16[1,96,1024]{2,1,0:T(8,128)(2,1)S(1)} collective-permute-done((bf16[1,96,1024]{2,1,0:T(8,128)(2,1)S(1)}, bf16[1,96,1024]{2,1,0:T(8,128)(2,1)S(1)}, u32[]{:S(2)}, u32[]{:S(2)}) %collective-permute-start.7) | collective-permute-done | bytes 196640 | tf_op jit(solution)/shard_map/ppermute | solution.py:31
  72.5 2.5 pack.7
  75.0 2.3 pack.8
  79.3 2.1 collective-permute-done.9.refs_2_
  81.4 9.5 %collective-permute-done.8.refs_1_ = bf16[5,80,1024]{2,1,0:T(8,128)(2,1)S(1)} collective-permute-done((bf16[5,80,1024]{2,1,0:T(8,128)(2,1)S(1)}, bf16[5,80,1024]{2,1,0:T(8,128)(2,1)S(1)}, u32[]{:S(2)}, u32[]{:S(2)}) %collective-permute-start.8) | collective-permute-done | bytes 819232 | tf_op jit(solution)/shard_map/ppermute | solution.py:31
  90.9 7.3 %collective-permute-done.10.refs_1_ = bf16[5,96,1024]{2,1,0:T(8,128)(2,1)S(1)} collective-permute-done((bf16[5,96,1024]{2,1,0:T(8,128)(2,1)}, bf16[5,96,1024]{2,1,0:T(8,128)(2,1)S(1)}, u32[]{:S(2)}, u32[]{:S(2)}) %collective-permute-start.10) | collective-permute-done | bytes 983072 | tf_op jit(solution)/shard_map/ppermute | solution.py:31
  98.2 3.0 pack.10.refs_3_
  101.2 2.7 pack.9
  106.2 1.7 collective-permute-done.13.refs_4_
  109.1 6.1 %assemble.2 = (bf16[32,48,1024]{2,1,0:T(8,128)(2,1)}, bf16[32,32,1024]{2,1,0:T(8,128)(2,1)}) custom-call(s32[2]{0:T(128)} %pad_add_fusion.1.place, bf16[4,80,1024]{2,1,0:T(8,128)(2,1)} %pad_maximum_fusion.4.refs_0_, bf16[4,80,1024]{2,1,0:T(8,128)(2,1)} %get-tuple-element.325.refs_1_, bf16[4,80,1024]{2,1,0:T(8,128)(2,1)} %copy-done.32, ...), custom_call_target="tpu_custom_call" | custom-call | flops 55000000 | bytes 175000 | tf_op jit(solution)/shard_map/assemble/pallas_call | solution.py:1078
  117.7 19.9 %mixer_forward.1 = (f32[528,1536]{1,0:T(8,128)}, f32[512,1536]{1,0:T(8,128)}, f32[512,1536]{1,0:T(8,128)}, f32[512,1536]{1,0:T(8,128)}, f32[512,1536]{1,0:T(8,12...) custom-call(bf16[528,1024]{1,0:T(8,128)(2,1)} %multiply_convert_fusion.normed, bf16[1536,1024]{1,0:T(8,128)(2,1)} %bitcast.189, ...), custom_call_target="tpu_custom_call" | custom-call | flops 286000000 | bytes 910000 | tf_op jit(solution)/shard_map/mixer_forward/pallas_call | solution.py:213
  139.4 10.4 %collective-permute-done.11.refs_1_ = bf16[5,96,1024]{2,1,0:T(8,128)(2,1)S(1)} collective-permute-done((bf16[5,96,1024]{2,1,0:T(8,128)(2,1)}, bf16[5,96,1024]{2,1,0:T(8,128)(2,1)S(1)}, u32[]{:S(2)}, u32[]{:S(2)}) %collective-permute-start.11) | collective-permute-done | bytes 983072 | tf_op jit(solution)/shard_map/ppermute | solution.py:31
  150.8 2.8 pack.11.refs_3_
  155.6 1.8 collective-permute-done.15
  158.8 4.6 collective-permute-start.17
  164.9 6.8 %assemble.3 = (bf16[32,48,1024]{2,1,0:T(8,128)(2,1)}, bf16[32,48,1024]{2,1,0:T(8,128)(2,1)}) custom-call(s32[2]{0:T(128)} %pad_add_fusion.1.place, bf16[4,96,1024]{2,1,0:T(8,128)(2,1)} %pad_maximum_fusion.2.refs_0_, bf16[4,96,1024]{2,1,0:T(8,128)(2,1)} %get-tuple-element.334.refs_1_, bf16[4,96,1024]{2,1,0:T(8,128)(2,1)} %collective-permute-done.12.refs_2_, ...), custom_call_target="tpu_custom_call" | custom-call | flops 55000000 | bytes 175000 | tf_op jit(solution)/shard_map/assemble/pallas_call | solution.py:1078
  171.7 8.5 %gelu_branch.1 = (f32[512,1536]{1,0:T(8,128)}, f32[512,1536]{1,0:T(8,128)}) custom-call(bf16[528,1024]{1,0:T(8,128)(2,1)} %multiply_convert_fusion.normed, bf16[1536,1024]{1,0:T(8,128)(2,1)} %bitcast.192, f32[16,1536]{1,0:T(8,128)} %select_select_fusion.vec), custom_call_target="tpu_custom_call" | custom-call | flops 88000000 | bytes 280000 | tf_op jit(solution)/shard_map/gelu_branch/pallas_call | solution.py:252
  180.9 7.9 %mixer_out.1 = (bf16[512,1536]{1,0:T(8,128)(2,1)}, f32[512,1024]{1,0:T(8,128)}, bf16[512,1024]{1,0:T(8,128)(2,1)}) custom-call(f32[512,1536]{1,0:T(8,128)} %get-tuple-element.373.active.active_in, f32[512,1536]{1,0:T(8,128)} %get-tuple-element.353.h, f32[512,1536]{1,0:T(8,128)} %get-tuple-element.352.f, f32[1,1536]{1,0:T(1,128)} %broadcast_select_fusion.3.state, ...), custom_call_target="tpu_custom_call" | custom-call | flops 99000000 | bytes 315000 | tf_op jit(solution)/shard_map/mixer_out/pallas_call | solution.py:288
  188.8 34.4 %feed.1 = (f32[512,1024]{1,0:T(8,128)}, f32[512,1024]{1,0:T(8,128)}, bf16[8,3,192,512]{3,2,1,0:T(8,128)(2,1)}, bf16[8,3,192,512]{3,2,1,0:T(8,128)(2,1)}) custom-call(s32[2]{0:T(128)} %pad_add_fusion.1.place, bf16[512,1024]{1,0:T(8,128)(2,1)} %get-tuple-element.388.normed, bf16[512,1024]{1,0:T(8,128)(2,1)} %copy-done.11, ...), custom_call_target="tpu_custom_call" | custom-call | flops 374000000 | bytes 1190000 | tf_op jit(solution)/shard_map/feed/pallas_call | solution.py:413
  223.9 12.3 %middle_back.1 = (f32[512,1024]{1,0:T(8,128)}, bf16[512,1024]{1,0:T(8,128)(2,1)}, f32[512,1536]{1,0:T(8,128)}, bf16[512,1536]{1,0:T(8,128)(2,1)}, f32[8,1024]{1,...) custom-call(f32[512,1024]{1,0:T(8,128)} %get-tuple-element.389.out_in.middle, f32[512,1024]{1,0:T(8,128)} %get-tuple-element.400.grad, ...), custom_call_target="tpu_custom_call" | custom-call | flops 143000000 | bytes 455000 | tf_op jit(solution)/shard_map/middle_back/pallas_call | solution.py:532
  237.0 2.0 collective-permute-start.20
  240.0 11.7 %feed_grads.3 = (bf16[2,3,2,96,1024]{4,3,2,1,0:T(8,128)(2,1)}, bf16[2,3,2,96,1024]{4,3,2,1,0:T(8,128)(2,1)}) custom-call(bf16[8,3,192,512]{3,2,1,0:T(8,128)(2,1)} %get-tuple-element.421.mine, bf16[8,3,192,512]{3,2,1,0:T(8,128)(2,1)} %collective-permute-done.21.theirs, bf16[512,1024]{1,0:T(8,128)(2,1)} %get-tuple-element.388.normed, ...), custom_call_target="tpu_custom_call" | custom-call | flops 22000001024 | bytes 70000000 | tf_op jit(solution)/shard_map/feed_grads/pallas_call | solution.py:475
  251.8 9.6 %feed_grads.2 = (bf16[4,3,96,1024]{3,2,1,0:T(8,128)(2,1)}, bf16[4,3,96,1024]{3,2,1,0:T(8,128)(2,1)}) custom-call(bf16[8,3,192,512]{3,2,1,0:T(8,128)(2,1)} %get-tuple-element.421.mine, bf16[8,3,192,512]{3,2,1,0:T(8,128)(2,1)} %collective-permute-done.21.theirs, bf16[512,1024]{1,0:T(8,128)(2,1)} %get-tuple-element.388.normed, bf16[512,1024]{1,0:T(8,128)(2,1)} %copy-done.11, ...), custom_call_target="tpu_custom_call" | custom-call | flops 22000001024 | bytes 70000000 | tf_op jit(solution)/shard_map/feed_grads/pallas_call | solution.py:475
  268.7 2.2 collective-permute-done.24
  270.9 3.4 collective-permute-done.25
  274.9 34.0 %mixer_back.2 = (bf16[8,1,2,48,3584]{4,3,2,1,0:T(8,128)(2,1)}, bf16[8,1,2,48,3584]{4,3,2,1,0:T(8,128)(2,1)}, f32[528,1024]{1,0:T(8,128)}) custom-call(s32[3]{0:T(128)} %pad_add_fusion.2.place, f32[512,1536]{1,0:T(8,128)} %get-tuple-element.411.state_grad, f32[512,1536]{1,0:T(8,128)} %get-tuple-element.412.r_in, f32[512,1536]{1,0:T(8,128)} %get-tuple-element.413.i_in, ...), custom_call_target="tpu_custom_call" | custom-call | flops 495000000 | bytes 1575000 | tf_op jit(solution)/shard_map/mixer_back/pallas_call | solution.py:714
  308.8 6.2 %collective-permute-done.27 = bf16[2,3,2,96,1024]{4,3,1,2,0:T(8,128)(2,1)} collective-permute-done((bf16[2,3,2,96,1024]{4,3,1,2,0:T(8,128)(2,1)S(1)}, bf16[2,3,2,96,1024]{4,3,1,2,0:T(8,128)(2,1)}, u32[]{:S(2)}, u32[]{:S(2)}) %collective-permute-start.27) | collective-permute-done | bytes 2359328 | tf_op jit(solution)/shard_map/ppermute | solution.py:31
  315.3 4.2 convert_add_fusion.1
  319.5 4.1 convert_add_fusion
  323.5 1.7 collective-permute-start.28
  325.8 16.5 %mixer_back.3 = (bf16[8,1,2,48,3584]{4,3,2,1,0:T(8,128)(2,1)}, bf16[8,1,2,48,3584]{4,3,2,1,0:T(8,128)(2,1)}, f32[528,1024]{1,0:T(8,128)}) custom-call(s32[3]{0:T(128)} %pad_add_fusion.2.place, f32[512,1536]{1,0:T(8,128)} %get-tuple-element.411.state_grad, f32[512,1536]{1,0:T(8,128)} %get-tuple-element.412.r_in, ...), custom_call_target="tpu_custom_call", output_to_operand_aliasing={{0}: (21, {}), {1}: (22, {})} | custom-call | flops 165000000 | bytes 525000 | tf_op jit(solution)/shard_map/mixer_back/pallas_call | solution.py:714
  342.3 8.1 %collective-permute-done.28 = bf16[2,3,96,1024]{3,2,1,0:T(8,128)(2,1)} collective-permute-done((bf16[2,3,96,1024]{3,2,1,0:T(8,128)(2,1)S(1)}, bf16[2,3,96,1024]{3,2,1,0:T(8,128)(2,1)}, u32[]{:S(2)}, u32[]{:S(2)}) %collective-permute-start.28) | collective-permute-done | bytes 1179680 | tf_op jit(solution)/shard_map/ppermute | solution.py:31
  354.1 4.0 collective-permute-done.30
  358.1 2.3 multiply_reduce_fusion.1
  360.4 3.5 multiply_subtract_fusion
  365.8 2.7 fusion.1
  368.6 2.7 fusion
  374.9 2.1 add_bitcast_fusion
  377.1 2.3 add_bitcast_fusion.1
  379.6 2.9 fusion.34
  382.4 2.1 fusion.33
  384.5 4.4 collective-permute-start.45
  388.9 15.2 %collective-permute-done.33 = bf16[2,2,1,48,3584]{4,3,2,1,0:T(8,128)(2,1)S(1)} collective-permute-done((bf16[2,2,1,48,3584]{4,3,2,1,0:T(8,128)(2,1)}, bf16[2,2,1,48,3584]{4,3,2,1,0:T(8,128)(2,1)S(1)}, u32[]{:S(2)}, u32[]{:S(2)}) %collective-permute-start.33) | collective-permute-done | bytes 1376288 | tf_op jit(solution)/shard_map/ppermute | solution.py:31
  410.1 14.4 %collective-permute-done.36 = bf16[2,1,48,3584]{3,2,1,0:T(8,128)(2,1)} collective-permute-done((bf16[2,1,48,3584]{3,2,1,0:T(8,128)(2,1)}, bf16[2,1,48,3584]{3,2,1,0:T(8,128)(2,1)}, u32[]{:S(2)}, u32[]{:S(2)}) %collective-permute-start.36) | collective-permute-done | bytes 688160 | tf_op jit(solution)/shard_map/ppermute | solution.py:31
  426.9 2.0 fusion.39
  430.3 3.2 collective-permute-done.41
  433.4 2.1 fusion.10
  436.2 5.2 %collective-permute-start.38 = (bf16[1,48,3584]{2,1,0:T(8,128)(2,1)S(1)}, bf16[1,48,3584]{2,1,0:T(8,128)(2,1)S(1)}, u32[]{:S(2)}, u32[]{:S(2)}) collective-permute-start(bf16[1,48,3584]{2,1,0:T(8,128)(2,1)S(1)} %copy-done.35), channel_id=1, source_target_pairs={{0,2},{1,3},{2,0},{3,1},{4,6},{5,7},{6,4},{7,5},{8,10},{9,11},{10,... | collective-permute-start | bytes 1032200 | tf_op jit(solution)/shard_map/ppermute | solution.py:31
  441.4 2.4 collective-permute-start.40
  444.9 17.2 %collective-permute-done.42 = f32[2,1024]{1,0:T(2,128)S(1)} collective-permute-done((f32[2,1024]{1,0:T(2,128)S(1)}, f32[2,1024]{1,0:T(2,128)S(1)}, u32[]{:S(2)}, u32[]{:S(2)}) %collective-permute-start.42) | collective-permute-done | bytes 8224 | tf_op jit(solution)/shard_map/ppermute | solution.py:31
  462.1 2.4 collective-permute-start.46
  464.7 7.9 %collective-permute-done.46 = f32[2,1024]{1,0:T(2,128)S(1)} collective-permute-done((f32[2,1024]{1,0:T(2,128)S(1)}, f32[2,1024]{1,0:T(2,128)S(1)}, u32[]{:S(2)}, u32[]{:S(2)}) %collective-permute-start.46) | collective-permute-done | bytes 8224 | tf_op jit(solution)/shard_map/ppermute | solution.py:31
  476.6 4.9 finish.1
  481.6 2.1 collective-permute-done.50.came
  484.6 3.6 finish_rest.1
  492.8 1.8 fusion.50
  (285 shorter events, 73.1 us)
Async XLA Ops:
  7.2 181.6 %all-gather.3.cloned.1.call-start = ((), (), s32[]{:S(2)}) async-start(), calls=%async_computation | async-start | bytes 19464192 | tf_op jit(solution)/shard_map/all_gather | solution.py:1175
  11.6 25.5 %collective-permute-start.1 = (bf16[2,80,1024]{2,1,0:T(8,128)(2,1)S(1)}, bf16[2,80,1024]{2,1,0:T(8,128)(2,1)S(1)}, u32[]{:S(2)}, u32[]{:S(2)}) collective-permute-start(bf16[2,80,1024]{2,1,0:T(8,128)(2,1)S(1)} %pad_maximum_fusion.7), channel_id=1, source_target_pairs={{0,2},{1,3},{2,0},{3,1},{4,6},{5,7},{6,4},{7,5},{8,10},{9,11},{10,... | collective-permute-start | bytes 983048 | tf_op jit(solution)/shard_map/ppermute | solution.py:31
  14.7 14.6 %collective-permute-start.2 = (bf16[1,80,1024]{2,1,0:T(8,128)(2,1)S(1)}, bf16[1,80,1024]{2,1,0:T(8,128)(2,1)S(1)}, u32[]{:S(2)}, u32[]{:S(2)}) collective-permute-start(bf16[1,80,1024]{2,1,0:T(8,128)(2,1)S(1)} %get-tuple-element.302), channel_id=1, source_target_pairs={{0,4},{1,5},{2,6},{3,7},{4,0},{5,1},{6,2},{7,3},{8,12},{9,13},{10,... | collective-permute-start | bytes 491528 | tf_op jit(solution)/shard_map/ppermute | solution.py:31
  17.3 19.8 %collective-permute-start.3 = (bf16[1,80,1024]{2,1,0:T(8,128)(2,1)S(1)}, bf16[1,80,1024]{2,1,0:T(8,128)(2,1)S(1)}, u32[]{:S(2)}, u32[]{:S(2)}) collective-permute-start(bf16[1,80,1024]{2,1,0:T(8,128)(2,1)S(1)} %get-tuple-element.302), channel_id=1, source_target_pairs={{0,6},{1,7},{2,4},{3,5},{4,2},{5,3},{6,0},{7,1},{8,14},{9,15},{10,... | collective-permute-start | bytes 491528 | tf_op jit(solution)/shard_map/ppermute | solution.py:31
  17.3 24.9 %collective-permute-start = (f32[3,1024]{1,0:T(4,128)S(1)}, f32[3,1024]{1,0:T(4,128)S(1)}, u32[]{:S(2)}, u32[]{:S(2)}) collective-permute-start(f32[3,1024]{1,0:T(4,128)S(1)} %slice.295), channel_id=1, source_target_pairs={{0,1},{1,2},{2,3},{3,4},{4,5},{5,6},{6,7},{8,9},{9,10},{10,11},{11... | collective-permute-start | bytes 36872 | tf_op jit(solution)/shard_map/ppermute | solution.py:26
  40.6 30.9 %collective-permute-start.4 = (bf16[5,80,1024]{2,1,0:T(8,128)(2,1)}, bf16[5,80,1024]{2,1,0:T(8,128)(2,1)S(1)}, u32[]{:S(2)}, u32[]{:S(2)}) collective-permute-start(bf16[5,80,1024]{2,1,0:T(8,128)(2,1)} %pack.6), channel_id=1, source_target_pairs={{0,1},{1,0},{2,3},{3,2},{4,5},{5,4},{6,7},{7,6},{8,9},{9,8},{10,11... | collective-permute-start | bytes 2457608 | tf_op jit(solution)/shard_map/ppermute | solution.py:31
  42.4 29.1 %collective-permute-start.5 = (bf16[2,96,1024]{2,1,0:T(8,128)(2,1)S(1)}, bf16[2,96,1024]{2,1,0:T(8,128)(2,1)S(1)}, u32[]{:S(2)}, u32[]{:S(2)}) collective-permute-start(bf16[2,96,1024]{2,1,0:T(8,128)(2,1)S(1)} %pad_maximum_fusion.6), channel_id=1, source_target_pairs={{0,2},{1,3},{2,0},{3,1},{4,6},{5,7},{6,4},{7,5},{8,10},{9,11},{10,... | collective-permute-start | bytes 1179656 | tf_op jit(solution)/shard_map/ppermute | solution.py:31
  42.9 17.6 %collective-permute-start.6 = (bf16[1,96,1024]{2,1,0:T(8,128)(2,1)S(1)}, bf16[1,96,1024]{2,1,0:T(8,128)(2,1)S(1)}, u32[]{:S(2)}, u32[]{:S(2)}) collective-permute-start(bf16[1,96,1024]{2,1,0:T(8,128)(2,1)S(1)} %get-tuple-element.315), channel_id=1, source_target_pairs={{0,4},{1,5},{2,6},{3,7},{4,0},{5,1},{6,2},{7,3},{8,12},{9,13},{10,... | collective-permute-start | bytes 589832 | tf_op jit(solution)/shard_map/ppermute | solution.py:31
  45.7 25.8 %collective-permute-start.7 = (bf16[1,96,1024]{2,1,0:T(8,128)(2,1)S(1)}, bf16[1,96,1024]{2,1,0:T(8,128)(2,1)S(1)}, u32[]{:S(2)}, u32[]{:S(2)}) collective-permute-start(bf16[1,96,1024]{2,1,0:T(8,128)(2,1)S(1)} %get-tuple-element.315), channel_id=1, source_target_pairs={{0,6},{1,7},{2,4},{3,5},{4,2},{5,3},{6,0},{7,1},{8,14},{9,15},{10,... | collective-permute-start | bytes 589832 | tf_op jit(solution)/shard_map/ppermute | solution.py:31
  60.4 14.5 %copy-start.26 = (bf16[1,96,1024]{2,1,0:T(8,128)(2,1)}, bf16[1,96,1024]{2,1,0:T(8,128)(2,1)S(1)}, u32[]{:S(2)}) copy-start(bf16[1,96,1024]{2,1,0:T(8,128)(2,1)S(1)} %collective-permute-done.6.refs_2_) | copy-start | bytes 589828
  77.3 26.6 %copy-start.46 = (s32[4096]{0:T(1024)S(1)}, s32[4096]{0:T(1024)}, u32[]{:S(2)}) copy-start(s32[4096]{0:T(1024)} %param.21) | copy-start | bytes 49156
  77.3 20.8 %collective-permute-start.10 = (bf16[5,96,1024]{2,1,0:T(8,128)(2,1)}, bf16[5,96,1024]{2,1,0:T(8,128)(2,1)S(1)}, u32[]{:S(2)}, u32[]{:S(2)}) collective-permute-start(bf16[5,96,1024]{2,1,0:T(8,128)(2,1)} %pack.8), channel_id=1, source_target_pairs={{0,1},{1,0},{2,3},{3,2},{4,5},{5,4},{6,7},{7,6},{8,9},{9,8},{10,11... | collective-permute-start | bytes 2949128 | tf_op jit(solution)/shard_map/ppermute | solution.py:31
  78.1 12.8 %collective-permute-start.8 = (bf16[5,80,1024]{2,1,0:T(8,128)(2,1)S(1)}, bf16[5,80,1024]{2,1,0:T(8,128)(2,1)S(1)}, u32[]{:S(2)}, u32[]{:S(2)}) collective-permute-start(bf16[5,80,1024]{2,1,0:T(8,128)(2,1)S(1)} %copy-done.23), channel_id=1, source_target_pairs={{0,16},{8,24},{16,0},{24,8},{1,17},{9,25},{17,1},{25,9},{2,18},{10... | collective-permute-start | bytes 2457608 | tf_op jit(solution)/shard_map/ppermute | solution.py:31
  79.3 2.1 collective-permute-start.9
  81.4 26.5 %copy-start.32 = (bf16[4,80,1024]{2,1,0:T(8,128)(2,1)}, bf16[4,80,1024]{2,1,0:T(8,128)(2,1)S(1)}, u32[]{:S(2)}) copy-start(bf16[4,80,1024]{2,1,0:T(8,128)(2,1)S(1)} %collective-permute-done.9.refs_2_) | copy-start | bytes 1966084
  103.9 4.1 collective-permute-start.13
  105.7 44.1 %collective-permute-start.11 = (bf16[5,96,1024]{2,1,0:T(8,128)(2,1)}, bf16[5,96,1024]{2,1,0:T(8,128)(2,1)S(1)}, u32[]{:S(2)}, u32[]{:S(2)}) collective-permute-start(bf16[5,96,1024]{2,1,0:T(8,128)(2,1)} %get-tuple-element.333.refs_0_), channel_id=1, source_target_pairs={{0,16},{8,24},{16,0},{24,8},{1,17},{9,25},{17,1},{25,9},{2,18},{10... | collective-permute-start | bytes 2949128 | tf_op jit(solution)/shard_map/ppermute | solution.py:31
  105.7 33.7 %collective-permute-start.12 = (bf16[4,96,1024]{2,1,0:T(8,128)(2,1)}, bf16[4,96,1024]{2,1,0:T(8,128)(2,1)}, u32[]{:S(2)}, u32[]{:S(2)}) collective-permute-start(bf16[4,96,1024]{2,1,0:T(8,128)(2,1)} %get-tuple-element.334.refs_1_), channel_id=1, source_target_pairs={{0,8},{8,0},{16,24},{24,16},{1,9},{9,1},{17,25},{25,17},{2,10},{10... | collective-permute-start | bytes 2359304 | tf_op jit(solution)/shard_map/ppermute | solution.py:31
  137.6 17.6 %copy-start.6 = (f32[512,1024]{1,0:T(8,128)S(1)}, f32[512,1024]{1,0:T(8,128)}, u32[]{:S(2)}) copy-start(f32[512,1024]{1,0:T(8,128)} %cot.1) | copy-start | bytes 6291460
  153.6 11.3 %collective-permute-start.14 = (bf16[10,96,1024]{2,1,0:T(8,128)(2,1)}, bf16[10,96,1024]{2,1,0:T(8,128)(2,1)}, u32[]{:S(2)}, u32[]{:S(2)}) collective-permute-start(bf16[10,96,1024]{2,1,0:T(8,128)(2,1)} %pack.11.refs_3_), channel_id=1, source_target_pairs={{0,8},{8,0},{16,24},{24,16},{1,9},{9,1},{17,25},{25,17},{2,10},{10... | collective-permute-start | bytes 5898248 | tf_op jit(solution)/shard_map/ppermute | solution.py:31
  153.7 3.8 collective-permute-start.15
  155.3 16.4 %copy-start.11 = (bf16[512,1024]{1,0:T(8,128)(2,1)}, bf16[512,1024]{1,0:T(8,128)(2,1)S(1)}, u32[]{:S(2)}) copy-start(bf16[512,1024]{1,0:T(8,128)(2,1)S(1)} %convert_element_type.424.cot) | copy-start | bytes 3145732
  155.4 33.4 %collective-permute-start.19 = (bf16[512,1024]{1,0:T(8,128)(2,1)S(1)}, bf16[512,1024]{1,0:T(8,128)(2,1)S(1)}, u32[]{:S(2)}, u32[]{:S(2)}) collective-permute-start(bf16[512,1024]{1,0:T(8,128)(2,1)S(1)} %convert_element_type.424.cot), channel_id=1, source_target_pairs={{0,8},{8,0},{16,24},{24,16},{1,9},{9,1},{17,25},{25,17},{2,10},{10... | collective-permute-start | bytes 3145736 | tf_op jit(solution)/shard_map/ppermute | solution.py:31
  157.5 22.7 %collective-permute-start.16 = (f32[2,1536]{1,0:T(2,128)S(1)}, f32[2,1536]{1,0:T(2,128)S(1)}, u32[]{:S(2)}, u32[]{:S(2)}) collective-permute-start(f32[2,1536]{1,0:T(2,128)S(1)} %pad_maximum_fusion.10), channel_id=1, source_target_pairs={{0,2},{1,3},{2,4},{3,5},{4,6},{5,7},{8,10},{9,11},{10,12},{11,13},... | collective-permute-start | bytes 36872 | tf_op jit(solution)/shard_map/ppermute | solution.py:26
  158.8 21.4 %collective-permute-start.17 = (f32[2,1536]{1,0:T(2,128)S(1)}, f32[2,1536]{1,0:T(2,128)S(1)}, u32[]{:S(2)}, u32[]{:S(2)}) collective-permute-start(f32[2,1536]{1,0:T(2,128)S(1)} %pad_maximum_fusion.10), channel_id=1, source_target_pairs={{0,4},{1,5},{2,6},{3,7},{8,12},{9,13},{10,14},{11,15},{16,20},{17,... | collective-permute-start | bytes 36872 | tf_op jit(solution)/shard_map/ppermute | solution.py:26
  163.4 16.8 %collective-permute-start.18 = (f32[2,1536]{1,0:T(2,128)S(1)}, f32[2,1536]{1,0:T(2,128)S(1)}, u32[]{:S(2)}, u32[]{:S(2)}) collective-permute-start(f32[2,1536]{1,0:T(2,128)S(1)} %pad_maximum_fusion.10), channel_id=1, source_target_pairs={{0,6},{1,7},{8,14},{9,15},{16,22},{17,23},{24,30},{25,31}} | collective-permute-start | bytes 36872 | tf_op jit(solution)/shard_map/ppermute | solution.py:26
  188.8 34.5 %copy-start.54 = (bf16[512,1024]{1,0:T(8,128)(2,1)}, bf16[512,1024]{1,0:T(8,128)(2,1)S(1)}, u32[]{:S(2)}) copy-start(bf16[512,1024]{1,0:T(8,128)(2,1)S(1)} %collective-permute-done.19.cot_too) | copy-start | bytes 3145732
  188.8 34.5 %copy-start.20 = (bf16[512,1024]{1,0:T(8,128)(2,1)S(1)}, bf16[512,1024]{1,0:T(8,128)(2,1)}, u32[]{:S(2)}) copy-start(bf16[512,1024]{1,0:T(8,128)(2,1)} %get-tuple-element.388.normed) | copy-start | bytes 3145732
  223.3 15.8 %collective-permute-start.21 = (bf16[8,3,192,512]{3,2,1,0:T(8,128)(2,1)}, bf16[8,3,192,512]{3,2,1,0:T(8,128)(2,1)}, u32[]{:S(2)}, u32[]{:S(2)}) collective-permute-start(bf16[8,3,192,512]{3,2,1,0:T(8,128)(2,1)} %get-tuple-element.422), channel_id=1, source_target_pairs={{0,8},{8,0},{16,24},{24,16},{1,9},{9,1},{17,25},{25,17},{2,10},{10... | collective-permute-start | bytes 14155784 | tf_op jit(solution)/shard_map/ppermute | solution.py:31
  223.4 15.7 %collective-permute-start.22 = (bf16[512,1024]{1,0:T(8,128)(2,1)S(1)}, bf16[512,1024]{1,0:T(8,128)(2,1)S(1)}, u32[]{:S(2)}, u32[]{:S(2)}) collective-permute-start(bf16[512,1024]{1,0:T(8,128)(2,1)S(1)} %copy-done.20), channel_id=1, source_target_pairs={{0,8},{8,0},{16,24},{24,16},{1,9},{9,1},{17,25},{25,17},{2,10},{10... | collective-permute-start | bytes 3145736 | tf_op jit(solution)/shard_map/ppermute | solution.py:31
  237.0 24.4 %collective-permute-start.20 = (f32[2,1536]{1,0:T(2,128)S(1)}, f32[2,1536]{1,0:T(2,128)S(1)}, u32[]{:S(2)}, u32[]{:S(2)}) collective-permute-start(f32[2,1536]{1,0:T(2,128)S(1)} %pad_maximum_fusion.8), channel_id=1, source_target_pairs={{0,1},{1,0},{2,3},{3,2},{4,5},{5,4},{6,7},{7,6},{8,9},{9,8},{10,11... | collective-permute-start | bytes 36872 | tf_op jit(solution)/shard_map/ppermute | solution.py:31
  261.9 53.1 %collective-permute-start.27 = (bf16[2,3,2,96,1024]{4,3,1,2,0:T(8,128)(2,1)S(1)}, bf16[2,3,2,96,1024]{4,3,1,2,0:T(8,128)(2,1)}, u32[]{:S(2)}, u32[]{:S(2)}) collective-permute-start(bf16[2,3,2,96,1024]{4,3,1,2,0:T(8,128)(2,1)S(1)} %copy.107), channel_id=1, source_target_pairs={{0,1},{1,0},{2,3},{3,2},{4,5},{5,4},{6,7},{7,6},{8,9},{9,8},{10,11... | collective-permute-start | bytes 7077896 | tf_op jit(solution)/shard_map/ppermute | solution.py:31
  262.0 53.3 %collective-permute-start.26 = (bf16[2,2,3,96,1024]{4,3,2,1,0:T(8,128)(2,1)}, bf16[2,2,3,96,1024]{4,3,2,1,0:T(8,128)(2,1)}, u32[]{:S(2)}, u32[]{:S(2)}) collective-permute-start(bf16[2,2,3,96,1024]{4,3,2,1,0:T(8,128)(2,1)} %bitcast.24), channel_id=1, source_target_pairs={{0,16},{8,24},{16,0},{24,8},{1,17},{9,25},{17,1},{25,9},{2,18},{10... | collective-permute-start | bytes 7077896 | tf_op jit(solution)/shard_map/ppermute | solution.py:31
  263.1 5.6 %collective-permute-start.23 = (f32[2,1536]{1,0:T(2,128)S(1)}, f32[2,1536]{1,0:T(2,128)S(1)}, u32[]{:S(2)}, u32[]{:S(2)}) collective-permute-start(f32[2,1536]{1,0:T(2,128)S(1)} %pad_maximum_fusion.11), channel_id=1, source_target_pairs={{2,0},{3,1},{4,2},{5,3},{6,4},{7,5},{10,8},{11,9},{12,10},{13,11},... | collective-permute-start | bytes 36872 | tf_op jit(solution)/shard_map/ppermute | solution.py:26
  264.4 6.5 %collective-permute-start.24 = (f32[2,1536]{1,0:T(2,128)S(1)}, f32[2,1536]{1,0:T(2,128)S(1)}, u32[]{:S(2)}, u32[]{:S(2)}) collective-permute-start(f32[2,1536]{1,0:T(2,128)S(1)} %pad_maximum_fusion.11), channel_id=1, source_target_pairs={{4,0},{5,1},{6,2},{7,3},{12,8},{13,9},{14,10},{15,11},{20,16},{21,... | collective-permute-start | bytes 36872 | tf_op jit(solution)/shard_map/ppermute | solution.py:26
  265.7 8.6 %collective-permute-start.25 = (f32[2,1536]{1,0:T(2,128)S(1)}, f32[2,1536]{1,0:T(2,128)S(1)}, u32[]{:S(2)}, u32[]{:S(2)}) collective-permute-start(f32[2,1536]{1,0:T(2,128)S(1)} %pad_maximum_fusion.11), channel_id=1, source_target_pairs={{6,0},{7,1},{14,8},{15,9},{22,16},{23,17},{30,24},{31,25}} | collective-permute-start | bytes 36872 | tf_op jit(solution)/shard_map/ppermute | solution.py:26
  274.9 40.4 %copy-start.15 = (bf16[2,3,2,96,1024]{4,3,2,1,0:T(8,128)(2,1)S(1)}, bf16[2,3,2,96,1024]{4,3,2,1,0:T(8,128)(2,1)}, u32[]{:S(2)}) copy-start(bf16[2,3,2,96,1024]{4,3,2,1,0:T(8,128)(2,1)} %get-tuple-element.460) | copy-start | bytes 7077892
  323.5 28.0 %copy-start.3 = (f32[512,1024]{1,0:T(8,128)S(1)}, f32[512,1024]{1,0:T(8,128)}, u32[]{:S(2)}) copy-start(f32[512,1024]{1,0:T(8,128)} %tokens.1) | copy-start | bytes 6291460
  323.5 26.9 %collective-permute-start.28 = (bf16[2,3,96,1024]{3,2,1,0:T(8,128)(2,1)S(1)}, bf16[2,3,96,1024]{3,2,1,0:T(8,128)(2,1)}, u32[]{:S(2)}, u32[]{:S(2)}) collective-permute-start(bf16[2,3,96,1024]{3,2,1,0:T(8,128)(2,1)S(1)} %get-tuple-element.473), channel_id=1, source_target_pairs={{0,1},{1,0},{2,3},{3,2},{4,5},{5,4},{6,7},{7,6},{8,9},{9,8},{10,11... | collective-permute-start | bytes 3538952 | tf_op jit(solution)/shard_map/ppermute | solution.py:31
  325.2 26.3 %collective-permute-start.29 = (bf16[2,3,96,1024]{3,2,1,0:T(8,128)(2,1)S(1)}, bf16[2,3,96,1024]{3,2,1,0:T(8,128)(2,1)}, u32[]{:S(2)}, u32[]{:S(2)}) collective-permute-start(bf16[2,3,96,1024]{3,2,1,0:T(8,128)(2,1)S(1)} %get-tuple-element.474), channel_id=1, source_target_pairs={{0,16},{8,24},{16,0},{24,8},{1,17},{9,25},{17,1},{25,9},{2,18},{10... | collective-permute-start | bytes 3538952 | tf_op jit(solution)/shard_map/ppermute | solution.py:31
  351.5 14.3 %collective-permute-start.31 = (bf16[8,1,2,48,3584]{4,3,2,1,0:T(8,128)(2,1)}, bf16[8,1,2,48,3584]{4,3,2,1,0:T(8,128)(2,1)}, u32[]{:S(2)}, u32[]{:S(2)}) collective-permute-start(bf16[8,1,2,48,3584]{4,3,2,1,0:T(8,128)(2,1)} %get-tuple-element.484), channel_id=1, source_target_pairs={{0,8},{8,0},{16,24},{24,16},{1,9},{9,1},{17,25},{25,17},{2,10},{10... | collective-permute-start | bytes 16515080 | tf_op jit(solution)/shard_map/ppermute | solution.py:31
  352.5 5.6 %collective-permute-start.30 = (f32[3,1024]{1,0:T(4,128)S(1)}, f32[3,1024]{1,0:T(4,128)S(1)}, u32[]{:S(2)}, u32[]{:S(2)}) collective-permute-start(f32[3,1024]{1,0:T(4,128)S(1)} %slice.332), channel_id=1, source_target_pairs={{1,0},{2,1},{3,2},{4,3},{5,4},{6,5},{7,6},{9,8},{10,9},{11,10},{12... | collective-permute-start | bytes 36872 | tf_op jit(solution)/shard_map/ppermute | solution.py:26
  363.9 1.2 collective-permute-start.32
  365.2 19.3 %collective-permute-start.35 = (f32[2,1024]{1,0:T(2,128)S(1)}, f32[2,1024]{1,0:T(2,128)S(1)}, u32[]{:S(2)}, u32[]{:S(2)}) collective-permute-start(f32[2,1024]{1,0:T(2,128)S(1)} %fusion.49), channel_id=1, source_target_pairs={{0,16},{8,24},{16,0},{24,8},{1,17},{9,25},{17,1},{25,9},{2,18},{10... | collective-permute-start | bytes 24584 | tf_op jit(solution)/shard_map/ppermute | solution.py:31
  371.9 32.2 %collective-permute-start.33 = (bf16[2,2,1,48,3584]{4,3,2,1,0:T(8,128)(2,1)}, bf16[2,2,1,48,3584]{4,3,2,1,0:T(8,128)(2,1)S(1)}, u32[]{:S(2)}, u32[]{:S(2)}) collective-permute-start(bf16[2,2,1,48,3584]{4,3,2,1,0:T(8,128)(2,1)} %fusion), channel_id=1, source_target_pairs={{0,16},{8,24},{16,0},{24,8},{1,17},{9,25},{17,1},{25,9},{2,18},{10... | collective-permute-start | bytes 4128776 | tf_op jit(solution)/shard_map/ppermute | solution.py:31
  373.3 31.9 %collective-permute-start.34 = (bf16[2,1,2,48,3584]{4,3,2,1,0:T(8,128)(2,1)}, bf16[2,1,2,48,3584]{4,3,2,1,0:T(8,128)(2,1)S(1)}, u32[]{:S(2)}, u32[]{:S(2)}) collective-permute-start(bf16[2,1,2,48,3584]{4,3,2,1,0:T(8,128)(2,1)} %fusion.1), channel_id=1, source_target_pairs={{0,1},{1,0},{2,3},{3,2},{4,5},{5,4},{6,7},{7,6},{8,9},{9,8},{10,11... | collective-permute-start | bytes 4128776 | tf_op jit(solution)/shard_map/ppermute | solution.py:31
  384.5 48.9 %collective-permute-start.43 = (bf16[3,96,1024]{2,1,0:T(8,128)(2,1)}, bf16[3,96,1024]{2,1,0:T(8,128)(2,1)}, u32[]{:S(2)}, u32[]{:S(2)}) collective-permute-start(bf16[3,96,1024]{2,1,0:T(8,128)(2,1)} %get-tuple-element.532), channel_id=1, source_target_pairs={{0,2},{1,3},{2,0},{3,1},{4,6},{5,7},{6,4},{7,5},{8,10},{9,11},{10,... | collective-permute-start | bytes 1769480 | tf_op jit(solution)/shard_map/ppermute | solution.py:31
  384.5 48.9 %collective-permute-start.44 = (bf16[3,96,1024]{2,1,0:T(8,128)(2,1)}, bf16[3,96,1024]{2,1,0:T(8,128)(2,1)}, u32[]{:S(2)}, u32[]{:S(2)}) collective-permute-start(bf16[3,96,1024]{2,1,0:T(8,128)(2,1)} %fusion.33), channel_id=1, source_target_pairs={{0,4},{1,5},{2,6},{3,7},{4,0},{5,1},{6,2},{7,3},{8,12},{9,13},{10,... | collective-permute-start | bytes 1769480 | tf_op jit(solution)/shard_map/ppermute | solution.py:31
  384.5 48.9 %collective-permute-start.45 = (bf16[3,96,1024]{2,1,0:T(8,128)(2,1)}, bf16[3,96,1024]{2,1,0:T(8,128)(2,1)}, u32[]{:S(2)}, u32[]{:S(2)}) collective-permute-start(bf16[3,96,1024]{2,1,0:T(8,128)(2,1)} %get-tuple-element.534), channel_id=1, source_target_pairs={{0,6},{1,7},{2,4},{3,5},{4,2},{5,3},{6,0},{7,1},{8,14},{9,15},{10,... | collective-permute-start | bytes 1769480 | tf_op jit(solution)/shard_map/ppermute | solution.py:31
  408.1 16.5 %collective-permute-start.36 = (bf16[2,1,48,3584]{3,2,1,0:T(8,128)(2,1)}, bf16[2,1,48,3584]{3,2,1,0:T(8,128)(2,1)}, u32[]{:S(2)}, u32[]{:S(2)}) collective-permute-start(bf16[2,1,48,3584]{3,2,1,0:T(8,128)(2,1)} %bitcast.44), channel_id=1, source_target_pairs={{0,1},{1,0},{2,3},{3,2},{4,5},{5,4},{6,7},{7,6},{8,9},{9,8},{10,11... | collective-permute-start | bytes 2064392 | tf_op jit(solution)/shard_map/ppermute | solution.py:31
  409.7 16.0 %collective-permute-start.37 = (bf16[2,1,48,3584]{3,2,1,0:T(8,128)(2,1)S(1)}, bf16[2,1,48,3584]{3,2,1,0:T(8,128)(2,1)}, u32[]{:S(2)}, u32[]{:S(2)}) collective-permute-start(bf16[2,1,48,3584]{3,2,1,0:T(8,128)(2,1)S(1)} %bitcast.213), channel_id=1, source_target_pairs={{0,16},{8,24},{16,0},{24,8},{1,17},{9,25},{17,1},{25,9},{2,18},{10... | collective-permute-start | bytes 2064392 | tf_op jit(solution)/shard_map/ppermute | solution.py:31
  410.1 16.8 %copy-start.9 = (f32[2,1,1,48,3584]{4,3,2,1,0:T(8,128)S(1)}, f32[2,1,1,48,3584]{4,3,2,1,0:T(8,128)}, u32[]{:S(2)}) copy-start(f32[2,1,1,48,3584]{4,3,2,1,0:T(8,128)} %get-tuple-element.654) | copy-start | bytes 4128772
  429.7 3.7 collective-permute-start.41
  435.5 37.2 %copy-start.8 = (f32[2,1,1,48,3584]{4,3,2,1,0:T(8,128)S(1)}, f32[2,1,1,48,3584]{4,3,2,1,0:T(8,128)}, u32[]{:S(2)}) copy-start(f32[2,1,1,48,3584]{4,3,2,1,0:T(8,128)} %get-tuple-element.656) | copy-start | bytes 4128772
  435.5 29.0 %collective-permute-start.47 = (bf16[3,96,1024]{2,1,0:T(8,128)(2,1)S(1)}, bf16[3,96,1024]{2,1,0:T(8,128)(2,1)S(1)}, u32[]{:S(2)}, u32[]{:S(2)}) collective-permute-start(bf16[3,96,1024]{2,1,0:T(8,128)(2,1)S(1)} %fusion.10), channel_id=1, source_target_pairs={{0,16},{8,24},{16,0},{24,8},{1,17},{9,25},{17,1},{25,9},{2,18},{10... | collective-permute-start | bytes 1769480 | tf_op jit(solution)/shard_map/ppermute | solution.py:31
  436.2 36.5 %collective-permute-start.38 = (bf16[1,48,3584]{2,1,0:T(8,128)(2,1)S(1)}, bf16[1,48,3584]{2,1,0:T(8,128)(2,1)S(1)}, u32[]{:S(2)}, u32[]{:S(2)}) collective-permute-start(bf16[1,48,3584]{2,1,0:T(8,128)(2,1)S(1)} %copy-done.35), channel_id=1, source_target_pairs={{0,2},{1,3},{2,0},{3,1},{4,6},{5,7},{6,4},{7,5},{8,10},{9,11},{10,... | collective-permute-start | bytes 1032200 | tf_op jit(solution)/shard_map/ppermute | solution.py:31
  441.4 31.3 %collective-permute-start.39 = (bf16[1,48,3584]{2,1,0:T(8,128)(2,1)S(1)}, bf16[1,48,3584]{2,1,0:T(8,128)(2,1)S(1)}, u32[]{:S(2)}, u32[]{:S(2)}) collective-permute-start(bf16[1,48,3584]{2,1,0:T(8,128)(2,1)S(1)} %fusion.38), channel_id=1, source_target_pairs={{0,4},{1,5},{2,6},{3,7},{4,0},{5,1},{6,2},{7,3},{8,12},{9,13},{10,... | collective-permute-start | bytes 1032200 | tf_op jit(solution)/shard_map/ppermute | solution.py:31
  441.4 31.3 %collective-permute-start.40 = (bf16[1,48,3584]{2,1,0:T(8,128)(2,1)S(1)}, bf16[1,48,3584]{2,1,0:T(8,128)(2,1)S(1)}, u32[]{:S(2)}, u32[]{:S(2)}) collective-permute-start(bf16[1,48,3584]{2,1,0:T(8,128)(2,1)S(1)} %copy-done.34), channel_id=1, source_target_pairs={{0,6},{1,7},{2,4},{3,5},{4,2},{5,3},{6,0},{7,1},{8,14},{9,15},{10,... | collective-permute-start | bytes 1032200 | tf_op jit(solution)/shard_map/ppermute | solution.py:31
  443.8 18.3 %collective-permute-start.42 = (f32[2,1024]{1,0:T(2,128)S(1)}, f32[2,1024]{1,0:T(2,128)S(1)}, u32[]{:S(2)}, u32[]{:S(2)}) collective-permute-start(f32[2,1024]{1,0:T(2,128)S(1)} %add.377), channel_id=1, source_target_pairs={{0,2},{1,3},{2,0},{3,1},{4,6},{5,7},{6,4},{7,5},{8,10},{9,11},{10,... | collective-permute-start | bytes 24584 | tf_op jit(solution)/shard_map/ppermute | solution.py:31
  462.1 10.6 %collective-permute-start.46 = (f32[2,1024]{1,0:T(2,128)S(1)}, f32[2,1024]{1,0:T(2,128)S(1)}, u32[]{:S(2)}, u32[]{:S(2)}) collective-permute-start(f32[2,1024]{1,0:T(2,128)S(1)} %add.383), channel_id=1, source_target_pairs={{0,4},{1,5},{2,6},{3,7},{4,0},{5,1},{6,2},{7,3},{8,12},{9,13},{10,... | collective-permute-start | bytes 24584 | tf_op jit(solution)/shard_map/ppermute | solution.py:31
  464.7 10.9 %collective-permute-start.49 = (bf16[2,3,96,1024]{3,2,1,0:T(8,128)(2,1)S(1)}, bf16[2,3,96,1024]{3,2,1,0:T(8,128)(2,1)S(1)}, u32[]{:S(2)}, u32[]{:S(2)}) collective-permute-start(bf16[2,3,96,1024]{3,2,1,0:T(8,128)(2,1)S(1)} %pad_maximum_fusion.1.pair), channel_id=1, source_target_pairs={{0,8},{8,0},{16,24},{24,16},{1,9},{9,1},{17,25},{25,17},{2,10},{10... | collective-permute-start | bytes 3538952 | tf_op jit(solution)/shard_map/ppermute | solution.py:31
  473.9 7.5 %collective-permute-start.48 = (bf16[1,48,3584]{2,1,0:T(8,128)(2,1)S(1)}, bf16[1,48,3584]{2,1,0:T(8,128)(2,1)S(1)}, u32[]{:S(2)}, u32[]{:S(2)}) collective-permute-start(bf16[1,48,3584]{2,1,0:T(8,128)(2,1)S(1)} %fusion.30), channel_id=1, source_target_pairs={{0,16},{8,24},{16,0},{24,8},{1,17},{9,25},{17,1},{25,9},{2,18},{10... | collective-permute-start | bytes 1032200 | tf_op jit(solution)/shard_map/ppermute | solution.py:31
  481.4 13.8 %copy-start.1 = (bf16[384,1024]{1,0:T(8,128)(2,1)S(1)}, bf16[384,1024]{1,0:T(8,128)(2,1)}, u32[]{:S(2)}) copy-start(bf16[384,1024]{1,0:T(8,128)(2,1)} %param.37) | copy-start | bytes 2359300
  481.5 2.2 collective-permute-start.50
  (46 other events, 188.6 us)
Sparse Core Ops, SparseCore 0:
  11.0 162.1 all-gather.2
where the time goes:
time: 509 us; the launch traced here: 503 us
  Pallas kernels  192 us (38%)
  waiting for transfers between devices  158 us (31%)
  starting transfers between devices  63.1 us (12%)
  other arithmetic  52.7 us (10%)
  local copies, waits for them, and re-layouts  21 us (4%)
  between operations  15.6 us (3%)
    ppermute x43, waiting for transfers between devices, swapped(): lax.ppermute(value, axis, [(source, source ^ bits) for source in range(co...  148 us
    pallas_call x2, Pallas kernels, mixer_back(): pl.pallas_call(functools.partial(mixer_back_kernel, rows, not so_far), gr...  50.5 us
    ppermute x43, starting transfers between devices, swapped(): lax.ppermute(value, axis, [(source, source ^ bits) for source in range(co...  46.5 us
    pallas_call x1, Pallas kernels, feed(): pl.pallas_call(functools.partial(feed_kernel, group), grid_spec=pltpu.Pre...  34.4 us
    pallas_call x2, Pallas kernels, feed_grads(): pl.pallas_call(functools.partial(feed_grads_kernel, parity, count), grid=...  21.4 us
    pallas_call x1, Pallas kernels, mixer_forward(): pl.pallas_call(mixer_forward_kernel, grid=(pairs,), in_specs=[whole(norme...  19.9 us
    ppermute x8, starting transfers between devices, moved_by(): lax.ppermute(value, axis, [(source, source + steps) for source in range(l...  16.6 us
    pallas_call x6, Pallas kernels, pack(): pl.pallas_call(functools.partial(pack_kernel, table, len(sources)), in_sp...  15.3 us
  transfers between devices with their start and end apart: 52, of which 27 were waited for; matrix products, arithmetic and copies ran while one was open for 9% of the time, Pallas kernels for 31%

commit v1 on v0

--- a/solution.py
+++ b/solution.py
@@ -849,6 +849,7 @@
 
     return (
         yield from owned(
+            clock,
             lambda place: near["y"][:, place],
             both(keep, came, every, 0, every, every, 1).astype(LOW),
             lambda place: near["x"][:, :, place],
@@ -858,16 +859,23 @@
     )
 
 
-def owned(near_y, far_y, near_x, far_x, meanwhile=None):
+def owned(clock, near_y, far_y, near_x, far_x, meanwhile=None):
     from_y, from_x = yield [(far_y, "rows", 2), (far_x, "chan", 1)] + (
         [meanwhile] if meanwhile else []
     )
     rest = lambda place: wide_of(near_y(place)) + wide_of(from_y[:, place])
     also = lambda place: wide_of(near_x(place)) + wide_of(from_x[:, :, place])
+    held = [from_y, from_x]
+
+    def later():
+        held[:] = clock.tick(held)
+
     rest_came, also_came = yield [
         (rest(1).astype(LOW), "chan", 1),
         (also(1).astype(LOW), "rows", 2),
+        later,
     ]
+    from_y, from_x = held
     rest, also = rest(0), also(0)
     parts = {}
     for index in range(rest.shape[0]):
@@ -900,9 +908,10 @@
     return four.reshape(matrices, 4 * part, lanes).astype(WIDE)
 
 
-def finish_rest_kernel(place, pair, came, into, gelu, out, gates, lines):
+def finish_rest_kernel(place, pair, came, time, into, gelu, out, decay, gate, lines, held):
+    del time
     part, model = pair.shape[2], into.shape[1]
-    lanes = gates.shape[1]
+    lanes = decay.shape[1]
     for quarter in range(4):
         turn = quarter ^ place[1]
         own, other = (ref[turn // 2, 0].astype(WIDE) for ref in (pair, came))
@@ -911,24 +920,30 @@
         into[rows, :] = value[:, 0:model]
         gelu[rows, :] = value[:, model : 2 * model]
         out[rows, :] = value[:, 2 * model : 3 * model]
-        gates[rows, :] = value[:, 3 * model : 3 * model + lanes]
-        lines[rows, :] = value[:, 3 * model + lanes :]
-
-
-def finish_rest(place, pair, came, model, width):
+        decay[rows, :] = value[:, 3 * model : 3 * model + lanes]
+        gate[rows, :] = value[:, 3 * model + lanes : 3 * model + 2 * lanes]
+        held[rows, :] = value[:, 3 * model + 2 * lanes :]
+    lines[...] = jnp.transpose(held[...])[:16]
+
+
+def finish_rest(place, pair, came, time, model, block):
     rows = 4 * pair.shape[2]
     vmem = pl.BlockSpec(memory_space=pltpu.VMEM)
     shape = lambda lanes: jax.ShapeDtypeStruct((rows, lanes), WIDE)
     return pl.pallas_call(
         finish_rest_kernel,
         grid_spec=pltpu.PrefetchScalarGridSpec(
-            num_scalar_prefetch=1, grid=(1,), in_specs=[vmem] * 2, out_specs=[vmem] * 5
+            num_scalar_prefetch=1,
+            grid=(1,),
+            in_specs=[vmem, vmem, pl.BlockSpec(memory_space=pl.ANY)],
+            out_specs=[vmem] * 6,
+            scratch_shapes=[pltpu.VMEM((rows, 128), WIDE)],
         ),
-        out_shape=[shape(model)] * 3 + [shape(width), shape(128)],
+        out_shape=[shape(model)] * 3 + [shape(block)] * 2 + [jax.ShapeDtypeStruct((16, rows), WIDE)],
         compiler_params=params(),
         cost_estimate=cost(3),
         name="finish_rest",
-    )(place, pair, came)
+    )(place, pair, came, time)
 
 
 def finish_kernel(place, pair, came, gate, up, down):
@@ -1231,7 +1246,11 @@
     near_x, far_x = clock.tick(feed_grads(1, *operands))
     moving.append(swapped(far_x, "chan", 1))
     stages = owned(
-        lambda place: split(near_y)[:, place], far_y, lambda place: near_x[:, :, place], far_x
+        clock,
+        lambda place: split(near_y)[:, place],
+        far_y,
+        lambda place: near_x[:, :, place],
+        far_x,
     )
     next(stages)
     fed = Sums(clock, stages, start=False)
@@ -1257,21 +1276,21 @@
     scale = lax.rsqrt(jnp.mean(tokens * tokens, axis=-1, keepdims=True) + 1e-06)
     gained = mixer_gain * error
     mean = jnp.mean(gained * tokens, axis=-1, keepdims=True)
-    tokens_grad = clock.tick(mid_grad + scale * gained - tokens * (scale * scale * scale * mean))
     mixer_gain_sum = jnp.sum(error * tokens * scale, 0)
 
     gains = Sums(clock, everywhere(jnp.stack([mixer_gain_sum, jnp.sum(feed_gain_sum, 0)])))
     gains.step()
     rest.step(pin=True)
     fed.step()
-    gains.moving = clock.tick(gains.moving)
+    gains.moving, gained, mean = clock.tick((gains.moving, gained, mean))
+    tokens_grad = clock.tick(mid_grad + scale * gained - tokens * (scale * scale * scale * mean))
     rest.step(pin=True)
     rest.step(pin=True)
     gains.step()
     gains.step()
+    gains.step()
     fed.step()
     fed = Sums(clock, settled(fed.result))
-    gains.step()
     fed.step()
     gains = gains.finish()
     rest.step()
@@ -1279,16 +1298,17 @@
     fed.step()
     feed_sum = clock.tick(finish(jnp.stack([me, row_place]).astype(jnp.int32), *fed.result))
     pair, came = rest.finish()
-    gains = gains + clock.time[:1, :1]
     if pair.shape[2] % 8:
         whole = ordered(pair, came)[0]
+        gains = gains + clock.time[:1, :1]
         input_sum, gelu_sum, out_sum = (whole[:, k * model : (k + 1) * model] for k in range(3))
-        gates_sum, lines = whole[:, 3 * model : 3 * model + width], whole[:, 3 * model + width :]
+        gates_sum = whole[:, 3 * model : 3 * model + width]
+        decay_sum, gate_sum = gates_sum[:, :block], gates_sum[:, block:]
+        lines = whole[:, 3 * model + width : 3 * model + width + 11].T
     else:
-        input_sum, gelu_sum, out_sum, gates_sum, lines = finish_rest(
-            jnp.stack([me, row_place]).astype(jnp.int32), pair, came, model, width
+        input_sum, gelu_sum, out_sum, decay_sum, gate_sum, lines = finish_rest(
+            jnp.stack([me, row_place]).astype(jnp.int32), pair, came, clock.time, model, block
         )
-    lines = lines[:, :11].T
     mean_decay = lines[10] / (length * lax.axis_size("rows") * chans)
     return (
         block_output,
@@ -1299,9 +1319,9 @@
         lines[1],
         lines[2:6],
         lines[6],
-        gates_sum[:, :block],
+        decay_sum,
         lines[7],
-        gates_sum[:, block:],
+        gate_sum,
         lines[8],
         lines[9],
         out_sum,

time: 509 us -> 509 us (level)
  local copies, waits for them, and re-layouts: 21 us -> 26.4 us
    unnamed x119 -> x150, local copies, waits for them, and re-layouts: 9.41 us -> 16.1 us
  transfers between devices with their start and end apart: 52 -> 52, of which waited for: 27 -> 30; matrix products, arithmetic and copies ran while one was open for 9% -> 10% of each run, Pallas kernels for 31% -> 31%
where the time goes in v1:
time: 509 us; the launch traced here: 502 us
  Pallas kernels  192 us (38%)
  waiting for transfers between devices  155 us (30%)
  starting transfers between devices  63.1 us (12%)
  other arithmetic  50.1 us (10%)
  local copies, waits for them, and re-layouts  26.4 us (5%)
  between operations  15.7 us (3%)
    ppermute x43, waiting for transfers between devices, swapped(): lax.ppermute(value, axis, [(source, source ^ bits) for source in range(co...  148 us
    pallas_call x2, Pallas kernels, mixer_back(): pl.pallas_call(functools.partial(mixer_back_kernel, rows, not so_far), gr...  50.3 us
    ppermute x43, starting transfers between devices, swapped(): lax.ppermute(value, axis, [(source, source ^ bits) for source in range(co...  46.2 us
    pallas_call x1, Pallas kernels, feed(): pl.pallas_call(functools.partial(feed_kernel, group), grid_spec=pltpu.Pre...  34.4 us
    pallas_call x2, Pallas kernels, feed_grads(): pl.pallas_call(functools.partial(feed_grads_kernel, parity, count), grid=...  21.4 us
    pallas_call x1, Pallas kernels, mixer_forward(): pl.pallas_call(mixer_forward_kernel, grid=(pairs,), in_specs=[whole(norme...  20 us
    ppermute x8, starting transfers between devices, moved_by(): lax.ppermute(value, axis, [(source, source + steps) for source in range(l...  16.9 us
    unnamed x150, local copies, waits for them, and re-layouts  16.1 us
  transfers between devices with their start and end apart: 52, of which 30 were waited for; matrix products, arithmetic and copies ran while one was open for 10% of the time, Pallas kernels for 31%

profile of v1, /device:TPU:0, one launch (start us, length us, event | category | flops | bytes accessed | tf_op | source)
XLA Modules:
  0.0 501.7 jit_solution(614082137659533743)
XLA Ops:
  11.6 3.1 collective-permute-start.1
  14.7 2.6 collective-permute-start.2
  17.4 3.6 collective-permute-start
  24.3 5.0 %collective-permute-done.2.refs_2_ = bf16[1,80,1024]{2,1,0:T(8,128)(2,1)S(1)} collective-permute-done((bf16[1,80,1024]{2,1,0:T(8,128)(2,1)S(1)}, bf16[1,80,1024]{2,1,0:T(8,128)(2,1)S(1)}, u32[]{:S(2)}, u32[]{:S(2)}) %collective-permute-start.2) | collective-permute-done | bytes 163872 | tf_op jit(solution)/shard_map/ppermute | solution.py:31
  29.3 7.8 %collective-permute-done.3.refs_3_ = bf16[1,80,1024]{2,1,0:T(8,128)(2,1)S(1)} collective-permute-done((bf16[1,80,1024]{2,1,0:T(8,128)(2,1)S(1)}, bf16[1,80,1024]{2,1,0:T(8,128)(2,1)S(1)}, u32[]{:S(2)}, u32[]{:S(2)}) %collective-permute-start.3) | collective-permute-done | bytes 163872 | tf_op jit(solution)/shard_map/ppermute | solution.py:31
  38.5 2.1 pack.6
  42.9 2.8 collective-permute-start.6
  48.4 12.0 %collective-permute-done.6.refs_2_ = bf16[1,96,1024]{2,1,0:T(8,128)(2,1)S(1)} collective-permute-done((bf16[1,96,1024]{2,1,0:T(8,128)(2,1)S(1)}, bf16[1,96,1024]{2,1,0:T(8,128)(2,1)S(1)}, u32[]{:S(2)}, u32[]{:S(2)}) %collective-permute-start.6) | collective-permute-done | bytes 196640 | tf_op jit(solution)/shard_map/ppermute | solution.py:31
  60.5 11.1 %collective-permute-done.7.refs_3_ = bf16[1,96,1024]{2,1,0:T(8,128)(2,1)S(1)} collective-permute-done((bf16[1,96,1024]{2,1,0:T(8,128)(2,1)S(1)}, bf16[1,96,1024]{2,1,0:T(8,128)(2,1)S(1)}, u32[]{:S(2)}, u32[]{:S(2)}) %collective-permute-start.7) | collective-permute-done | bytes 196640 | tf_op jit(solution)/shard_map/ppermute | solution.py:31
  72.5 2.5 pack.7
  75.0 2.3 pack.8
  79.3 2.1 collective-permute-done.9.refs_2_
  81.4 9.5 %collective-permute-done.8.refs_1_ = bf16[5,80,1024]{2,1,0:T(8,128)(2,1)S(1)} collective-permute-done((bf16[5,80,1024]{2,1,0:T(8,128)(2,1)S(1)}, bf16[5,80,1024]{2,1,0:T(8,128)(2,1)S(1)}, u32[]{:S(2)}, u32[]{:S(2)}) %collective-permute-start.8) | collective-permute-done | bytes 819232 | tf_op jit(solution)/shard_map/ppermute | solution.py:31
  90.9 7.3 %collective-permute-done.10.refs_1_ = bf16[5,96,1024]{2,1,0:T(8,128)(2,1)S(1)} collective-permute-done((bf16[5,96,1024]{2,1,0:T(8,128)(2,1)}, bf16[5,96,1024]{2,1,0:T(8,128)(2,1)S(1)}, u32[]{:S(2)}, u32[]{:S(2)}) %collective-permute-start.10) | collective-permute-done | bytes 983072 | tf_op jit(solution)/shard_map/ppermute | solution.py:31
  98.2 3.0 pack.10.refs_3_
  101.2 2.7 pack.9
  106.3 2.1 collective-permute-done.13.refs_4_
  109.6 6.1 %assemble.2 = (bf16[32,48,1024]{2,1,0:T(8,128)(2,1)}, bf16[32,32,1024]{2,1,0:T(8,128)(2,1)}) custom-call(s32[2]{0:T(128)} %pad_add_fusion.1.place, bf16[4,80,1024]{2,1,0:T(8,128)(2,1)} %pad_maximum_fusion.4.refs_0_, bf16[4,80,1024]{2,1,0:T(8,128)(2,1)} %get-tuple-element.334.refs_1_, bf16[4,80,1024]{2,1,0:T(8,128)(2,1)} %copy-done.48, ...), custom_call_target="tpu_custom_call" | custom-call | flops 55000000 | bytes 175000 | tf_op jit(solution)/shard_map/assemble/pallas_call | solution.py:1093
  118.2 20.0 %mixer_forward.1 = (f32[528,1536]{1,0:T(8,128)}, f32[512,1536]{1,0:T(8,128)}, f32[512,1536]{1,0:T(8,128)}, f32[512,1536]{1,0:T(8,128)}, f32[512,1536]{1,0:T(8,12...) custom-call(bf16[528,1024]{1,0:T(8,128)(2,1)} %multiply_convert_fusion.normed, bf16[1536,1024]{1,0:T(8,128)(2,1)} %bitcast.196, ...), custom_call_target="tpu_custom_call" | custom-call | flops 286000000 | bytes 910000 | tf_op jit(solution)/shard_map/mixer_forward/pallas_call | solution.py:213
  139.9 9.9 %collective-permute-done.11.refs_1_ = bf16[5,96,1024]{2,1,0:T(8,128)(2,1)S(1)} collective-permute-done((bf16[5,96,1024]{2,1,0:T(8,128)(2,1)}, bf16[5,96,1024]{2,1,0:T(8,128)(2,1)S(1)}, u32[]{:S(2)}, u32[]{:S(2)}) %collective-permute-start.11) | collective-permute-done | bytes 983072 | tf_op jit(solution)/shard_map/ppermute | solution.py:31
  150.8 2.8 pack.11.refs_3_
  155.6 1.8 collective-permute-done.15
  158.8 4.7 collective-permute-start.17
  164.9 6.8 %assemble.3 = (bf16[32,48,1024]{2,1,0:T(8,128)(2,1)}, bf16[32,48,1024]{2,1,0:T(8,128)(2,1)}) custom-call(s32[2]{0:T(128)} %pad_add_fusion.1.place, bf16[4,96,1024]{2,1,0:T(8,128)(2,1)} %pad_maximum_fusion.2.refs_0_, bf16[4,96,1024]{2,1,0:T(8,128)(2,1)} %get-tuple-element.343.refs_1_, bf16[4,96,1024]{2,1,0:T(8,128)(2,1)} %collective-permute-done.12.refs_2_, ...), custom_call_target="tpu_custom_call" | custom-call | flops 55000000 | bytes 175000 | tf_op jit(solution)/shard_map/assemble/pallas_call | solution.py:1093
  171.8 8.6 %gelu_branch.1 = (f32[512,1536]{1,0:T(8,128)}, f32[512,1536]{1,0:T(8,128)}) custom-call(bf16[528,1024]{1,0:T(8,128)(2,1)} %multiply_convert_fusion.normed, bf16[1536,1024]{1,0:T(8,128)(2,1)} %bitcast.199, f32[16,1536]{1,0:T(8,128)} %select_select_fusion.vec), custom_call_target="tpu_custom_call" | custom-call | flops 88000000 | bytes 280000 | tf_op jit(solution)/shard_map/gelu_branch/pallas_call | solution.py:252
  181.0 8.0 %mixer_out.1 = (bf16[512,1536]{1,0:T(8,128)(2,1)}, f32[512,1024]{1,0:T(8,128)}, bf16[512,1024]{1,0:T(8,128)(2,1)}) custom-call(f32[512,1536]{1,0:T(8,128)} %get-tuple-element.382.active.active_in, f32[512,1536]{1,0:T(8,128)} %get-tuple-element.362.h, f32[512,1536]{1,0:T(8,128)} %get-tuple-element.361.f, f32[1,1536]{1,0:T(1,128)} %broadcast_select_fusion.3.state, ...), custom_call_target="tpu_custom_call" | custom-call | flops 99000000 | bytes 315000 | tf_op jit(solution)/shard_map/mixer_out/pallas_call | solution.py:288
  189.0 34.4 %feed.1 = (f32[512,1024]{1,0:T(8,128)}, f32[512,1024]{1,0:T(8,128)}, bf16[8,3,192,512]{3,2,1,0:T(8,128)(2,1)}, bf16[8,3,192,512]{3,2,1,0:T(8,128)(2,1)}) custom-call(s32[2]{0:T(128)} %pad_add_fusion.1.place, bf16[512,1024]{1,0:T(8,128)(2,1)} %get-tuple-element.397.normed, bf16[512,1024]{1,0:T(8,128)(2,1)} %copy-done.16, ...), custom_call_target="tpu_custom_call" | custom-call | flops 374000000 | bytes 1190000 | tf_op jit(solution)/shard_map/feed/pallas_call | solution.py:413
  224.0 12.3 %middle_back.1 = (f32[512,1024]{1,0:T(8,128)}, bf16[512,1024]{1,0:T(8,128)(2,1)}, f32[512,1536]{1,0:T(8,128)}, bf16[512,1536]{1,0:T(8,128)(2,1)}, f32[8,1024]{1,...) custom-call(f32[512,1024]{1,0:T(8,128)} %get-tuple-element.398.out_in.middle, f32[512,1024]{1,0:T(8,128)} %get-tuple-element.409.grad, ...), custom_call_target="tpu_custom_call" | custom-call | flops 143000000 | bytes 455000 | tf_op jit(solution)/shard_map/middle_back/pallas_call | solution.py:532
  237.2 2.1 collective-permute-start.20
  240.3 11.6 %feed_grads.3 = (bf16[2,3,2,96,1024]{4,3,2,1,0:T(8,128)(2,1)}, bf16[2,3,2,96,1024]{4,3,2,1,0:T(8,128)(2,1)}) custom-call(bf16[8,3,192,512]{3,2,1,0:T(8,128)(2,1)} %get-tuple-element.430.mine, bf16[8,3,192,512]{3,2,1,0:T(8,128)(2,1)} %collective-permute-done.21.theirs, bf16[512,1024]{1,0:T(8,128)(2,1)} %get-tuple-element.397.normed, ...), custom_call_target="tpu_custom_call" | custom-call | flops 22000001024 | bytes 70000000 | tf_op jit(solution)/shard_map/feed_grads/pallas_call | solution.py:475
  251.9 9.7 %feed_grads.2 = (bf16[4,3,96,1024]{3,2,1,0:T(8,128)(2,1)}, bf16[4,3,96,1024]{3,2,1,0:T(8,128)(2,1)}) custom-call(bf16[8,3,192,512]{3,2,1,0:T(8,128)(2,1)} %get-tuple-element.430.mine, bf16[8,3,192,512]{3,2,1,0:T(8,128)(2,1)} %collective-permute-done.21.theirs, bf16[512,1024]{1,0:T(8,128)(2,1)} %get-tuple-element.397.normed, bf16[512,1024]{1,0:T(8,128)(2,1)} %copy-done.16, ...), custom_call_target="tpu_custom_call" | custom-call | flops 22000001024 | bytes 70000000 | tf_op jit(solution)/shard_map/feed_grads/pallas_call | solution.py:475
  270.1 2.2 collective-permute-done.24
  272.3 3.4 collective-permute-done.25
  276.3 33.9 %mixer_back.2 = (bf16[8,1,2,48,3584]{4,3,2,1,0:T(8,128)(2,1)}, bf16[8,1,2,48,3584]{4,3,2,1,0:T(8,128)(2,1)}, f32[528,1024]{1,0:T(8,128)}) custom-call(s32[3]{0:T(128)} %pad_add_fusion.2.place, f32[512,1536]{1,0:T(8,128)} %get-tuple-element.420.state_grad, f32[512,1536]{1,0:T(8,128)} %get-tuple-element.421.r_in, f32[512,1536]{1,0:T(8,128)} %get-tuple-element.422.i_in, ...), custom_call_target="tpu_custom_call" | custom-call | flops 495000000 | bytes 1575000 | tf_op jit(solution)/shard_map/mixer_back/pallas_call | solution.py:714
  310.1 6.4 %collective-permute-done.27 = bf16[2,3,2,96,1024]{4,3,1,2,0:T(8,128)(2,1)S(1)} collective-permute-done((bf16[2,3,2,96,1024]{4,3,1,2,0:T(8,128)(2,1)}, bf16[2,3,2,96,1024]{4,3,1,2,0:T(8,128)(2,1)S(1)}, u32[]{:S(2)}, u32[]{:S(2)}) %collective-permute-start.27) | collective-permute-done | bytes 2359328 | tf_op jit(solution)/shard_map/ppermute | solution.py:31
  318.0 1.7 fusion.4
  321.3 16.5 %mixer_back.3 = (bf16[8,1,2,48,3584]{4,3,2,1,0:T(8,128)(2,1)}, bf16[8,1,2,48,3584]{4,3,2,1,0:T(8,128)(2,1)}, f32[528,1024]{1,0:T(8,128)}) custom-call(s32[3]{0:T(128)} %pad_add_fusion.2.place, f32[512,1536]{1,0:T(8,128)} %get-tuple-element.420.state_grad, f32[512,1536]{1,0:T(8,128)} %get-tuple-element.421.r_in, ...), custom_call_target="tpu_custom_call", output_to_operand_aliasing={{0}: (21, {}), {1}: (22, {})} | custom-call | flops 165000000 | bytes 525000 | tf_op jit(solution)/shard_map/mixer_back/pallas_call | solution.py:714
  337.8 8.9 %collective-permute-done.28 = bf16[2,3,96,1024]{3,2,1,0:T(8,128)(2,1)S(1)} collective-permute-done((bf16[2,3,96,1024]{3,2,1,0:T(8,128)(2,1)S(1)}, bf16[2,3,96,1024]{3,2,1,0:T(8,128)(2,1)S(1)}, u32[]{:S(2)}, u32[]{:S(2)}) %collective-permute-start.28) | collective-permute-done | bytes 1179680 | tf_op jit(solution)/shard_map/ppermute | solution.py:31
  349.8 3.7 convert_add_fusion
  353.5 1.8 collective-permute-start.30
  355.3 3.5 convert_add_fusion.1
  359.4 1.9 multiply_reduce_fusion.1
  363.3 2.7 fusion.2
  366.0 2.7 fusion.1
  370.8 2.0 collective-permute-start.35
  372.8 2.1 add_bitcast_fusion
  375.0 3.1 add_bitcast_fusion.1
  380.2 1.7 copy-done.8
  383.9 1.7 multiply_subtract_fusion
  385.7 4.2 collective-permute-start.46
  390.0 11.6 %collective-permute-done.34 = bf16[2,2,1,48,3584]{4,3,2,1,0:T(8,128)(2,1)S(1)} collective-permute-done((bf16[2,2,1,48,3584]{4,3,2,1,0:T(8,128)(2,1)}, bf16[2,2,1,48,3584]{4,3,2,1,0:T(8,128)(2,1)S(1)}, u32[]{:S(2)}, u32[]{:S(2)}) %collective-permute-start.34) | collective-permute-done | bytes 1376288 | tf_op jit(solution)/shard_map/ppermute | solution.py:31
  405.1 1.7 collective-permute-start.36
  410.6 1.7 convert_add_fusion.2
  412.3 9.4 %collective-permute-done.36 = bf16[2,1,48,3584]{3,2,1,0:T(8,128)(2,1)S(1)} collective-permute-done((bf16[2,1,48,3584]{3,2,1,0:T(8,128)(2,1)}, bf16[2,1,48,3584]{3,2,1,0:T(8,128)(2,1)S(1)}, u32[]{:S(2)}, u32[]{:S(2)}) %collective-permute-start.36) | collective-permute-done | bytes 688160 | tf_op jit(solution)/shard_map/ppermute | solution.py:31
  423.1 2.1 fusion.40
  426.6 3.0 collective-permute-done.41
  430.4 2.9 collective-permute-done.42
  433.3 2.1 fusion.11
  436.1 6.7 %collective-permute-start.38 = (bf16[1,48,3584]{2,1,0:T(8,128)(2,1)S(1)}, bf16[1,48,3584]{2,1,0:T(8,128)(2,1)S(1)}, u32[]{:S(2)}, u32[]{:S(2)}) collective-permute-start(bf16[1,48,3584]{2,1,0:T(8,128)(2,1)S(1)} %copy-done.51), channel_id=1, source_target_pairs={{0,2},{1,3},{2,0},{3,1},{4,6},{5,7},{6,4},{7,5},{8,10},{9,11},{10,... | collective-permute-start | bytes 1032200 | tf_op jit(solution)/shard_map/ppermute | solution.py:31
  442.9 2.4 collective-permute-start.40
  446.6 27.6 %collective-permute-done.43 = f32[2,1024]{1,0:T(2,128)S(1)} collective-permute-done((f32[2,1024]{1,0:T(2,128)S(1)}, f32[2,1024]{1,0:T(2,128)S(1)}, u32[]{:S(2)}, u32[]{:S(2)}) %collective-permute-start.43) | collective-permute-done | bytes 8224 | tf_op jit(solution)/shard_map/ppermute | solution.py:31
  478.0 4.9 finish.1
  482.9 2.0 collective-permute-done.48
  488.1 3.6 finish_rest.1
  (318 shorter events, 79.8 us)
Async XLA Ops:
  7.2 181.7 %all-gather.3.cloned.1.call-start = ((), (), s32[]{:S(2)}) async-start(), calls=%async_computation | async-start | bytes 19464192 | tf_op jit(solution)/shard_map/all_gather | solution.py:1190
  11.6 25.5 %collective-permute-start.1 = (bf16[2,80,1024]{2,1,0:T(8,128)(2,1)S(1)}, bf16[2,80,1024]{2,1,0:T(8,128)(2,1)S(1)}, u32[]{:S(2)}, u32[]{:S(2)}) collective-permute-start(bf16[2,80,1024]{2,1,0:T(8,128)(2,1)S(1)} %pad_maximum_fusion.7), channel_id=1, source_target_pairs={{0,2},{1,3},{2,0},{3,1},{4,6},{5,7},{6,4},{7,5},{8,10},{9,11},{10,... | collective-permute-start | bytes 983048 | tf_op jit(solution)/shard_map/ppermute | solution.py:31
  14.7 14.6 %collective-permute-start.2 = (bf16[1,80,1024]{2,1,0:T(8,128)(2,1)S(1)}, bf16[1,80,1024]{2,1,0:T(8,128)(2,1)S(1)}, u32[]{:S(2)}, u32[]{:S(2)}) collective-permute-start(bf16[1,80,1024]{2,1,0:T(8,128)(2,1)S(1)} %get-tuple-element.311), channel_id=1, source_target_pairs={{0,4},{1,5},{2,6},{3,7},{4,0},{5,1},{6,2},{7,3},{8,12},{9,13},{10,... | collective-permute-start | bytes 491528 | tf_op jit(solution)/shard_map/ppermute | solution.py:31
  17.3 19.8 %collective-permute-start.3 = (bf16[1,80,1024]{2,1,0:T(8,128)(2,1)S(1)}, bf16[1,80,1024]{2,1,0:T(8,128)(2,1)S(1)}, u32[]{:S(2)}, u32[]{:S(2)}) collective-permute-start(bf16[1,80,1024]{2,1,0:T(8,128)(2,1)S(1)} %get-tuple-element.311), channel_id=1, source_target_pairs={{0,6},{1,7},{2,4},{3,5},{4,2},{5,3},{6,0},{7,1},{8,14},{9,15},{10,... | collective-permute-start | bytes 491528 | tf_op jit(solution)/shard_map/ppermute | solution.py:31
  17.4 24.8 %collective-permute-start = (f32[3,1024]{1,0:T(4,128)S(1)}, f32[3,1024]{1,0:T(4,128)S(1)}, u32[]{:S(2)}, u32[]{:S(2)}) collective-permute-start(f32[3,1024]{1,0:T(4,128)S(1)} %slice.283), channel_id=1, source_target_pairs={{0,1},{1,2},{2,3},{3,4},{4,5},{5,6},{6,7},{8,9},{9,10},{10,11},{11... | collective-permute-start | bytes 36872 | tf_op jit(solution)/shard_map/ppermute | solution.py:26
  40.6 30.9 %collective-permute-start.4 = (bf16[5,80,1024]{2,1,0:T(8,128)(2,1)}, bf16[5,80,1024]{2,1,0:T(8,128)(2,1)S(1)}, u32[]{:S(2)}, u32[]{:S(2)}) collective-permute-start(bf16[5,80,1024]{2,1,0:T(8,128)(2,1)} %pack.6), channel_id=1, source_target_pairs={{0,1},{1,0},{2,3},{3,2},{4,5},{5,4},{6,7},{7,6},{8,9},{9,8},{10,11... | collective-permute-start | bytes 2457608 | tf_op jit(solution)/shard_map/ppermute | solution.py:31
  42.4 29.1 %collective-permute-start.5 = (bf16[2,96,1024]{2,1,0:T(8,128)(2,1)S(1)}, bf16[2,96,1024]{2,1,0:T(8,128)(2,1)S(1)}, u32[]{:S(2)}, u32[]{:S(2)}) collective-permute-start(bf16[2,96,1024]{2,1,0:T(8,128)(2,1)S(1)} %pad_maximum_fusion.6), channel_id=1, source_target_pairs={{0,2},{1,3},{2,0},{3,1},{4,6},{5,7},{6,4},{7,5},{8,10},{9,11},{10,... | collective-permute-start | bytes 1179656 | tf_op jit(solution)/shard_map/ppermute | solution.py:31
  42.9 17.6 %collective-permute-start.6 = (bf16[1,96,1024]{2,1,0:T(8,128)(2,1)S(1)}, bf16[1,96,1024]{2,1,0:T(8,128)(2,1)S(1)}, u32[]{:S(2)}, u32[]{:S(2)}) collective-permute-start(bf16[1,96,1024]{2,1,0:T(8,128)(2,1)S(1)} %get-tuple-element.324), channel_id=1, source_target_pairs={{0,4},{1,5},{2,6},{3,7},{4,0},{5,1},{6,2},{7,3},{8,12},{9,13},{10,... | collective-permute-start | bytes 589832 | tf_op jit(solution)/shard_map/ppermute | solution.py:31
  45.7 25.8 %collective-permute-start.7 = (bf16[1,96,1024]{2,1,0:T(8,128)(2,1)S(1)}, bf16[1,96,1024]{2,1,0:T(8,128)(2,1)S(1)}, u32[]{:S(2)}, u32[]{:S(2)}) collective-permute-start(bf16[1,96,1024]{2,1,0:T(8,128)(2,1)S(1)} %get-tuple-element.324), channel_id=1, source_target_pairs={{0,6},{1,7},{2,4},{3,5},{4,2},{5,3},{6,0},{7,1},{8,14},{9,15},{10,... | collective-permute-start | bytes 589832 | tf_op jit(solution)/shard_map/ppermute | solution.py:31
  77.3 26.7 %copy-start.61 = (s32[4096]{0:T(1024)S(1)}, s32[4096]{0:T(1024)}, u32[]{:S(2)}) copy-start(s32[4096]{0:T(1024)} %param.21) | copy-start | bytes 49156
  77.3 20.9 %collective-permute-start.10 = (bf16[5,96,1024]{2,1,0:T(8,128)(2,1)}, bf16[5,96,1024]{2,1,0:T(8,128)(2,1)S(1)}, u32[]{:S(2)}, u32[]{:S(2)}) collective-permute-start(bf16[5,96,1024]{2,1,0:T(8,128)(2,1)} %pack.8), channel_id=1, source_target_pairs={{0,1},{1,0},{2,3},{3,2},{4,5},{5,4},{6,7},{7,6},{8,9},{9,8},{10,11... | collective-permute-start | bytes 2949128 | tf_op jit(solution)/shard_map/ppermute | solution.py:31
  78.1 12.8 %collective-permute-start.8 = (bf16[5,80,1024]{2,1,0:T(8,128)(2,1)S(1)}, bf16[5,80,1024]{2,1,0:T(8,128)(2,1)S(1)}, u32[]{:S(2)}, u32[]{:S(2)}) collective-permute-start(bf16[5,80,1024]{2,1,0:T(8,128)(2,1)S(1)} %copy-done.37), channel_id=1, source_target_pairs={{0,16},{8,24},{16,0},{24,8},{1,17},{9,25},{17,1},{25,9},{2,18},{10... | collective-permute-start | bytes 2457608 | tf_op jit(solution)/shard_map/ppermute | solution.py:31
  79.3 2.1 collective-permute-start.9
  81.4 26.9 %copy-start.48 = (bf16[4,80,1024]{2,1,0:T(8,128)(2,1)}, bf16[4,80,1024]{2,1,0:T(8,128)(2,1)S(1)}, u32[]{:S(2)}) copy-start(bf16[4,80,1024]{2,1,0:T(8,128)(2,1)S(1)} %collective-permute-done.9.refs_2_) | copy-start | bytes 1966084
  103.9 4.4 collective-permute-start.13
  105.8 44.0 %collective-permute-start.11 = (bf16[5,96,1024]{2,1,0:T(8,128)(2,1)}, bf16[5,96,1024]{2,1,0:T(8,128)(2,1)S(1)}, u32[]{:S(2)}, u32[]{:S(2)}) collective-permute-start(bf16[5,96,1024]{2,1,0:T(8,128)(2,1)} %get-tuple-element.342.refs_0_), channel_id=1, source_target_pairs={{0,16},{8,24},{16,0},{24,8},{1,17},{9,25},{17,1},{25,9},{2,18},{10... | collective-permute-start | bytes 2949128 | tf_op jit(solution)/shard_map/ppermute | solution.py:31
  105.8 34.1 %collective-permute-start.12 = (bf16[4,96,1024]{2,1,0:T(8,128)(2,1)}, bf16[4,96,1024]{2,1,0:T(8,128)(2,1)}, u32[]{:S(2)}, u32[]{:S(2)}) collective-permute-start(bf16[4,96,1024]{2,1,0:T(8,128)(2,1)} %get-tuple-element.343.refs_1_), channel_id=1, source_target_pairs={{0,8},{8,0},{16,24},{24,16},{1,9},{9,1},{17,25},{25,17},{2,10},{10... | collective-permute-start | bytes 2359304 | tf_op jit(solution)/shard_map/ppermute | solution.py:31
  153.6 11.4 %collective-permute-start.14 = (bf16[10,96,1024]{2,1,0:T(8,128)(2,1)}, bf16[10,96,1024]{2,1,0:T(8,128)(2,1)}, u32[]{:S(2)}, u32[]{:S(2)}) collective-permute-start(bf16[10,96,1024]{2,1,0:T(8,128)(2,1)} %pack.11.refs_3_), channel_id=1, source_target_pairs={{0,8},{8,0},{16,24},{24,16},{1,9},{9,1},{17,25},{25,17},{2,10},{10... | collective-permute-start | bytes 5898248 | tf_op jit(solution)/shard_map/ppermute | solution.py:31
  153.7 3.8 collective-permute-start.15
  155.4 33.6 %collective-permute-start.19 = (bf16[512,1024]{1,0:T(8,128)(2,1)S(1)}, bf16[512,1024]{1,0:T(8,128)(2,1)S(1)}, u32[]{:S(2)}, u32[]{:S(2)}) collective-permute-start(bf16[512,1024]{1,0:T(8,128)(2,1)S(1)} %convert_element_type.424.cot), channel_id=1, source_target_pairs={{0,8},{8,0},{16,24},{24,16},{1,9},{9,1},{17,25},{25,17},{2,10},{10... | collective-permute-start | bytes 3145736 | tf_op jit(solution)/shard_map/ppermute | solution.py:31
  157.5 22.9 %collective-permute-start.16 = (f32[2,1536]{1,0:T(2,128)S(1)}, f32[2,1536]{1,0:T(2,128)S(1)}, u32[]{:S(2)}, u32[]{:S(2)}) collective-permute-start(f32[2,1536]{1,0:T(2,128)S(1)} %pad_maximum_fusion.10), channel_id=1, source_target_pairs={{0,2},{1,3},{2,4},{3,5},{4,6},{5,7},{8,10},{9,11},{10,12},{11,13},... | collective-permute-start | bytes 36872 | tf_op jit(solution)/shard_map/ppermute | solution.py:26
  158.8 21.6 %collective-permute-start.17 = (f32[2,1536]{1,0:T(2,128)S(1)}, f32[2,1536]{1,0:T(2,128)S(1)}, u32[]{:S(2)}, u32[]{:S(2)}) collective-permute-start(f32[2,1536]{1,0:T(2,128)S(1)} %pad_maximum_fusion.10), channel_id=1, source_target_pairs={{0,4},{1,5},{2,6},{3,7},{8,12},{9,13},{10,14},{11,15},{16,20},{17,... | collective-permute-start | bytes 36872 | tf_op jit(solution)/shard_map/ppermute | solution.py:26
  163.5 16.9 %collective-permute-start.18 = (f32[2,1536]{1,0:T(2,128)S(1)}, f32[2,1536]{1,0:T(2,128)S(1)}, u32[]{:S(2)}, u32[]{:S(2)}) collective-permute-start(f32[2,1536]{1,0:T(2,128)S(1)} %pad_maximum_fusion.10), channel_id=1, source_target_pairs={{0,6},{1,7},{8,14},{9,15},{16,22},{17,23},{24,30},{25,31}} | collective-permute-start | bytes 36872 | tf_op jit(solution)/shard_map/ppermute | solution.py:26
  188.9 34.5 %copy-start.70 = (bf16[512,1024]{1,0:T(8,128)(2,1)}, bf16[512,1024]{1,0:T(8,128)(2,1)S(1)}, u32[]{:S(2)}) copy-start(bf16[512,1024]{1,0:T(8,128)(2,1)S(1)} %collective-permute-done.19.cot_too) | copy-start | bytes 3145732
  189.0 34.5 %copy-start.34 = (bf16[512,1024]{1,0:T(8,128)(2,1)S(1)}, bf16[512,1024]{1,0:T(8,128)(2,1)}, u32[]{:S(2)}) copy-start(bf16[512,1024]{1,0:T(8,128)(2,1)} %get-tuple-element.397.normed) | copy-start | bytes 3145732
  223.4 15.8 %collective-permute-start.21 = (bf16[8,3,192,512]{3,2,1,0:T(8,128)(2,1)}, bf16[8,3,192,512]{3,2,1,0:T(8,128)(2,1)}, u32[]{:S(2)}, u32[]{:S(2)}) collective-permute-start(bf16[8,3,192,512]{3,2,1,0:T(8,128)(2,1)} %get-tuple-element.431), channel_id=1, source_target_pairs={{0,8},{8,0},{16,24},{24,16},{1,9},{9,1},{17,25},{25,17},{2,10},{10... | collective-permute-start | bytes 14155784 | tf_op jit(solution)/shard_map/ppermute | solution.py:31
  223.5 15.7 %collective-permute-start.22 = (bf16[512,1024]{1,0:T(8,128)(2,1)S(1)}, bf16[512,1024]{1,0:T(8,128)(2,1)S(1)}, u32[]{:S(2)}, u32[]{:S(2)}) collective-permute-start(bf16[512,1024]{1,0:T(8,128)(2,1)S(1)} %copy-done.34), channel_id=1, source_target_pairs={{0,8},{8,0},{16,24},{24,16},{1,9},{9,1},{17,25},{25,17},{2,10},{10... | collective-permute-start | bytes 3145736 | tf_op jit(solution)/shard_map/ppermute | solution.py:31
  237.2 24.5 %collective-permute-start.20 = (f32[2,1536]{1,0:T(2,128)S(1)}, f32[2,1536]{1,0:T(2,128)S(1)}, u32[]{:S(2)}, u32[]{:S(2)}) collective-permute-start(f32[2,1536]{1,0:T(2,128)S(1)} %pad_maximum_fusion.8), channel_id=1, source_target_pairs={{0,1},{1,0},{2,3},{3,2},{4,5},{5,4},{6,7},{7,6},{8,9},{9,8},{10,11... | collective-permute-start | bytes 36872 | tf_op jit(solution)/shard_map/ppermute | solution.py:31
  263.4 53.2 %collective-permute-start.27 = (bf16[2,3,2,96,1024]{4,3,1,2,0:T(8,128)(2,1)}, bf16[2,3,2,96,1024]{4,3,1,2,0:T(8,128)(2,1)S(1)}, u32[]{:S(2)}, u32[]{:S(2)}) collective-permute-start(bf16[2,3,2,96,1024]{4,3,1,2,0:T(8,128)(2,1)} %copy.105), channel_id=1, source_target_pairs={{0,1},{1,0},{2,3},{3,2},{4,5},{5,4},{6,7},{7,6},{8,9},{9,8},{10,11... | collective-permute-start | bytes 7077896 | tf_op jit(solution)/shard_map/ppermute | solution.py:31
  263.4 53.3 %collective-permute-start.26 = (bf16[2,2,3,96,1024]{4,3,2,1,0:T(8,128)(2,1)}, bf16[2,2,3,96,1024]{4,3,2,1,0:T(8,128)(2,1)}, u32[]{:S(2)}, u32[]{:S(2)}) collective-permute-start(bf16[2,2,3,96,1024]{4,3,2,1,0:T(8,128)(2,1)} %bitcast.23), channel_id=1, source_target_pairs={{0,16},{8,24},{16,0},{24,8},{1,17},{9,25},{17,1},{25,9},{2,18},{10... | collective-permute-start | bytes 7077896 | tf_op jit(solution)/shard_map/ppermute | solution.py:31
  264.5 5.6 %collective-permute-start.23 = (f32[2,1536]{1,0:T(2,128)S(1)}, f32[2,1536]{1,0:T(2,128)S(1)}, u32[]{:S(2)}, u32[]{:S(2)}) collective-permute-start(f32[2,1536]{1,0:T(2,128)S(1)} %pad_maximum_fusion.11), channel_id=1, source_target_pairs={{2,0},{3,1},{4,2},{5,3},{6,4},{7,5},{10,8},{11,9},{12,10},{13,11},... | collective-permute-start | bytes 36872 | tf_op jit(solution)/shard_map/ppermute | solution.py:26
  265.8 6.5 %collective-permute-start.24 = (f32[2,1536]{1,0:T(2,128)S(1)}, f32[2,1536]{1,0:T(2,128)S(1)}, u32[]{:S(2)}, u32[]{:S(2)}) collective-permute-start(f32[2,1536]{1,0:T(2,128)S(1)} %pad_maximum_fusion.11), channel_id=1, source_target_pairs={{4,0},{5,1},{6,2},{7,3},{12,8},{13,9},{14,10},{15,11},{20,16},{21,... | collective-permute-start | bytes 36872 | tf_op jit(solution)/shard_map/ppermute | solution.py:26
  267.1 8.6 %collective-permute-start.25 = (f32[2,1536]{1,0:T(2,128)S(1)}, f32[2,1536]{1,0:T(2,128)S(1)}, u32[]{:S(2)}, u32[]{:S(2)}) collective-permute-start(f32[2,1536]{1,0:T(2,128)S(1)} %pad_maximum_fusion.11), channel_id=1, source_target_pairs={{6,0},{7,1},{14,8},{15,9},{22,16},{23,17},{30,24},{31,25}} | collective-permute-start | bytes 36872 | tf_op jit(solution)/shard_map/ppermute | solution.py:26
  276.3 40.4 %copy-start.18 = (bf16[2,3,2,96,1024]{4,3,2,1,0:T(8,128)(2,1)S(1)}, bf16[2,3,2,96,1024]{4,3,2,1,0:T(8,128)(2,1)}, u32[]{:S(2)}) copy-start(bf16[2,3,2,96,1024]{4,3,2,1,0:T(8,128)(2,1)} %get-tuple-element.470) | copy-start | bytes 7077892
  319.7 29.0 %copy-start.3 = (f32[512,1024]{1,0:T(8,128)S(1)}, f32[512,1024]{1,0:T(8,128)}, u32[]{:S(2)}) copy-start(f32[512,1024]{1,0:T(8,128)} %tokens.1) | copy-start | bytes 6291460
  319.7 27.0 %collective-permute-start.28 = (bf16[2,3,96,1024]{3,2,1,0:T(8,128)(2,1)S(1)}, bf16[2,3,96,1024]{3,2,1,0:T(8,128)(2,1)S(1)}, u32[]{:S(2)}, u32[]{:S(2)}) collective-permute-start(bf16[2,3,96,1024]{3,2,1,0:T(8,128)(2,1)S(1)} %fusion.4), channel_id=1, source_target_pairs={{0,1},{1,0},{2,3},{3,2},{4,5},{5,4},{6,7},{7,6},{8,9},{9,8},{10,11... | collective-permute-start | bytes 3538952 | tf_op jit(solution)/shard_map/ppermute | solution.py:31
  320.7 26.4 %collective-permute-start.29 = (bf16[2,3,96,1024]{3,2,1,0:T(8,128)(2,1)S(1)}, bf16[2,3,96,1024]{3,2,1,0:T(8,128)(2,1)S(1)}, u32[]{:S(2)}, u32[]{:S(2)}) collective-permute-start(bf16[2,3,96,1024]{3,2,1,0:T(8,128)(2,1)S(1)} %fusion.5), channel_id=1, source_target_pairs={{0,16},{8,24},{16,0},{24,8},{1,17},{9,25},{17,1},{25,9},{2,18},{10... | collective-permute-start | bytes 3538952 | tf_op jit(solution)/shard_map/ppermute | solution.py:31
  347.7 15.5 %collective-permute-start.33 = (bf16[8,1,2,48,3584]{4,3,2,1,0:T(8,128)(2,1)}, bf16[8,1,2,48,3584]{4,3,2,1,0:T(8,128)(2,1)}, u32[]{:S(2)}, u32[]{:S(2)}) collective-permute-start(bf16[8,1,2,48,3584]{4,3,2,1,0:T(8,128)(2,1)} %get-tuple-element.502), channel_id=1, source_target_pairs={{0,8},{8,0},{16,24},{24,16},{1,9},{9,1},{17,25},{25,17},{2,10},{10... | collective-permute-start | bytes 16515080 | tf_op jit(solution)/shard_map/ppermute | solution.py:31
  353.5 5.9 %collective-permute-start.30 = (f32[3,1024]{1,0:T(4,128)S(1)}, f32[3,1024]{1,0:T(4,128)S(1)}, u32[]{:S(2)}, u32[]{:S(2)}) collective-permute-start(f32[3,1024]{1,0:T(4,128)S(1)} %slice.320), channel_id=1, source_target_pairs={{1,0},{2,1},{3,2},{4,3},{5,4},{6,5},{7,6},{9,8},{10,9},{11,10},{12... | collective-permute-start | bytes 36872 | tf_op jit(solution)/shard_map/ppermute | solution.py:26
  361.3 1.2 collective-permute-start.31
  362.6 20.3 %collective-permute-start.32 = (f32[2,1024]{1,0:T(2,128)S(1)}, f32[2,1024]{1,0:T(2,128)S(1)}, u32[]{:S(2)}, u32[]{:S(2)}) collective-permute-start(f32[2,1024]{1,0:T(2,128)S(1)} %fusion.49), channel_id=1, source_target_pairs={{0,16},{8,24},{16,0},{24,8},{1,17},{9,25},{17,1},{25,9},{2,18},{10... | collective-permute-start | bytes 24584 | tf_op jit(solution)/shard_map/ppermute | solution.py:31
  369.4 32.2 %collective-permute-start.34 = (bf16[2,2,1,48,3584]{4,3,2,1,0:T(8,128)(2,1)}, bf16[2,2,1,48,3584]{4,3,2,1,0:T(8,128)(2,1)S(1)}, u32[]{:S(2)}, u32[]{:S(2)}) collective-permute-start(bf16[2,2,1,48,3584]{4,3,2,1,0:T(8,128)(2,1)} %fusion.1), channel_id=1, source_target_pairs={{0,16},{8,24},{16,0},{24,8},{1,17},{9,25},{17,1},{25,9},{2,18},{10... | collective-permute-start | bytes 4128776 | tf_op jit(solution)/shard_map/ppermute | solution.py:31
  370.8 32.2 %collective-permute-start.35 = (bf16[2,1,2,48,3584]{4,3,2,1,0:T(8,128)(2,1)}, bf16[2,1,2,48,3584]{4,3,2,1,0:T(8,128)(2,1)S(1)}, u32[]{:S(2)}, u32[]{:S(2)}) collective-permute-start(bf16[2,1,2,48,3584]{4,3,2,1,0:T(8,128)(2,1)} %fusion.2), channel_id=1, source_target_pairs={{0,1},{1,0},{2,3},{3,2},{4,5},{5,4},{6,7},{7,6},{8,9},{9,8},{10,11... | collective-permute-start | bytes 4128776 | tf_op jit(solution)/shard_map/ppermute | solution.py:31
  374.9 29.2 %copy-start.6 = (f32[2,2,1,48,3584]{4,3,2,1,0:T(8,128)}, f32[2,2,1,48,3584]{4,3,2,1,0:T(8,128)S(1)}, u32[]{:S(2)}) copy-start(f32[2,2,1,48,3584]{4,3,2,1,0:T(8,128)S(1)} %add_bitcast_fusion) | copy-start | bytes 8257540
  378.7 24.2 %copy-start.4 = (f32[2,1,2,48,3584]{4,3,2,1,0:T(8,128)}, f32[2,1,2,48,3584]{4,3,2,1,0:T(8,128)S(1)}, u32[]{:S(2)}) copy-start(f32[2,1,2,48,3584]{4,3,2,1,0:T(8,128)S(1)} %add_bitcast_fusion.1) | copy-start | bytes 8257540
  385.6 47.7 %collective-permute-start.44 = (bf16[3,96,1024]{2,1,0:T(8,128)(2,1)}, bf16[3,96,1024]{2,1,0:T(8,128)(2,1)}, u32[]{:S(2)}, u32[]{:S(2)}) collective-permute-start(bf16[3,96,1024]{2,1,0:T(8,128)(2,1)} %get-tuple-element.553), channel_id=1, source_target_pairs={{0,2},{1,3},{2,0},{3,1},{4,6},{5,7},{6,4},{7,5},{8,10},{9,11},{10,... | collective-permute-start | bytes 1769480 | tf_op jit(solution)/shard_map/ppermute | solution.py:31
  385.7 47.6 %collective-permute-start.45 = (bf16[3,96,1024]{2,1,0:T(8,128)(2,1)}, bf16[3,96,1024]{2,1,0:T(8,128)(2,1)}, u32[]{:S(2)}, u32[]{:S(2)}) collective-permute-start(bf16[3,96,1024]{2,1,0:T(8,128)(2,1)} %fusion.34), channel_id=1, source_target_pairs={{0,4},{1,5},{2,6},{3,7},{4,0},{5,1},{6,2},{7,3},{8,12},{9,13},{10,... | collective-permute-start | bytes 1769480 | tf_op jit(solution)/shard_map/ppermute | solution.py:31
  385.7 47.6 %collective-permute-start.46 = (bf16[3,96,1024]{2,1,0:T(8,128)(2,1)}, bf16[3,96,1024]{2,1,0:T(8,128)(2,1)}, u32[]{:S(2)}, u32[]{:S(2)}) collective-permute-start(bf16[3,96,1024]{2,1,0:T(8,128)(2,1)} %get-tuple-element.555), channel_id=1, source_target_pairs={{0,6},{1,7},{2,4},{3,5},{4,2},{5,3},{6,0},{7,1},{8,14},{9,15},{10,... | collective-permute-start | bytes 1769480 | tf_op jit(solution)/shard_map/ppermute | solution.py:31
  405.1 16.7 %collective-permute-start.36 = (bf16[2,1,48,3584]{3,2,1,0:T(8,128)(2,1)}, bf16[2,1,48,3584]{3,2,1,0:T(8,128)(2,1)S(1)}, u32[]{:S(2)}, u32[]{:S(2)}) collective-permute-start(bf16[2,1,48,3584]{3,2,1,0:T(8,128)(2,1)} %bitcast.47), channel_id=1, source_target_pairs={{0,1},{1,0},{2,3},{3,2},{4,5},{5,4},{6,7},{7,6},{8,9},{9,8},{10,11... | collective-permute-start | bytes 2064392 | tf_op jit(solution)/shard_map/ppermute | solution.py:31
  406.8 16.2 %collective-permute-start.37 = (bf16[2,1,48,3584]{3,2,1,0:T(8,128)(2,1)}, bf16[2,1,48,3584]{3,2,1,0:T(8,128)(2,1)}, u32[]{:S(2)}, u32[]{:S(2)}) collective-permute-start(bf16[2,1,48,3584]{3,2,1,0:T(8,128)(2,1)} %bitcast.48), channel_id=1, source_target_pairs={{0,16},{8,24},{16,0},{24,8},{1,17},{9,25},{17,1},{25,9},{2,18},{10... | collective-permute-start | bytes 2064392 | tf_op jit(solution)/shard_map/ppermute | solution.py:31
  425.9 3.7 collective-permute-start.41
  429.6 3.7 collective-permute-start.42
  435.4 38.7 %copy-start.14 = (f32[2,1,1,48,3584]{4,3,2,1,0:T(8,128)S(1)}, f32[2,1,1,48,3584]{4,3,2,1,0:T(8,128)}, u32[]{:S(2)}) copy-start(f32[2,1,1,48,3584]{4,3,2,1,0:T(8,128)} %copy-done.13) | copy-start | bytes 4128772
  435.4 38.7 %copy-start.43 = (bf16[2,1,48,3584]{3,2,1,0:T(8,128)(2,1)S(1)}, bf16[2,1,48,3584]{3,2,1,0:T(8,128)(2,1)}, u32[]{:S(2)}) copy-start(bf16[2,1,48,3584]{3,2,1,0:T(8,128)(2,1)} %copy-done.42) | copy-start | bytes 2064388
  435.5 11.0 %collective-permute-start.47 = (bf16[3,96,1024]{2,1,0:T(8,128)(2,1)S(1)}, bf16[3,96,1024]{2,1,0:T(8,128)(2,1)S(1)}, u32[]{:S(2)}, u32[]{:S(2)}) collective-permute-start(bf16[3,96,1024]{2,1,0:T(8,128)(2,1)S(1)} %fusion.11), channel_id=1, source_target_pairs={{0,16},{8,24},{16,0},{24,8},{1,17},{9,25},{17,1},{25,9},{2,18},{10... | collective-permute-start | bytes 1769480 | tf_op jit(solution)/shard_map/ppermute | solution.py:31
  436.1 38.0 %collective-permute-start.38 = (bf16[1,48,3584]{2,1,0:T(8,128)(2,1)S(1)}, bf16[1,48,3584]{2,1,0:T(8,128)(2,1)S(1)}, u32[]{:S(2)}, u32[]{:S(2)}) collective-permute-start(bf16[1,48,3584]{2,1,0:T(8,128)(2,1)S(1)} %copy-done.51), channel_id=1, source_target_pairs={{0,2},{1,3},{2,0},{3,1},{4,6},{5,7},{6,4},{7,5},{8,10},{9,11},{10,... | collective-permute-start | bytes 1032200 | tf_op jit(solution)/shard_map/ppermute | solution.py:31
  442.9 31.3 %collective-permute-start.39 = (bf16[1,48,3584]{2,1,0:T(8,128)(2,1)S(1)}, bf16[1,48,3584]{2,1,0:T(8,128)(2,1)S(1)}, u32[]{:S(2)}, u32[]{:S(2)}) collective-permute-start(bf16[1,48,3584]{2,1,0:T(8,128)(2,1)S(1)} %fusion.39), channel_id=1, source_target_pairs={{0,4},{1,5},{2,6},{3,7},{4,0},{5,1},{6,2},{7,3},{8,12},{9,13},{10,... | collective-permute-start | bytes 1032200 | tf_op jit(solution)/shard_map/ppermute | solution.py:31
  442.9 31.3 %collective-permute-start.40 = (bf16[1,48,3584]{2,1,0:T(8,128)(2,1)S(1)}, bf16[1,48,3584]{2,1,0:T(8,128)(2,1)S(1)}, u32[]{:S(2)}, u32[]{:S(2)}) collective-permute-start(bf16[1,48,3584]{2,1,0:T(8,128)(2,1)S(1)} %copy-done.50), channel_id=1, source_target_pairs={{0,6},{1,7},{2,4},{3,5},{4,2},{5,3},{6,0},{7,1},{8,14},{9,15},{10,... | collective-permute-start | bytes 1032200 | tf_op jit(solution)/shard_map/ppermute | solution.py:31
  445.2 28.9 %collective-permute-start.43 = (f32[2,1024]{1,0:T(2,128)S(1)}, f32[2,1024]{1,0:T(2,128)S(1)}, u32[]{:S(2)}, u32[]{:S(2)}) collective-permute-start(f32[2,1024]{1,0:T(2,128)S(1)} %add.372), channel_id=1, source_target_pairs={{0,4},{1,5},{2,6},{3,7},{4,0},{5,1},{6,2},{7,3},{8,12},{9,13},{10,... | collective-permute-start | bytes 24584 | tf_op jit(solution)/shard_map/ppermute | solution.py:31
  446.6 30.4 %copy-start.15 = (bf16[2,3,96,1024]{3,2,1,0:T(8,128)(2,1)}, bf16[2,3,96,1024]{3,2,1,0:T(8,128)(2,1)S(1)}, u32[]{:S(2)}) copy-start(bf16[2,3,96,1024]{3,2,1,0:T(8,128)(2,1)S(1)} %pad_maximum_fusion.1.pair) | copy-start | bytes 3538948
  474.1 2.8 collective-permute-start.49
  474.2 20.2 %copy-start.1 = (bf16[384,1024]{1,0:T(8,128)(2,1)S(1)}, bf16[384,1024]{1,0:T(8,128)(2,1)}, u32[]{:S(2)}) copy-start(bf16[384,1024]{1,0:T(8,128)(2,1)} %param.37) | copy-start | bytes 2359300
  474.4 10.5 %collective-permute-start.48 = (bf16[1,48,3584]{2,1,0:T(8,128)(2,1)S(1)}, bf16[1,48,3584]{2,1,0:T(8,128)(2,1)S(1)}, u32[]{:S(2)}, u32[]{:S(2)}) collective-permute-start(bf16[1,48,3584]{2,1,0:T(8,128)(2,1)S(1)} %fusion.31), channel_id=1, source_target_pairs={{0,16},{8,24},{16,0},{24,8},{1,17},{9,25},{17,1},{25,9},{2,18},{10... | collective-permute-start | bytes 1032200 | tf_op jit(solution)/shard_map/ppermute | solution.py:31
  485.0 2.2 collective-permute-start.50
  (62 other events, 300.0 us)
Sparse Core Ops, SparseCore 0:
  11.0 162.1 all-gather.2

commit v2 on v1

--- a/solution.py
+++ b/solution.py
@@ -873,8 +873,7 @@
     rest_came, also_came = yield [
         (rest(1).astype(LOW), "chan", 1),
         (also(1).astype(LOW), "rows", 2),
-        later,
-    ]
+    ] + ([later] if meanwhile else [])
     from_y, from_x = held
     rest, also = rest(0), also(0)
     parts = {}
@@ -1292,9 +1291,10 @@
     fed.step()
     fed = Sums(clock, settled(fed.result))
     fed.step()
+    rest.step()
+    rest = Sums(clock, settled(rest.result))
     gains = gains.finish()
     rest.step()
-    rest = Sums(clock, settled(rest.result))
     fed.step()
     feed_sum = clock.tick(finish(jnp.stack([me, row_place]).astype(jnp.int32), *fed.result))
     pair, came = rest.finish()

time: 509 us -> 508 us (level)
  local copies, waits for them, and re-layouts: 26.4 us -> 19.7 us
    ppermute x43, waiting for transfers between devices: 148 us -> 142 us  [swapped(): lax.ppermute(value, axis, [(source, source ^ bits) for source in range(co...]
    unnamed x150 -> x136, local copies, waits for them, and re-layouts: 16.1 us -> 10.9 us
  transfers between devices with their start and end apart: 52 -> 52, of which waited for: 30 -> 29; matrix products, arithmetic and copies ran while one was open for 10% -> 9% of each run, Pallas kernels for 31% -> 31%
where the time goes in v2:
time: 508 us; the launch traced here: 499 us
  Pallas kernels  192 us (38%)
  waiting for transfers between devices  153 us (30%)
  starting transfers between devices  65.6 us (13%)
  other arithmetic  54.1 us (11%)
  local copies, waits for them, and re-layouts  19.7 us (4%)
  between operations  15.7 us (3%)
    ppermute x43, waiting for transfers between devices, swapped(): lax.ppermute(value, axis, [(source, source ^ bits) for source in range(co...  142 us
    pallas_call x2, Pallas kernels, mixer_back(): pl.pallas_call(functools.partial(mixer_back_kernel, rows, not so_far), gr...  50.4 us
    ppermute x43, starting transfers between devices, swapped(): lax.ppermute(value, axis, [(source, source ^ bits) for source in range(co...  48.9 us
    pallas_call x1, Pallas kernels, feed(): pl.pallas_call(functools.partial(feed_kernel, group), grid_spec=pltpu.Pre...  34.4 us
    pallas_call x2, Pallas kernels, feed_grads(): pl.pallas_call(functools.partial(feed_grads_kernel, parity, count), grid=...  21.3 us
    pallas_call x1, Pallas kernels, mixer_forward(): pl.pallas_call(mixer_forward_kernel, grid=(pairs,), in_specs=[whole(norme...  20 us
    ppermute x8, starting transfers between devices, moved_by(): lax.ppermute(value, axis, [(source, source + steps) for source in range(l...  16.6 us
    pallas_call x6, Pallas kernels, pack(): pl.pallas_call(functools.partial(pack_kernel, table, len(sources)), in_sp...  15.3 us
  transfers between devices with their start and end apart: 52, of which 29 were waited for; matrix products, arithmetic and copies ran while one was open for 9% of the time, Pallas kernels for 31%

profile of v2, /device:TPU:0, one launch (start us, length us, event | category | flops | bytes accessed | tf_op | source)
XLA Modules:
  0.0 499.5 jit_solution(3131052731168998272)
XLA Ops:
  11.7 3.1 collective-permute-start.1
  14.8 2.6 collective-permute-start.2
  17.4 3.6 collective-permute-start
  24.4 5.1 %collective-permute-done.2.refs_2_ = bf16[1,80,1024]{2,1,0:T(8,128)(2,1)S(1)} collective-permute-done((bf16[1,80,1024]{2,1,0:T(8,128)(2,1)S(1)}, bf16[1,80,1024]{2,1,0:T(8,128)(2,1)S(1)}, u32[]{:S(2)}, u32[]{:S(2)}) %collective-permute-start.2) | collective-permute-done | bytes 163872 | tf_op jit(solution)/shard_map/ppermute | solution.py:31
  29.5 7.8 %collective-permute-done.3.refs_3_ = bf16[1,80,1024]{2,1,0:T(8,128)(2,1)S(1)} collective-permute-done((bf16[1,80,1024]{2,1,0:T(8,128)(2,1)S(1)}, bf16[1,80,1024]{2,1,0:T(8,128)(2,1)S(1)}, u32[]{:S(2)}, u32[]{:S(2)}) %collective-permute-start.3) | collective-permute-done | bytes 163872 | tf_op jit(solution)/shard_map/ppermute | solution.py:31
  38.6 2.1 pack.6
  43.0 2.8 collective-permute-start.6
  48.5 12.0 %collective-permute-done.6.refs_2_ = bf16[1,96,1024]{2,1,0:T(8,128)(2,1)S(1)} collective-permute-done((bf16[1,96,1024]{2,1,0:T(8,128)(2,1)S(1)}, bf16[1,96,1024]{2,1,0:T(8,128)(2,1)S(1)}, u32[]{:S(2)}, u32[]{:S(2)}) %collective-permute-start.6) | collective-permute-done | bytes 196640 | tf_op jit(solution)/shard_map/ppermute | solution.py:31
  60.5 11.1 %collective-permute-done.7.refs_3_ = bf16[1,96,1024]{2,1,0:T(8,128)(2,1)S(1)} collective-permute-done((bf16[1,96,1024]{2,1,0:T(8,128)(2,1)S(1)}, bf16[1,96,1024]{2,1,0:T(8,128)(2,1)S(1)}, u32[]{:S(2)}, u32[]{:S(2)}) %collective-permute-start.7) | collective-permute-done | bytes 196640 | tf_op jit(solution)/shard_map/ppermute | solution.py:31
  72.5 2.5 pack.7
  75.1 2.3 pack.8
  79.3 2.1 collective-permute-done.9.refs_2_
  81.4 9.6 %collective-permute-done.8.refs_1_ = bf16[5,80,1024]{2,1,0:T(8,128)(2,1)S(1)} collective-permute-done((bf16[5,80,1024]{2,1,0:T(8,128)(2,1)S(1)}, bf16[5,80,1024]{2,1,0:T(8,128)(2,1)S(1)}, u32[]{:S(2)}, u32[]{:S(2)}) %collective-permute-start.8) | collective-permute-done | bytes 819232 | tf_op jit(solution)/shard_map/ppermute | solution.py:31
  91.0 7.4 %collective-permute-done.10.refs_1_ = bf16[5,96,1024]{2,1,0:T(8,128)(2,1)S(1)} collective-permute-done((bf16[5,96,1024]{2,1,0:T(8,128)(2,1)}, bf16[5,96,1024]{2,1,0:T(8,128)(2,1)S(1)}, u32[]{:S(2)}, u32[]{:S(2)}) %collective-permute-start.10) | collective-permute-done | bytes 983072 | tf_op jit(solution)/shard_map/ppermute | solution.py:31
  98.4 2.9 pack.10.refs_3_
  101.4 2.7 pack.9
  106.5 2.4 collective-permute-done.13.refs_4_
  110.0 6.1 %assemble.2 = (bf16[32,48,1024]{2,1,0:T(8,128)(2,1)}, bf16[32,32,1024]{2,1,0:T(8,128)(2,1)}) custom-call(s32[2]{0:T(128)} %pad_add_fusion.1.place, bf16[4,80,1024]{2,1,0:T(8,128)(2,1)} %pad_maximum_fusion.4.refs_0_, bf16[4,80,1024]{2,1,0:T(8,128)(2,1)} %get-tuple-element.331.refs_1_, bf16[4,80,1024]{2,1,0:T(8,128)(2,1)} %copy-done.43, ...), custom_call_target="tpu_custom_call" | custom-call | flops 55000000 | bytes 175000 | tf_op jit(solution)/shard_map/assemble/pallas_call | solution.py:1092
  118.6 20.0 %mixer_forward.1 = (f32[528,1536]{1,0:T(8,128)}, f32[512,1536]{1,0:T(8,128)}, f32[512,1536]{1,0:T(8,128)}, f32[512,1536]{1,0:T(8,128)}, f32[512,1536]{1,0:T(8,12...) custom-call(bf16[528,1024]{1,0:T(8,128)(2,1)} %multiply_convert_fusion.normed, bf16[1536,1024]{1,0:T(8,128)(2,1)} %bitcast.196, ...), custom_call_target="tpu_custom_call" | custom-call | flops 286000000 | bytes 910000 | tf_op jit(solution)/shard_map/mixer_forward/pallas_call | solution.py:213
  140.4 9.5 %collective-permute-done.11.refs_1_ = bf16[5,96,1024]{2,1,0:T(8,128)(2,1)S(1)} collective-permute-done((bf16[5,96,1024]{2,1,0:T(8,128)(2,1)}, bf16[5,96,1024]{2,1,0:T(8,128)(2,1)S(1)}, u32[]{:S(2)}, u32[]{:S(2)}) %collective-permute-start.11) | collective-permute-done | bytes 983072 | tf_op jit(solution)/shard_map/ppermute | solution.py:31
  150.8 2.8 pack.11.refs_3_
  155.7 1.8 collective-permute-done.15
  158.8 4.6 collective-permute-start.17
  165.0 6.9 %assemble.3 = (bf16[32,48,1024]{2,1,0:T(8,128)(2,1)}, bf16[32,48,1024]{2,1,0:T(8,128)(2,1)}) custom-call(s32[2]{0:T(128)} %pad_add_fusion.1.place, bf16[4,96,1024]{2,1,0:T(8,128)(2,1)} %pad_maximum_fusion.2.refs_0_, bf16[4,96,1024]{2,1,0:T(8,128)(2,1)} %get-tuple-element.340.refs_1_, bf16[4,96,1024]{2,1,0:T(8,128)(2,1)} %collective-permute-done.12.refs_2_, ...), custom_call_target="tpu_custom_call" | custom-call | flops 55000000 | bytes 175000 | tf_op jit(solution)/shard_map/assemble/pallas_call | solution.py:1092
  171.9 8.5 %gelu_branch.1 = (f32[512,1536]{1,0:T(8,128)}, f32[512,1536]{1,0:T(8,128)}) custom-call(bf16[528,1024]{1,0:T(8,128)(2,1)} %multiply_convert_fusion.normed, bf16[1536,1024]{1,0:T(8,128)(2,1)} %bitcast.199, f32[16,1536]{1,0:T(8,128)} %select_select_fusion.vec), custom_call_target="tpu_custom_call" | custom-call | flops 88000000 | bytes 280000 | tf_op jit(solution)/shard_map/gelu_branch/pallas_call | solution.py:252
  181.0 7.9 %mixer_out.1 = (bf16[512,1536]{1,0:T(8,128)(2,1)}, f32[512,1024]{1,0:T(8,128)}, bf16[512,1024]{1,0:T(8,128)(2,1)}) custom-call(f32[512,1536]{1,0:T(8,128)} %get-tuple-element.379.active.active_in, f32[512,1536]{1,0:T(8,128)} %get-tuple-element.359.h, f32[512,1536]{1,0:T(8,128)} %get-tuple-element.358.f, f32[1,1536]{1,0:T(1,128)} %broadcast_select_fusion.3.state, ...), custom_call_target="tpu_custom_call" | custom-call | flops 99000000 | bytes 315000 | tf_op jit(solution)/shard_map/mixer_out/pallas_call | solution.py:288
  189.0 34.4 %feed.1 = (f32[512,1024]{1,0:T(8,128)}, f32[512,1024]{1,0:T(8,128)}, bf16[8,3,192,512]{3,2,1,0:T(8,128)(2,1)}, bf16[8,3,192,512]{3,2,1,0:T(8,128)(2,1)}) custom-call(s32[2]{0:T(128)} %pad_add_fusion.1.place, bf16[512,1024]{1,0:T(8,128)(2,1)} %get-tuple-element.394.normed, bf16[512,1024]{1,0:T(8,128)(2,1)} %copy-done.17, ...), custom_call_target="tpu_custom_call" | custom-call | flops 374000000 | bytes 1190000 | tf_op jit(solution)/shard_map/feed/pallas_call | solution.py:413
  224.0 12.3 %middle_back.1 = (f32[512,1024]{1,0:T(8,128)}, bf16[512,1024]{1,0:T(8,128)(2,1)}, f32[512,1536]{1,0:T(8,128)}, bf16[512,1536]{1,0:T(8,128)(2,1)}, f32[8,1024]{1,...) custom-call(f32[512,1024]{1,0:T(8,128)} %get-tuple-element.395.out_in.middle, f32[512,1024]{1,0:T(8,128)} %get-tuple-element.406.grad, ...), custom_call_target="tpu_custom_call" | custom-call | flops 143000000 | bytes 455000 | tf_op jit(solution)/shard_map/middle_back/pallas_call | solution.py:532
  237.1 2.2 collective-permute-start.20
  240.3 11.6 %feed_grads.3 = (bf16[2,3,2,96,1024]{4,3,2,1,0:T(8,128)(2,1)}, bf16[2,3,2,96,1024]{4,3,2,1,0:T(8,128)(2,1)}) custom-call(bf16[8,3,192,512]{3,2,1,0:T(8,128)(2,1)} %get-tuple-element.427.mine, bf16[8,3,192,512]{3,2,1,0:T(8,128)(2,1)} %collective-permute-done.21.theirs, bf16[512,1024]{1,0:T(8,128)(2,1)} %get-tuple-element.394.normed, ...), custom_call_target="tpu_custom_call" | custom-call | flops 22000001024 | bytes 70000000 | tf_op jit(solution)/shard_map/feed_grads/pallas_call | solution.py:475
  251.9 9.7 %feed_grads.2 = (bf16[4,3,96,1024]{3,2,1,0:T(8,128)(2,1)}, bf16[4,3,96,1024]{3,2,1,0:T(8,128)(2,1)}) custom-call(bf16[8,3,192,512]{3,2,1,0:T(8,128)(2,1)} %get-tuple-element.427.mine, bf16[8,3,192,512]{3,2,1,0:T(8,128)(2,1)} %collective-permute-done.21.theirs, bf16[512,1024]{1,0:T(8,128)(2,1)} %get-tuple-element.394.normed, bf16[512,1024]{1,0:T(8,128)(2,1)} %copy-done.17, ...), custom_call_target="tpu_custom_call" | custom-call | flops 22000001024 | bytes 70000000 | tf_op jit(solution)/shard_map/feed_grads/pallas_call | solution.py:475
  268.8 2.2 collective-permute-done.24
  271.0 3.4 collective-permute-done.25
  275.0 33.9 %mixer_back.2 = (bf16[8,1,2,48,3584]{4,3,2,1,0:T(8,128)(2,1)}, bf16[8,1,2,48,3584]{4,3,2,1,0:T(8,128)(2,1)}, f32[528,1024]{1,0:T(8,128)}) custom-call(s32[3]{0:T(128)} %pad_add_fusion.2.place, f32[512,1536]{1,0:T(8,128)} %get-tuple-element.417.state_grad, f32[512,1536]{1,0:T(8,128)} %get-tuple-element.418.r_in, f32[512,1536]{1,0:T(8,128)} %get-tuple-element.419.i_in, ...), custom_call_target="tpu_custom_call" | custom-call | flops 495000000 | bytes 1575000 | tf_op jit(solution)/shard_map/mixer_back/pallas_call | solution.py:714
  308.9 6.4 %collective-permute-done.27 = bf16[2,3,2,96,1024]{4,3,1,2,0:T(8,128)(2,1)} collective-permute-done((bf16[2,3,2,96,1024]{4,3,1,2,0:T(8,128)(2,1)S(1)}, bf16[2,3,2,96,1024]{4,3,1,2,0:T(8,128)(2,1)}, u32[]{:S(2)}, u32[]{:S(2)}) %collective-permute-start.27) | collective-permute-done | bytes 2359328 | tf_op jit(solution)/shard_map/ppermute | solution.py:31
  315.5 4.5 convert_add_fusion.1
  320.0 4.1 convert_add_fusion
  326.3 16.5 %mixer_back.3 = (bf16[8,1,2,48,3584]{4,3,2,1,0:T(8,128)(2,1)}, bf16[8,1,2,48,3584]{4,3,2,1,0:T(8,128)(2,1)}, f32[528,1024]{1,0:T(8,128)}) custom-call(s32[3]{0:T(128)} %pad_add_fusion.2.place, f32[512,1536]{1,0:T(8,128)} %get-tuple-element.417.state_grad, f32[512,1536]{1,0:T(8,128)} %get-tuple-element.418.r_in, ...), custom_call_target="tpu_custom_call", output_to_operand_aliasing={{0}: (21, {}), {1}: (22, {})} | custom-call | flops 165000000 | bytes 525000 | tf_op jit(solution)/shard_map/mixer_back/pallas_call | solution.py:714
  342.8 8.2 %collective-permute-done.28 = bf16[2,3,96,1024]{3,2,1,0:T(8,128)(2,1)} collective-permute-done((bf16[2,3,96,1024]{3,2,1,0:T(8,128)(2,1)S(1)}, bf16[2,3,96,1024]{3,2,1,0:T(8,128)(2,1)}, u32[]{:S(2)}, u32[]{:S(2)}) %collective-permute-start.28) | collective-permute-done | bytes 1179680 | tf_op jit(solution)/shard_map/ppermute | solution.py:31
  354.9 4.0 collective-permute-done.30
  358.9 3.4 multiply_reduce_fusion.1
  364.1 2.7 fusion.2
  366.9 2.7 fusion.1
  373.3 2.1 add_bitcast_fusion
  375.5 3.2 add_bitcast_fusion.1
  379.0 3.4 fusion.35
  382.4 2.2 fusion.34
  384.7 1.7 multiply_subtract_fusion
  386.4 4.4 collective-permute-start.43
  390.8 11.6 %collective-permute-done.34 = bf16[2,2,1,48,3584]{4,3,2,1,0:T(8,128)(2,1)S(1)} collective-permute-done((bf16[2,2,1,48,3584]{4,3,2,1,0:T(8,128)(2,1)}, bf16[2,2,1,48,3584]{4,3,2,1,0:T(8,128)(2,1)S(1)}, u32[]{:S(2)}, u32[]{:S(2)}) %collective-permute-start.34) | collective-permute-done | bytes 1376288 | tf_op jit(solution)/shard_map/ppermute | solution.py:31
  411.1 1.7 convert_add_fusion.2
  412.8 9.3 %collective-permute-done.36 = bf16[2,1,48,3584]{3,2,1,0:T(8,128)(2,1)S(1)} collective-permute-done((bf16[2,1,48,3584]{3,2,1,0:T(8,128)(2,1)}, bf16[2,1,48,3584]{3,2,1,0:T(8,128)(2,1)S(1)}, u32[]{:S(2)}, u32[]{:S(2)}) %collective-permute-start.36) | collective-permute-done | bytes 688160 | tf_op jit(solution)/shard_map/ppermute | solution.py:31
  423.6 2.1 fusion.40
  427.0 3.2 collective-permute-done.44
  430.2 3.6 collective-permute-done.45
  433.9 2.1 fusion.11
  436.6 6.6 %collective-permute-start.38 = (bf16[1,48,3584]{2,1,0:T(8,128)(2,1)S(1)}, bf16[1,48,3584]{2,1,0:T(8,128)(2,1)S(1)}, u32[]{:S(2)}, u32[]{:S(2)}) collective-permute-start(bf16[1,48,3584]{2,1,0:T(8,128)(2,1)S(1)} %copy-done.46), channel_id=1, source_target_pairs={{0,2},{1,3},{2,0},{3,1},{4,6},{5,7},{6,4},{7,5},{8,10},{9,11},{10,... | collective-permute-start | bytes 1032200 | tf_op jit(solution)/shard_map/ppermute | solution.py:31
  443.2 2.4 collective-permute-start.40
  447.1 7.8 %collective-permute-done.38 = bf16[1,48,3584]{2,1,0:T(8,128)(2,1)S(1)} collective-permute-done((bf16[1,48,3584]{2,1,0:T(8,128)(2,1)S(1)}, bf16[1,48,3584]{2,1,0:T(8,128)(2,1)S(1)}, u32[]{:S(2)}, u32[]{:S(2)}) %collective-permute-start.38) | collective-permute-done | bytes 344096 | tf_op jit(solution)/shard_map/ppermute | solution.py:31
  454.9 15.0 %collective-permute-done.39 = bf16[1,48,3584]{2,1,0:T(8,128)(2,1)S(1)} collective-permute-done((bf16[1,48,3584]{2,1,0:T(8,128)(2,1)S(1)}, bf16[1,48,3584]{2,1,0:T(8,128)(2,1)S(1)}, u32[]{:S(2)}, u32[]{:S(2)}) %collective-permute-start.39) | collective-permute-done | bytes 344096 | tf_op jit(solution)/shard_map/ppermute | solution.py:31
  470.1 1.7 collective-permute-start.47
  471.8 4.8 collective-permute-start.48
  480.1 4.9 finish.1
  485.9 3.6 finish_rest.1
  (301 shorter events, 74.0 us)
Async XLA Ops:
  7.2 181.7 %all-gather.3.cloned.1.call-start = ((), (), s32[]{:S(2)}) async-start(), calls=%async_computation | async-start | bytes 19464192 | tf_op jit(solution)/shard_map/all_gather | solution.py:1189
  11.7 25.5 %collective-permute-start.1 = (bf16[2,80,1024]{2,1,0:T(8,128)(2,1)S(1)}, bf16[2,80,1024]{2,1,0:T(8,128)(2,1)S(1)}, u32[]{:S(2)}, u32[]{:S(2)}) collective-permute-start(bf16[2,80,1024]{2,1,0:T(8,128)(2,1)S(1)} %pad_maximum_fusion.7), channel_id=1, source_target_pairs={{0,2},{1,3},{2,0},{3,1},{4,6},{5,7},{6,4},{7,5},{8,10},{9,11},{10,... | collective-permute-start | bytes 983048 | tf_op jit(solution)/shard_map/ppermute | solution.py:31
  14.8 14.7 %collective-permute-start.2 = (bf16[1,80,1024]{2,1,0:T(8,128)(2,1)S(1)}, bf16[1,80,1024]{2,1,0:T(8,128)(2,1)S(1)}, u32[]{:S(2)}, u32[]{:S(2)}) collective-permute-start(bf16[1,80,1024]{2,1,0:T(8,128)(2,1)S(1)} %get-tuple-element.308), channel_id=1, source_target_pairs={{0,4},{1,5},{2,6},{3,7},{4,0},{5,1},{6,2},{7,3},{8,12},{9,13},{10,... | collective-permute-start | bytes 491528 | tf_op jit(solution)/shard_map/ppermute | solution.py:31
  17.4 19.9 %collective-permute-start.3 = (bf16[1,80,1024]{2,1,0:T(8,128)(2,1)S(1)}, bf16[1,80,1024]{2,1,0:T(8,128)(2,1)S(1)}, u32[]{:S(2)}, u32[]{:S(2)}) collective-permute-start(bf16[1,80,1024]{2,1,0:T(8,128)(2,1)S(1)} %get-tuple-element.308), channel_id=1, source_target_pairs={{0,6},{1,7},{2,4},{3,5},{4,2},{5,3},{6,0},{7,1},{8,14},{9,15},{10,... | collective-permute-start | bytes 491528 | tf_op jit(solution)/shard_map/ppermute | solution.py:31
  17.4 24.9 %collective-permute-start = (f32[3,1024]{1,0:T(4,128)S(1)}, f32[3,1024]{1,0:T(4,128)S(1)}, u32[]{:S(2)}, u32[]{:S(2)}) collective-permute-start(f32[3,1024]{1,0:T(4,128)S(1)} %slice.283), channel_id=1, source_target_pairs={{0,1},{1,2},{2,3},{3,4},{4,5},{5,6},{6,7},{8,9},{9,10},{10,11},{11... | collective-permute-start | bytes 36872 | tf_op jit(solution)/shard_map/ppermute | solution.py:26
  40.7 30.9 %collective-permute-start.4 = (bf16[5,80,1024]{2,1,0:T(8,128)(2,1)}, bf16[5,80,1024]{2,1,0:T(8,128)(2,1)S(1)}, u32[]{:S(2)}, u32[]{:S(2)}) collective-permute-start(bf16[5,80,1024]{2,1,0:T(8,128)(2,1)} %pack.6), channel_id=1, source_target_pairs={{0,1},{1,0},{2,3},{3,2},{4,5},{5,4},{6,7},{7,6},{8,9},{9,8},{10,11... | collective-permute-start | bytes 2457608 | tf_op jit(solution)/shard_map/ppermute | solution.py:31
  42.5 29.0 %collective-permute-start.5 = (bf16[2,96,1024]{2,1,0:T(8,128)(2,1)S(1)}, bf16[2,96,1024]{2,1,0:T(8,128)(2,1)S(1)}, u32[]{:S(2)}, u32[]{:S(2)}) collective-permute-start(bf16[2,96,1024]{2,1,0:T(8,128)(2,1)S(1)} %pad_maximum_fusion.6), channel_id=1, source_target_pairs={{0,2},{1,3},{2,0},{3,1},{4,6},{5,7},{6,4},{7,5},{8,10},{9,11},{10,... | collective-permute-start | bytes 1179656 | tf_op jit(solution)/shard_map/ppermute | solution.py:31
  43.0 17.5 %collective-permute-start.6 = (bf16[1,96,1024]{2,1,0:T(8,128)(2,1)S(1)}, bf16[1,96,1024]{2,1,0:T(8,128)(2,1)S(1)}, u32[]{:S(2)}, u32[]{:S(2)}) collective-permute-start(bf16[1,96,1024]{2,1,0:T(8,128)(2,1)S(1)} %get-tuple-element.321), channel_id=1, source_target_pairs={{0,4},{1,5},{2,6},{3,7},{4,0},{5,1},{6,2},{7,3},{8,12},{9,13},{10,... | collective-permute-start | bytes 589832 | tf_op jit(solution)/shard_map/ppermute | solution.py:31
  45.8 25.8 %collective-permute-start.7 = (bf16[1,96,1024]{2,1,0:T(8,128)(2,1)S(1)}, bf16[1,96,1024]{2,1,0:T(8,128)(2,1)S(1)}, u32[]{:S(2)}, u32[]{:S(2)}) collective-permute-start(bf16[1,96,1024]{2,1,0:T(8,128)(2,1)S(1)} %get-tuple-element.321), channel_id=1, source_target_pairs={{0,6},{1,7},{2,4},{3,5},{4,2},{5,3},{6,0},{7,1},{8,14},{9,15},{10,... | collective-permute-start | bytes 589832 | tf_op jit(solution)/shard_map/ppermute | solution.py:31
  77.4 26.8 %copy-start.56 = (s32[4096]{0:T(1024)S(1)}, s32[4096]{0:T(1024)}, u32[]{:S(2)}) copy-start(s32[4096]{0:T(1024)} %param.21) | copy-start | bytes 49156
  77.4 21.1 %collective-permute-start.10 = (bf16[5,96,1024]{2,1,0:T(8,128)(2,1)}, bf16[5,96,1024]{2,1,0:T(8,128)(2,1)S(1)}, u32[]{:S(2)}, u32[]{:S(2)}) collective-permute-start(bf16[5,96,1024]{2,1,0:T(8,128)(2,1)} %pack.8), channel_id=1, source_target_pairs={{0,1},{1,0},{2,3},{3,2},{4,5},{5,4},{6,7},{7,6},{8,9},{9,8},{10,11... | collective-permute-start | bytes 2949128 | tf_op jit(solution)/shard_map/ppermute | solution.py:31
  78.2 12.8 %collective-permute-start.8 = (bf16[5,80,1024]{2,1,0:T(8,128)(2,1)S(1)}, bf16[5,80,1024]{2,1,0:T(8,128)(2,1)S(1)}, u32[]{:S(2)}, u32[]{:S(2)}) collective-permute-start(bf16[5,80,1024]{2,1,0:T(8,128)(2,1)S(1)} %copy-done.32), channel_id=1, source_target_pairs={{0,16},{8,24},{16,0},{24,8},{1,17},{9,25},{17,1},{25,9},{2,18},{10... | collective-permute-start | bytes 2457608 | tf_op jit(solution)/shard_map/ppermute | solution.py:31
  79.3 2.1 collective-permute-start.9
  81.4 27.4 %copy-start.43 = (bf16[4,80,1024]{2,1,0:T(8,128)(2,1)}, bf16[4,80,1024]{2,1,0:T(8,128)(2,1)S(1)}, u32[]{:S(2)}) copy-start(bf16[4,80,1024]{2,1,0:T(8,128)(2,1)S(1)} %collective-permute-done.9.refs_2_) | copy-start | bytes 1966084
  104.1 4.7 collective-permute-start.13
  106.0 43.9 %collective-permute-start.11 = (bf16[5,96,1024]{2,1,0:T(8,128)(2,1)}, bf16[5,96,1024]{2,1,0:T(8,128)(2,1)S(1)}, u32[]{:S(2)}, u32[]{:S(2)}) collective-permute-start(bf16[5,96,1024]{2,1,0:T(8,128)(2,1)} %get-tuple-element.339.refs_0_), channel_id=1, source_target_pairs={{0,16},{8,24},{16,0},{24,8},{1,17},{9,25},{17,1},{25,9},{2,18},{10... | collective-permute-start | bytes 2949128 | tf_op jit(solution)/shard_map/ppermute | solution.py:31
  106.0 34.4 %collective-permute-start.12 = (bf16[4,96,1024]{2,1,0:T(8,128)(2,1)}, bf16[4,96,1024]{2,1,0:T(8,128)(2,1)}, u32[]{:S(2)}, u32[]{:S(2)}) collective-permute-start(bf16[4,96,1024]{2,1,0:T(8,128)(2,1)} %get-tuple-element.340.refs_1_), channel_id=1, source_target_pairs={{0,8},{8,0},{16,24},{24,16},{1,9},{9,1},{17,25},{25,17},{2,10},{10... | collective-permute-start | bytes 2359304 | tf_op jit(solution)/shard_map/ppermute | solution.py:31
  153.6 11.3 %collective-permute-start.14 = (bf16[10,96,1024]{2,1,0:T(8,128)(2,1)}, bf16[10,96,1024]{2,1,0:T(8,128)(2,1)}, u32[]{:S(2)}, u32[]{:S(2)}) collective-permute-start(bf16[10,96,1024]{2,1,0:T(8,128)(2,1)} %pack.11.refs_3_), channel_id=1, source_target_pairs={{0,8},{8,0},{16,24},{24,16},{1,9},{9,1},{17,25},{25,17},{2,10},{10... | collective-permute-start | bytes 5898248 | tf_op jit(solution)/shard_map/ppermute | solution.py:31
  153.7 3.8 collective-permute-start.15
  155.4 33.5 %collective-permute-start.19 = (bf16[512,1024]{1,0:T(8,128)(2,1)S(1)}, bf16[512,1024]{1,0:T(8,128)(2,1)S(1)}, u32[]{:S(2)}, u32[]{:S(2)}) collective-permute-start(bf16[512,1024]{1,0:T(8,128)(2,1)S(1)} %convert_element_type.424.cot), channel_id=1, source_target_pairs={{0,8},{8,0},{16,24},{24,16},{1,9},{9,1},{17,25},{25,17},{2,10},{10... | collective-permute-start | bytes 3145736 | tf_op jit(solution)/shard_map/ppermute | solution.py:31
  157.5 22.8 %collective-permute-start.16 = (f32[2,1536]{1,0:T(2,128)S(1)}, f32[2,1536]{1,0:T(2,128)S(1)}, u32[]{:S(2)}, u32[]{:S(2)}) collective-permute-start(f32[2,1536]{1,0:T(2,128)S(1)} %pad_maximum_fusion.10), channel_id=1, source_target_pairs={{0,2},{1,3},{2,4},{3,5},{4,6},{5,7},{8,10},{9,11},{10,12},{11,13},... | collective-permute-start | bytes 36872 | tf_op jit(solution)/shard_map/ppermute | solution.py:26
  158.8 21.5 %collective-permute-start.17 = (f32[2,1536]{1,0:T(2,128)S(1)}, f32[2,1536]{1,0:T(2,128)S(1)}, u32[]{:S(2)}, u32[]{:S(2)}) collective-permute-start(f32[2,1536]{1,0:T(2,128)S(1)} %pad_maximum_fusion.10), channel_id=1, source_target_pairs={{0,4},{1,5},{2,6},{3,7},{8,12},{9,13},{10,14},{11,15},{16,20},{17,... | collective-permute-start | bytes 36872 | tf_op jit(solution)/shard_map/ppermute | solution.py:26
  163.5 16.9 %collective-permute-start.18 = (f32[2,1536]{1,0:T(2,128)S(1)}, f32[2,1536]{1,0:T(2,128)S(1)}, u32[]{:S(2)}, u32[]{:S(2)}) collective-permute-start(f32[2,1536]{1,0:T(2,128)S(1)} %pad_maximum_fusion.10), channel_id=1, source_target_pairs={{0,6},{1,7},{8,14},{9,15},{16,22},{17,23},{24,30},{25,31}} | collective-permute-start | bytes 36872 | tf_op jit(solution)/shard_map/ppermute | solution.py:26
  188.9 34.5 %copy-start.65 = (bf16[512,1024]{1,0:T(8,128)(2,1)}, bf16[512,1024]{1,0:T(8,128)(2,1)S(1)}, u32[]{:S(2)}) copy-start(bf16[512,1024]{1,0:T(8,128)(2,1)S(1)} %collective-permute-done.19.cot_too) | copy-start | bytes 3145732
  189.0 34.5 %copy-start.29 = (bf16[512,1024]{1,0:T(8,128)(2,1)S(1)}, bf16[512,1024]{1,0:T(8,128)(2,1)}, u32[]{:S(2)}) copy-start(bf16[512,1024]{1,0:T(8,128)(2,1)} %get-tuple-element.394.normed) | copy-start | bytes 3145732
  223.4 15.9 %collective-permute-start.21 = (bf16[8,3,192,512]{3,2,1,0:T(8,128)(2,1)}, bf16[8,3,192,512]{3,2,1,0:T(8,128)(2,1)}, u32[]{:S(2)}, u32[]{:S(2)}) collective-permute-start(bf16[8,3,192,512]{3,2,1,0:T(8,128)(2,1)} %get-tuple-element.428), channel_id=1, source_target_pairs={{0,8},{8,0},{16,24},{24,16},{1,9},{9,1},{17,25},{25,17},{2,10},{10... | collective-permute-start | bytes 14155784 | tf_op jit(solution)/shard_map/ppermute | solution.py:31
  223.5 15.9 %collective-permute-start.22 = (bf16[512,1024]{1,0:T(8,128)(2,1)S(1)}, bf16[512,1024]{1,0:T(8,128)(2,1)S(1)}, u32[]{:S(2)}, u32[]{:S(2)}) collective-permute-start(bf16[512,1024]{1,0:T(8,128)(2,1)S(1)} %copy-done.29), channel_id=1, source_target_pairs={{0,8},{8,0},{16,24},{24,16},{1,9},{9,1},{17,25},{25,17},{2,10},{10... | collective-permute-start | bytes 3145736 | tf_op jit(solution)/shard_map/ppermute | solution.py:31
  237.1 24.5 %collective-permute-start.20 = (f32[2,1536]{1,0:T(2,128)S(1)}, f32[2,1536]{1,0:T(2,128)S(1)}, u32[]{:S(2)}, u32[]{:S(2)}) collective-permute-start(f32[2,1536]{1,0:T(2,128)S(1)} %pad_maximum_fusion.8), channel_id=1, source_target_pairs={{0,1},{1,0},{2,3},{3,2},{4,5},{5,4},{6,7},{7,6},{8,9},{9,8},{10,11... | collective-permute-start | bytes 36872 | tf_op jit(solution)/shard_map/ppermute | solution.py:31
  262.1 53.1 %collective-permute-start.27 = (bf16[2,3,2,96,1024]{4,3,1,2,0:T(8,128)(2,1)S(1)}, bf16[2,3,2,96,1024]{4,3,1,2,0:T(8,128)(2,1)}, u32[]{:S(2)}, u32[]{:S(2)}) collective-permute-start(bf16[2,3,2,96,1024]{4,3,1,2,0:T(8,128)(2,1)S(1)} %copy.105), channel_id=1, source_target_pairs={{0,1},{1,0},{2,3},{3,2},{4,5},{5,4},{6,7},{7,6},{8,9},{9,8},{10,11... | collective-permute-start | bytes 7077896 | tf_op jit(solution)/shard_map/ppermute | solution.py:31
  262.2 53.3 %collective-permute-start.26 = (bf16[2,2,3,96,1024]{4,3,2,1,0:T(8,128)(2,1)}, bf16[2,2,3,96,1024]{4,3,2,1,0:T(8,128)(2,1)}, u32[]{:S(2)}, u32[]{:S(2)}) collective-permute-start(bf16[2,2,3,96,1024]{4,3,2,1,0:T(8,128)(2,1)} %bitcast.24), channel_id=1, source_target_pairs={{0,16},{8,24},{16,0},{24,8},{1,17},{9,25},{17,1},{25,9},{2,18},{10... | collective-permute-start | bytes 7077896 | tf_op jit(solution)/shard_map/ppermute | solution.py:31
  263.2 5.6 %collective-permute-start.23 = (f32[2,1536]{1,0:T(2,128)S(1)}, f32[2,1536]{1,0:T(2,128)S(1)}, u32[]{:S(2)}, u32[]{:S(2)}) collective-permute-start(f32[2,1536]{1,0:T(2,128)S(1)} %pad_maximum_fusion.11), channel_id=1, source_target_pairs={{2,0},{3,1},{4,2},{5,3},{6,4},{7,5},{10,8},{11,9},{12,10},{13,11},... | collective-permute-start | bytes 36872 | tf_op jit(solution)/shard_map/ppermute | solution.py:26
  264.5 6.5 %collective-permute-start.24 = (f32[2,1536]{1,0:T(2,128)S(1)}, f32[2,1536]{1,0:T(2,128)S(1)}, u32[]{:S(2)}, u32[]{:S(2)}) collective-permute-start(f32[2,1536]{1,0:T(2,128)S(1)} %pad_maximum_fusion.11), channel_id=1, source_target_pairs={{4,0},{5,1},{6,2},{7,3},{12,8},{13,9},{14,10},{15,11},{20,16},{21,... | collective-permute-start | bytes 36872 | tf_op jit(solution)/shard_map/ppermute | solution.py:26
  265.8 8.6 %collective-permute-start.25 = (f32[2,1536]{1,0:T(2,128)S(1)}, f32[2,1536]{1,0:T(2,128)S(1)}, u32[]{:S(2)}, u32[]{:S(2)}) collective-permute-start(f32[2,1536]{1,0:T(2,128)S(1)} %pad_maximum_fusion.11), channel_id=1, source_target_pairs={{6,0},{7,1},{14,8},{15,9},{22,16},{23,17},{30,24},{31,25}} | collective-permute-start | bytes 36872 | tf_op jit(solution)/shard_map/ppermute | solution.py:26
  275.0 40.5 %copy-start.21 = (bf16[2,3,2,96,1024]{4,3,2,1,0:T(8,128)(2,1)S(1)}, bf16[2,3,2,96,1024]{4,3,2,1,0:T(8,128)(2,1)}, u32[]{:S(2)}) copy-start(bf16[2,3,2,96,1024]{4,3,2,1,0:T(8,128)(2,1)} %get-tuple-element.466) | copy-start | bytes 7077892
  324.1 28.2 %copy-start.3 = (f32[512,1024]{1,0:T(8,128)S(1)}, f32[512,1024]{1,0:T(8,128)}, u32[]{:S(2)}) copy-start(f32[512,1024]{1,0:T(8,128)} %tokens.1) | copy-start | bytes 6291460
  324.1 26.9 %collective-permute-start.28 = (bf16[2,3,96,1024]{3,2,1,0:T(8,128)(2,1)S(1)}, bf16[2,3,96,1024]{3,2,1,0:T(8,128)(2,1)}, u32[]{:S(2)}, u32[]{:S(2)}) collective-permute-start(bf16[2,3,96,1024]{3,2,1,0:T(8,128)(2,1)S(1)} %get-tuple-element.479), channel_id=1, source_target_pairs={{0,1},{1,0},{2,3},{3,2},{4,5},{5,4},{6,7},{7,6},{8,9},{9,8},{10,11... | collective-permute-start | bytes 3538952 | tf_op jit(solution)/shard_map/ppermute | solution.py:31
  325.8 26.5 %collective-permute-start.29 = (bf16[2,3,96,1024]{3,2,1,0:T(8,128)(2,1)}, bf16[2,3,96,1024]{3,2,1,0:T(8,128)(2,1)}, u32[]{:S(2)}, u32[]{:S(2)}) collective-permute-start(bf16[2,3,96,1024]{3,2,1,0:T(8,128)(2,1)} %get-tuple-element.480), channel_id=1, source_target_pairs={{0,16},{8,24},{16,0},{24,8},{1,17},{9,25},{17,1},{25,9},{2,18},{10... | collective-permute-start | bytes 3538952 | tf_op jit(solution)/shard_map/ppermute | solution.py:31
  352.3 11.8 %collective-permute-start.33 = (bf16[8,1,2,48,3584]{4,3,2,1,0:T(8,128)(2,1)}, bf16[8,1,2,48,3584]{4,3,2,1,0:T(8,128)(2,1)}, u32[]{:S(2)}, u32[]{:S(2)}) collective-permute-start(bf16[8,1,2,48,3584]{4,3,2,1,0:T(8,128)(2,1)} %get-tuple-element.497), channel_id=1, source_target_pairs={{0,8},{8,0},{16,24},{24,16},{1,9},{9,1},{17,25},{25,17},{2,10},{10... | collective-permute-start | bytes 16515080 | tf_op jit(solution)/shard_map/ppermute | solution.py:31
  353.3 5.6 %collective-permute-start.30 = (f32[3,1024]{1,0:T(4,128)S(1)}, f32[3,1024]{1,0:T(4,128)S(1)}, u32[]{:S(2)}, u32[]{:S(2)}) collective-permute-start(f32[3,1024]{1,0:T(4,128)S(1)} %slice.320), channel_id=1, source_target_pairs={{1,0},{2,1},{3,2},{4,3},{5,4},{6,5},{7,6},{9,8},{10,9},{11,10},{12... | collective-permute-start | bytes 36872 | tf_op jit(solution)/shard_map/ppermute | solution.py:26
  362.3 1.2 collective-permute-start.31
  363.6 21.1 %collective-permute-start.32 = (f32[2,1024]{1,0:T(2,128)S(1)}, f32[2,1024]{1,0:T(2,128)S(1)}, u32[]{:S(2)}, u32[]{:S(2)}) collective-permute-start(f32[2,1024]{1,0:T(2,128)S(1)} %fusion.49), channel_id=1, source_target_pairs={{0,16},{8,24},{16,0},{24,8},{1,17},{9,25},{17,1},{25,9},{2,18},{10... | collective-permute-start | bytes 24584 | tf_op jit(solution)/shard_map/ppermute | solution.py:31
  370.2 32.2 %collective-permute-start.34 = (bf16[2,2,1,48,3584]{4,3,2,1,0:T(8,128)(2,1)}, bf16[2,2,1,48,3584]{4,3,2,1,0:T(8,128)(2,1)S(1)}, u32[]{:S(2)}, u32[]{:S(2)}) collective-permute-start(bf16[2,2,1,48,3584]{4,3,2,1,0:T(8,128)(2,1)} %fusion.1), channel_id=1, source_target_pairs={{0,16},{8,24},{16,0},{24,8},{1,17},{9,25},{17,1},{25,9},{2,18},{10... | collective-permute-start | bytes 4128776 | tf_op jit(solution)/shard_map/ppermute | solution.py:31
  371.8 31.9 %collective-permute-start.35 = (bf16[2,1,2,48,3584]{4,3,2,1,0:T(8,128)(2,1)}, bf16[2,1,2,48,3584]{4,3,2,1,0:T(8,128)(2,1)S(1)}, u32[]{:S(2)}, u32[]{:S(2)}) collective-permute-start(bf16[2,1,2,48,3584]{4,3,2,1,0:T(8,128)(2,1)} %fusion.2), channel_id=1, source_target_pairs={{0,1},{1,0},{2,3},{3,2},{4,5},{5,4},{6,7},{7,6},{8,9},{9,8},{10,11... | collective-permute-start | bytes 4128776 | tf_op jit(solution)/shard_map/ppermute | solution.py:31
  375.5 29.3 %copy-start.7 = (f32[2,2,1,48,3584]{4,3,2,1,0:T(8,128)}, f32[2,2,1,48,3584]{4,3,2,1,0:T(8,128)S(1)}, u32[]{:S(2)}) copy-start(f32[2,2,1,48,3584]{4,3,2,1,0:T(8,128)S(1)} %add_bitcast_fusion) | copy-start | bytes 8257540
  378.7 25.0 %copy-start.5 = (f32[2,1,2,48,3584]{4,3,2,1,0:T(8,128)}, f32[2,1,2,48,3584]{4,3,2,1,0:T(8,128)S(1)}, u32[]{:S(2)}) copy-start(f32[2,1,2,48,3584]{4,3,2,1,0:T(8,128)S(1)} %add_bitcast_fusion.1) | copy-start | bytes 8257540
  386.4 47.5 %collective-permute-start.41 = (bf16[3,96,1024]{2,1,0:T(8,128)(2,1)}, bf16[3,96,1024]{2,1,0:T(8,128)(2,1)}, u32[]{:S(2)}, u32[]{:S(2)}) collective-permute-start(bf16[3,96,1024]{2,1,0:T(8,128)(2,1)} %get-tuple-element.534), channel_id=1, source_target_pairs={{0,2},{1,3},{2,0},{3,1},{4,6},{5,7},{6,4},{7,5},{8,10},{9,11},{10,... | collective-permute-start | bytes 1769480 | tf_op jit(solution)/shard_map/ppermute | solution.py:31
  386.4 47.5 %collective-permute-start.42 = (bf16[3,96,1024]{2,1,0:T(8,128)(2,1)}, bf16[3,96,1024]{2,1,0:T(8,128)(2,1)}, u32[]{:S(2)}, u32[]{:S(2)}) collective-permute-start(bf16[3,96,1024]{2,1,0:T(8,128)(2,1)} %fusion.34), channel_id=1, source_target_pairs={{0,4},{1,5},{2,6},{3,7},{4,0},{5,1},{6,2},{7,3},{8,12},{9,13},{10,... | collective-permute-start | bytes 1769480 | tf_op jit(solution)/shard_map/ppermute | solution.py:31
  386.4 47.5 %collective-permute-start.43 = (bf16[3,96,1024]{2,1,0:T(8,128)(2,1)}, bf16[3,96,1024]{2,1,0:T(8,128)(2,1)}, u32[]{:S(2)}, u32[]{:S(2)}) collective-permute-start(bf16[3,96,1024]{2,1,0:T(8,128)(2,1)} %get-tuple-element.536), channel_id=1, source_target_pairs={{0,6},{1,7},{2,4},{3,5},{4,2},{5,3},{6,0},{7,1},{8,14},{9,15},{10,... | collective-permute-start | bytes 1769480 | tf_op jit(solution)/shard_map/ppermute | solution.py:31
  405.8 16.4 %collective-permute-start.36 = (bf16[2,1,48,3584]{3,2,1,0:T(8,128)(2,1)}, bf16[2,1,48,3584]{3,2,1,0:T(8,128)(2,1)S(1)}, u32[]{:S(2)}, u32[]{:S(2)}) collective-permute-start(bf16[2,1,48,3584]{3,2,1,0:T(8,128)(2,1)} %bitcast.47), channel_id=1, source_target_pairs={{0,1},{1,0},{2,3},{3,2},{4,5},{5,4},{6,7},{7,6},{8,9},{9,8},{10,11... | collective-permute-start | bytes 2064392 | tf_op jit(solution)/shard_map/ppermute | solution.py:31
  407.3 16.2 %collective-permute-start.37 = (bf16[2,1,48,3584]{3,2,1,0:T(8,128)(2,1)}, bf16[2,1,48,3584]{3,2,1,0:T(8,128)(2,1)}, u32[]{:S(2)}, u32[]{:S(2)}) collective-permute-start(bf16[2,1,48,3584]{3,2,1,0:T(8,128)(2,1)} %bitcast.48), channel_id=1, source_target_pairs={{0,16},{8,24},{16,0},{24,8},{1,17},{9,25},{17,1},{25,9},{2,18},{10... | collective-permute-start | bytes 2064392 | tf_op jit(solution)/shard_map/ppermute | solution.py:31
  426.4 16.8 %copy-start.45 = (bf16[1,48,3584]{2,1,0:T(8,128)(2,1)S(1)}, bf16[1,48,3584]{2,1,0:T(8,128)(2,1)}, u32[]{:S(2)}) copy-start(bf16[1,48,3584]{2,1,0:T(8,128)(2,1)} %get-tuple-element.533) | copy-start | bytes 1032196
  426.5 3.7 collective-permute-start.44
  430.2 3.7 collective-permute-start.45
  436.0 33.9 %copy-start.15 = (f32[2,1,1,48,3584]{4,3,2,1,0:T(8,128)S(1)}, f32[2,1,1,48,3584]{4,3,2,1,0:T(8,128)}, u32[]{:S(2)}) copy-start(f32[2,1,1,48,3584]{4,3,2,1,0:T(8,128)} %copy-done.14) | copy-start | bytes 4128772
  436.0 33.9 %copy-start.38 = (bf16[2,1,48,3584]{3,2,1,0:T(8,128)(2,1)S(1)}, bf16[2,1,48,3584]{3,2,1,0:T(8,128)(2,1)}, u32[]{:S(2)}) copy-start(bf16[2,1,48,3584]{3,2,1,0:T(8,128)(2,1)} %copy-done.37) | copy-start | bytes 2064388
  436.0 11.0 %collective-permute-start.46 = (bf16[3,96,1024]{2,1,0:T(8,128)(2,1)S(1)}, bf16[3,96,1024]{2,1,0:T(8,128)(2,1)S(1)}, u32[]{:S(2)}, u32[]{:S(2)}) collective-permute-start(bf16[3,96,1024]{2,1,0:T(8,128)(2,1)S(1)} %fusion.11), channel_id=1, source_target_pairs={{0,16},{8,24},{16,0},{24,8},{1,17},{9,25},{17,1},{25,9},{2,18},{10... | collective-permute-start | bytes 1769480 | tf_op jit(solution)/shard_map/ppermute | solution.py:31
  436.6 18.3 %collective-permute-start.38 = (bf16[1,48,3584]{2,1,0:T(8,128)(2,1)S(1)}, bf16[1,48,3584]{2,1,0:T(8,128)(2,1)S(1)}, u32[]{:S(2)}, u32[]{:S(2)}) collective-permute-start(bf16[1,48,3584]{2,1,0:T(8,128)(2,1)S(1)} %copy-done.46), channel_id=1, source_target_pairs={{0,2},{1,3},{2,0},{3,1},{4,6},{5,7},{6,4},{7,5},{8,10},{9,11},{10,... | collective-permute-start | bytes 1032200 | tf_op jit(solution)/shard_map/ppermute | solution.py:31
  443.2 26.6 %collective-permute-start.39 = (bf16[1,48,3584]{2,1,0:T(8,128)(2,1)S(1)}, bf16[1,48,3584]{2,1,0:T(8,128)(2,1)S(1)}, u32[]{:S(2)}, u32[]{:S(2)}) collective-permute-start(bf16[1,48,3584]{2,1,0:T(8,128)(2,1)S(1)} %fusion.39), channel_id=1, source_target_pairs={{0,4},{1,5},{2,6},{3,7},{4,0},{5,1},{6,2},{7,3},{8,12},{9,13},{10,... | collective-permute-start | bytes 1032200 | tf_op jit(solution)/shard_map/ppermute | solution.py:31
  443.2 26.6 %collective-permute-start.40 = (bf16[1,48,3584]{2,1,0:T(8,128)(2,1)S(1)}, bf16[1,48,3584]{2,1,0:T(8,128)(2,1)S(1)}, u32[]{:S(2)}, u32[]{:S(2)}) collective-permute-start(bf16[1,48,3584]{2,1,0:T(8,128)(2,1)S(1)} %copy-done.45), channel_id=1, source_target_pairs={{0,6},{1,7},{2,4},{3,5},{4,2},{5,3},{6,0},{7,1},{8,14},{9,15},{10,... | collective-permute-start | bytes 1032200 | tf_op jit(solution)/shard_map/ppermute | solution.py:31
  447.1 32.0 %copy-start.16 = (bf16[2,3,96,1024]{3,2,1,0:T(8,128)(2,1)}, bf16[2,3,96,1024]{3,2,1,0:T(8,128)(2,1)S(1)}, u32[]{:S(2)}) copy-start(bf16[2,3,96,1024]{3,2,1,0:T(8,128)(2,1)S(1)} %pad_maximum_fusion.1.pair) | copy-start | bytes 3538948
  470.1 8.2 %collective-permute-start.47 = (bf16[1,48,3584]{2,1,0:T(8,128)(2,1)S(1)}, bf16[1,48,3584]{2,1,0:T(8,128)(2,1)S(1)}, u32[]{:S(2)}, u32[]{:S(2)}) collective-permute-start(bf16[1,48,3584]{2,1,0:T(8,128)(2,1)S(1)} %fusion.31), channel_id=1, source_target_pairs={{0,16},{8,24},{16,0},{24,8},{1,17},{9,25},{17,1},{25,9},{2,18},{10... | collective-permute-start | bytes 1032200 | tf_op jit(solution)/shard_map/ppermute | solution.py:31
  471.8 7.2 %collective-permute-start.50 = (bf16[2,3,96,1024]{3,2,1,0:T(8,128)(2,1)S(1)}, bf16[2,3,96,1024]{3,2,1,0:T(8,128)(2,1)S(1)}, u32[]{:S(2)}, u32[]{:S(2)}) collective-permute-start(bf16[2,3,96,1024]{3,2,1,0:T(8,128)(2,1)S(1)} %pad_maximum_fusion.1.pair), channel_id=1, source_target_pairs={{0,8},{8,0},{16,24},{24,16},{1,9},{9,1},{17,25},{25,17},{2,10},{10... | collective-permute-start | bytes 3538952 | tf_op jit(solution)/shard_map/ppermute | solution.py:31
  471.8 6.5 %collective-permute-start.48 = (f32[2,1024]{1,0:T(2,128)S(1)}, f32[2,1024]{1,0:T(2,128)S(1)}, u32[]{:S(2)}, u32[]{:S(2)}) collective-permute-start(f32[2,1024]{1,0:T(2,128)S(1)} %add.374), channel_id=1, source_target_pairs={{0,4},{1,5},{2,6},{3,7},{4,0},{5,1},{6,2},{7,3},{8,12},{9,13},{10,... | collective-permute-start | bytes 24584 | tf_op jit(solution)/shard_map/ppermute | solution.py:31
  478.4 6.6 %collective-permute-start.49 = (bf16[2,1,48,3584]{3,2,1,0:T(8,128)(2,1)S(1)}, bf16[2,1,48,3584]{3,2,1,0:T(8,128)(2,1)S(1)}, u32[]{:S(2)}, u32[]{:S(2)}) collective-permute-start(bf16[2,1,48,3584]{3,2,1,0:T(8,128)(2,1)S(1)} %pad_maximum_fusion.3.pair), channel_id=1, source_target_pairs={{0,8},{8,0},{16,24},{24,16},{1,9},{9,1},{17,25},{25,17},{2,10},{10... | collective-permute-start | bytes 2064392 | tf_op jit(solution)/shard_map/ppermute | solution.py:31
  (55 other events, 270.1 us)
Sparse Core Ops, SparseCore 0:
  11.0 162.2 all-gather.2
